TPU v7x, 32 devices: a whole 2x2x4 slice. The times are simulated.
32 devices in a mesh: group: 8 (over z, y), roll: 4 (over x, core).
Axes of the slice: x: 2, y: 2, z: 4, core: 2. Of those that a mesh axis runs over, the one named last changes fastest.
Arguments:
- prefix_latent: float32 [8192, 576], P(('group', 'roll')), parts along dimension 0, may hold values from -8 to 8
- suffix_latent: bfloat16 [256, 256, 576], P(('group', 'roll')), parts along dimension 0, may hold values from -8 to 8
- suffix_len: int32 [256], P(('group', 'roll')), parts along dimension 0, may hold values from 1 to 256, as said below
- new_latent: bfloat16 [256, 2, 576], P(('group', 'roll')), parts along dimension 0, may hold values from -8 to 8
- queries: bfloat16 [256, 2, 64, 576], P(('group', 'roll')), parts along dimension 0, may hold values from -8 to 8
- w_uv: bfloat16 [64, 512, 128], P('roll'), may hold values from -1 to 1
- w_out: bfloat16 [8192, 7168], P('roll'), may hold values from -0.25 to 0.25
Outputs:
- layer_out: bfloat16 [256, 2, 7168], P(('group', 'roll')), parts along dimension 0
There are 8 independent parts, one for each index of `group`. A program takes and returns all parts, laid end to end along the dimension named above; an argument that names none is the same for every part. Nothing has to cross between parts.
Inputs may be any that keep to these rules, and one draw needn't show every extreme that they name: Row r uses the first suffix_len[r] positions of its suffix cache; in every draw some row has 256 and some row has 1.
All inputs are finite; a program needn't handle non-finite values.
Results may differ from a plain program's by a relative error of at most 0.012.
Values may be sent and summed in bfloat16 or wider, within the bound.
No kernel may reach another device: no remote copies, remote signals or barrier semaphores. Data moves between devices by JAX's collectives and lax.ppermute only.
A program may use at most 128 MiB of HBM per device.

v0:
```python
import jax
import jax.numpy as jnp
from jax import lax
from jax.sharding import PartitionSpec as P

LATENT = 512
QK_HEAD = 192


def absorb(state_now, scores, live_mask, value_fn):
    running_max, running_sum, running_acc = state_now
    scores = jnp.where(live_mask, scores, -1e30)
    next_max = jnp.maximum(running_max, jnp.max(scores, axis=-1))
    shrink = jnp.exp(running_max - next_max)
    weights = jnp.where(live_mask, jnp.exp(scores - next_max[..., None]), 0.0)
    running_sum = running_sum * shrink + jnp.sum(weights, axis=-1)
    running_acc = running_acc * shrink[..., None] + value_fn(weights.astype(jnp.bfloat16))
    return (next_max, running_sum, running_acc)


def on_device(prefix_latent, suffix_latent, suffix_len, new_latent, queries, w_uv, w_out):
    scaling = QK_HEAD ** (-0.5)
    rows_here, steps_here, heads_all, row_width = queries.shape
    lead_shape = (rows_here, steps_here, heads_all)
    start_state = (
        jnp.full(lead_shape, -1e30, jnp.float32),
        jnp.zeros(lead_shape, jnp.float32),
        jnp.zeros(lead_shape + (LATENT,), jnp.float32),
    )
    piece = lax.all_gather(prefix_latent.astype(jnp.bfloat16), "roll", axis=0, tiled=True)
    scores = (
        jnp.einsum("rshc,nc->rshn", queries, piece, preferred_element_type=jnp.float32) * scaling
    )

    def prefix_values(weight_bf):
        return jnp.einsum(
            "rshn,nc->rshc", weight_bf, piece[:, :LATENT], preferred_element_type=jnp.float32
        )

    state_now = absorb(start_state, scores, True, prefix_values)
    new_scores = (
        jnp.einsum("rshc,rtc->rsht", queries, new_latent, preferred_element_type=jnp.float32)
        * scaling
    )
    step_ids = jnp.arange(steps_here, dtype=jnp.int32)
    causal = (step_ids[None, :] <= step_ids[:, None])[None, :, None, :]

    def new_values(weight_bf):
        return jnp.einsum(
            "rsht,rtc->rshc",
            weight_bf,
            new_latent[:, :, :LATENT],
            preferred_element_type=jnp.float32,
        )

    state_now = absorb(state_now, new_scores, causal, new_values)
    scores = (
        jnp.einsum("rshc,rnc->rshn", queries, suffix_latent, preferred_element_type=jnp.float32)
        * scaling
    )
    positions = jnp.arange(suffix_latent.shape[1], dtype=jnp.int32)
    live_mask = (positions[None, :] < suffix_len[:, None])[:, None, None, :]

    def suffix_values(weight_bf):
        return jnp.einsum(
            "rshn,rnc->rshc",
            weight_bf,
            suffix_latent[:, :, :LATENT],
            preferred_element_type=jnp.float32,
        )

    state_now = absorb(state_now, scores, live_mask, suffix_values)
    running_max, running_sum, running_acc = state_now
    attended = (running_acc / running_sum[..., None]).astype(jnp.bfloat16)
    head_vals = jnp.einsum(
        "rshc,hcv->rshv",
        lax.all_to_all(attended, "roll", split_axis=2, concat_axis=0, tiled=True),
        w_uv,
        preferred_element_type=jnp.float32,
    ).astype(jnp.bfloat16)
    head_out = head_vals.reshape(
        head_vals.shape[0], head_vals.shape[1], head_vals.shape[2] * head_vals.shape[3]
    )
    count = lax.axis_size("roll") * rows_here
    flat_rows = head_out.reshape(count * head_out.shape[1], head_out.shape[2])
    result = jnp.dot(flat_rows, w_out, preferred_element_type=jnp.float32)
    return lax.psum_scatter(
        result.reshape(count, head_out.shape[1], w_out.shape[1]).astype(jnp.bfloat16),
        "roll",
        scatter_dimension=0,
        tiled=True,
    )


def solution(mesh):
    in_specs = (
        P(("group", "roll"), None),
        P(("group", "roll"), None, None),
        P(("group", "roll")),
        P(("group", "roll"), None, None),
        P(("group", "roll"), None, None, None),
        P("roll", None, None),
        P("roll", None),
    )
    out_specs = P(("group", "roll"), None, None)
    return jax.shard_map(
        on_device, mesh=mesh, in_specs=in_specs, out_specs=out_specs, check_vma=False
    )
```

profile of v0, /device:TPU:0, one launch (start us, length us, event | category | flops | bytes accessed | tf_op | source)
XLA Modules:
  0.0 102.6 jit_solution(6271426400411096190)
XLA Ops:
  6.5 2.0 %convert_element_type.24 = bf16[256,576]{0,1:T(8,128)(2,1)} convert(f32[256,576]{0,1:T(8,128)} %param.7) | non-fusion elementwise | flops 147456 | bytes 884736 | tf_op jit(solution)/shard_map/convert_element_type | solution.py:30
  8.5 0.0 all-gather.2.cloned.1.call-update
  8.5 0.0 reduce-scatter.4.cloned.1.call-start
  8.6 0.7 iota_compare_fusion
  9.3 2.1 %fusion.58 = (f32[8,2,64]{2,1,0:T(2,128)S(1)}, f32[8,2,64,2]{2,3,1,0:T(2,128)S(1)}) fusion(bf16[8,2,64,576]{3,2,1,0:T(8,128)(2,1)} %param.11, bf16[8,2,576]{2,1,0:T(2,128)(2,1)} %param.10, pred[2,2]{1,0:T(4,128)(4,1)S(1)} %iota_compare_fusion.1), kind=kOutput, calls=%fused_computation.57 | convolution fusion | flops 2364416 | bytes 1210372 | tf_op jit(solution)/shard_map/rshc,rtc->rsht/dot_general | solution.py:42
  11.4 2.8 %fusion.57 = (f32[8,2,64]{2,1,0:T(2,128)S(1)}, f32[8,2,64,256]{3,2,1,0:T(8,128)S(1)}) fusion(bf16[8,2,64,576]{3,2,1,0:T(8,128)(2,1)} %param.11, bf16[8,256,576]{1,2,0:T(8,128)(2,1)} %param.8, pred[8,256]{1,0:T(8,128)(4,1)S(1)} %iota_compare_fusion), kind=kOutput, calls=%fused_computation.56 | convolution fusion | flops 302775296 | bytes 4593664 | tf_op jit(solution)/shard_map/rshc,rnc->rshn/dot_general | solution.py:58
  14.2 15.1 %all-gather.2.cloned.1.call-done = bf16[1024,576]{0,1:T(8,128)(2,1)} async-done(((bf16[256,576]{0,1:T(8,128)(2,1)}), bf16[1024,576]{0,1:T(8,128)(2,1)}) %all-gather.2.cloned.1.call-update) | async-done | bytes 1179664 | tf_op jit(solution)/shard_map/all_gather | solution.py:30
  29.2 3.7 %multiply_reduce_fusion = (f32[8,2,64]{2,1,0:T(2,128)S(1)}, f32[8,2,64,1024]{3,2,1,0:T(8,128)S(1)}) fusion(bf16[8,2,64,576]{3,2,1,0:T(8,128)(2,1)} %param.11, bf16[1024,576]{0,1:T(8,128)(2,1)} %all-gather.2.cloned.1.call-done), kind=kOutput, calls=%fused_computation.5 | convolution fusion | flops 1210055680 | bytes 6557696 | tf_op jit(solution)/shard_map/rshc,nc->rshn/dot_general | solution.py:32
  33.0 0.4 fusion.38
  33.4 0.8 fusion.14
  34.2 0.0 copy-start.3
  34.2 0.9 fusion.8
  35.2 0.1 fusion.50
  35.3 0.2 copy-done.3
  35.5 1.3 %fusion.12 = f32[8,2,64,512]{3,2,1,0:T(8,128)S(1)} fusion(f32[8,2,64,1024]{3,2,1,0:T(8,128)S(1)} %get-tuple-element.17, f32[8,2,64]{2,1,0:T(2,128)S(1)} %get-tuple-element.11, bf16[1024,576]{0,1:T(8,128)(2,1)S(1)} %copy-done.3), kind=kOutput, calls=%fused_computation.10 | convolution fusion | flops 1076887552 | bytes 7348224 | tf_op jit(solution)/shard_map/rshn,nc->rshc/dot_general | solution.py:36
  36.9 1.2 %divide_convert_fusion = bf16[8,2,64,512]{3,2,1,0:T(8,128)(2,1)S(1)} fusion(f32[8,2,64,512]{3,2,1,0:T(8,128)S(1)} %fusion.14, f32[8,2,64,512]{3,2,1,0:T(8,128)S(1)} %fusion.12, f32[8,2,64]{2,1,0:T(2,128)S(1)} %get-tuple-element.5, f32[8,2,64]{2,1,0:T(2,128)S(1)} %get-tuple-element.7, f32[8,2,64]{2,1,0:T(2,128)S(1)} %get-tuple-element.6, ...), kind=kOutput, calls=%fused_computation.15 | convolution fusion | flops 5773312 | bytes 5317120 | tf_op jit(solution)/shard_map/rsht,rtc->rshc/dot_general | solution.py:49
  38.1 1.1 %copy.19 = bf16[8,2,64,512]{3,1,0,2:T(2,128)(2,1)S(1)} copy(bf16[8,2,64,512]{3,2,1,0:T(8,128)(2,1)S(1)} %divide_convert_fusion) | data formatting | bytes 2097152 | tf_op jit(solution)/shard_map/convert_element_type | solution.py:74
  39.2 16.9 %all_to_all.18 = bf16[8,2,64,512]{3,1,0,2:T(2,128)(2,1)S(1)} all-to-all(bf16[8,2,64,512]{3,1,0,2:T(2,128)(2,1)S(1)} %copy.19), channel_id=1, replica_groups=mesh['group'=8,'roll'=4] {'roll'}, dimensions={2} | all-to-all | bytes 2097152 | tf_op jit(solution)/shard_map/all_to_all | solution.py:77
  56.0 0.5 fusion.32
  56.5 12.2 %fusion.5 = bf16[2,4,8,7168]{3,2,1,0:T(8,128)(2,1)S(1)} fusion(bf16[2048,7168]{1,0:T(8,128)(2,1)} %param.13, bf16[16,2,4,8,128]{4,3,2,1,0:T(8,128)(2,1)S(1)} %fusion.32), kind=kOutput, calls=%fused_computation.3 | convolution fusion | flops 1879506944 | bytes 30539776 | tf_op jit(solution)/shard_map/dot_general | solution.py:86
  68.7 1.0 copy.35
  69.7 0.0 reduce-scatter.4.cloned.1.call-update
  69.7 24.2 %reduce-scatter.4.cloned.1.call-done = bf16[8,14336]{1,0:T(8,128)(2,1)} async-done(((bf16[32,14336]{1,0:T(8,128)(2,1)}), bf16[8,14336]{1,0:T(8,128)(2,1)}) %reduce-scatter.4.cloned.1.call-update) | async-done | bytes 229392
  93.9 1.9 %copy.22 = bf16[8,2,7168]{2,1,0:T(2,128)(2,1)} copy(bf16[8,2,7168]{2,0,1:T(8,128)(2,1)} %bitcast.77) | data formatting | bytes 458752 | tf_op jit(solution)/shard_map/reduce_scatter | solution.py:87
  (10 shorter events, 0.1 us)
Async XLA Ops:
  6.5 49.5 %copy-start = (bf16[16,512,128]{2,1,0:T(8,128)(2,1)S(1)}, bf16[16,512,128]{2,1,0:T(8,128)(2,1)}, u32[]{:S(2)}) copy-start(bf16[16,512,128]{2,1,0:T(8,128)(2,1)} %param.12) | copy-start | bytes 6291460
  6.5 22.7 %all-gather.2.cloned.1.call-start = ((), (), s32[]{:S(2)}) async-start(), calls=%async_computation.2 | async-start | bytes 1474560 | tf_op jit(solution)/shard_map/all_gather | solution.py:30
  8.5 85.4 %reduce-scatter.4.cloned.1.call-start = ((), (), s32[]{:S(2)}) async-start(), calls=%async_computation.3 | async-start | bytes 1146880
  29.2 4.2 %copy-start.1 = (bf16[8,256,576]{1,2,0:T(8,128)(2,1)S(1)}, bf16[8,256,576]{1,2,0:T(8,128)(2,1)}, u32[]{:S(2)}) copy-start(bf16[8,256,576]{1,2,0:T(8,128)(2,1)} %param.8) | copy-start | bytes 7077892
  34.2 1.3 %copy-start.3 = (bf16[1024,576]{0,1:T(8,128)(2,1)S(1)}, bf16[1024,576]{0,1:T(8,128)(2,1)}, u32[]{:S(2)}) copy-start(bf16[1024,576]{0,1:T(8,128)(2,1)} %all-gather.2.cloned.1.call-done) | copy-start | bytes 3538948
  35.5 1.3 %copy-start.2 = (bf16[8,2,576]{2,1,0:T(2,128)(2,1)S(1)}, bf16[8,2,576]{2,1,0:T(2,128)(2,1)}, u32[]{:S(2)}) copy-start(bf16[8,2,576]{2,1,0:T(2,128)(2,1)} %param.10) | copy-start | bytes 55300
Sparse Core Ops, SparseCore 0:
  8.9 20.2 all-gather.1
  69.8 24.0 reduce-scatter.3
where the time goes:
time: 103 us
  waiting for transfers between devices  39.3 us (38%)
  matrix products  24.5 us (24%)
  blocking collectives  16.9 us (16%)
  between operations  13.5 us (13%)
  other arithmetic  4.22 us (4%)
  local copies, waits for them, and re-layouts  4.13 us (4%)
    unnamed x3, waiting for transfers between devices  24.3 us
    all_to_all x1, blocking collectives, on_device(): lax.all_to_all(attended, 'roll', split_axis=2, concat_axis=0, tiled=True)  16.9 us
    all_gather x1, waiting for transfers between devices, on_device(): lax.all_gather(prefix_latent.astype(jnp.bfloat16), 'roll', axis=0, tiled=...  15.1 us
    dot_general x1, matrix products, on_device(): result = jnp.dot(flat_rows, w_out, preferred_element_type=jnp.float32)  12.2 us
    dot_general x1, matrix products, on_device(): jnp.einsum('rshc,nc->rshn', queries, piece, preferred_element_type=jnp.fl...  3.69 us
    dot_general x1, matrix products, on_device(): jnp.einsum('rshc,rnc->rshn', queries, suffix_latent, preferred_element_ty...  2.77 us
  transfers between devices with their start and end apart: 2, of which 2 were waited for; matrix products, arithmetic and copies ran while one was open for 5% of the time, Pallas kernels for 0%

commit v1 on v0

v1 whole, which is shorter than its diff:
```python
import functools
import math

import jax
import jax.numpy as jnp
from jax import lax
from jax.experimental import pallas as pl
from jax.experimental.pallas import tpu as pltpu
from jax.sharding import PartitionSpec as P

LATENT = 512
QK_HEAD = 192
SCALE2 = QK_HEAD**-0.5 * math.log2(math.e)
NEG = -1e30
CHUNK_HEADS = 4
OUT_PARTS = 2
MIB = 2**20


def dot_nt(a, b):
    return lax.dot_general(a, b, (((1,), (1,)), ((), ())), preferred_element_type=jnp.float32)


def dot_nn(a, b):
    return jnp.dot(a, b, preferred_element_type=jnp.float32)


def near_kernel(len_ref, q_ref, suf_ref, new_ref, *refs):
    key_refs, (m_ref, l_ref, acc_ref) = refs[:-3], refs[-3:]
    row = pl.program_id(0)
    steps, heads, width = q_ref.shape[1:]
    rows = steps * heads
    q = q_ref[0].reshape(rows, width)
    keys = [k[...] for k in key_refs] + [suf_ref[0]]
    scores = [dot_nn(q, k) for k in keys]
    at = lax.broadcasted_iota(jnp.int32, scores[-1].shape, 1)
    scores[-1] = jnp.where(at < len_ref[row], scores[-1], NEG)
    new = new_ref[row]
    new_scores = dot_nt(q, new)
    step = lax.broadcasted_iota(jnp.int32, new_scores.shape, 0) // heads
    token = lax.broadcasted_iota(jnp.int32, new_scores.shape, 1)
    new_scores = jnp.where(token <= step, new_scores, NEG)
    m = jnp.max(new_scores, axis=1, keepdims=True)
    for s in scores:
        m = jnp.maximum(m, jnp.max(s, axis=1, keepdims=True))
    new_weights = jnp.exp2((new_scores - m) * SCALE2)
    l = jnp.sum(new_weights, axis=1, keepdims=True)
    new_probs = new_weights.astype(jnp.bfloat16).astype(jnp.float32)
    new_values = new[:, :LATENT].astype(jnp.float32)
    acc = new_probs[:, 0:1] * new_values[0:1]
    for t in range(1, new.shape[0]):
        acc += new_probs[:, t : t + 1] * new_values[t : t + 1]
    for s, k in zip(scores, keys):
        p = jnp.exp2((s - m) * SCALE2)
        l += jnp.sum(p, axis=1, keepdims=True)
        acc += dot_nt(p.astype(jnp.bfloat16), k[:LATENT])
    m_ref[...] = jnp.broadcast_to(m, m_ref.shape)
    l_ref[...] = jnp.broadcast_to(l, l_ref.shape)
    acc_ref[...] = acc


def near_attention(suffix_len, queries, suffix_t, new_latent, keys):
    rows, steps, heads, width = queries.shape
    per = steps * heads
    whole = pl.BlockSpec(memory_space=pltpu.VMEM)
    return pl.pallas_call(
        near_kernel,
        grid=(rows,),
        in_specs=[
            pl.BlockSpec(memory_space=pltpu.SMEM),
            pl.BlockSpec((1, steps, heads, width), lambda r: (r, 0, 0, 0)),
            pl.BlockSpec((1,) + suffix_t.shape[1:], lambda r: (r, 0, 0)),
            whole,
        ]
        + [whole] * len(keys),
        out_specs=[
            pl.BlockSpec((per, 128), lambda r: (r, 0)),
            pl.BlockSpec((per, 128), lambda r: (r, 0)),
            pl.BlockSpec((per, LATENT), lambda r: (r, 0)),
        ],
        out_shape=[
            jax.ShapeDtypeStruct((rows * per, 128), jnp.float32),
            jax.ShapeDtypeStruct((rows * per, 128), jnp.float32),
            jax.ShapeDtypeStruct((rows * per, LATENT), jnp.float32),
        ],
        compiler_params=pltpu.CompilerParams(vmem_limit_bytes=20 * MIB),
        cost_estimate=pl.CostEstimate(
            flops=2 * rows * per * 1100 * 768, bytes_accessed=8 * MIB, transcendentals=rows * per * 768
        ),
        name="near_attention",
    )(suffix_len, queries, suffix_t, new_latent, *keys)


def far_kernel(n_keys, axis_size, pairs, q_ref, m_ref, l_ref, acc_ref, *refs):
    key_refs, out_refs, done = refs[:n_keys], refs[n_keys:-1], refs[-1]
    at = pl.program_id(0)
    per = m_ref.shape[0]
    heads, width = q_ref.shape[2:]
    q = q_ref[...].reshape(per, width)
    keys = [k[...] for k in key_refs]
    scores = [dot_nn(q, k) for k in keys]
    old_m = m_ref[:, 0:1]
    m = old_m
    for s in scores:
        m = jnp.maximum(m, jnp.max(s, axis=1, keepdims=True))
    shrink = jnp.exp2((old_m - m) * SCALE2)
    l = l_ref[:, 0:1] * shrink
    acc = acc_ref[...] * shrink
    for s, k in zip(scores, keys):
        p = jnp.exp2((s - m) * SCALE2)
        l += jnp.sum(p, axis=1, keepdims=True)
        acc += dot_nt(p.astype(jnp.bfloat16), k[:LATENT])
    attended = acc / l
    for g in range(LATENT // 128):
        done[g, pl.ds(pl.multiple_of(at * per, per), per), :] = attended[:, g * 128 : (g + 1) * 128]

    @pl.when(at == pl.num_programs(0) - 1)
    def _():
        me = lax.axis_index("roll")
        share = heads // axis_size
        for c in range(share // CHUNK_HEADS):
            for k in range(axis_size):
                first = jnp.bitwise_xor(me, k) * share + c * CHUNK_HEADS
                for i in range(CHUNK_HEADS):
                    for g in range(LATENT // 128):
                        out_refs[c * axis_size + k][
                            i * pairs : (i + 1) * pairs, g * 128 : (g + 1) * 128
                        ] = done[g, pl.ds(first + i, pairs, stride=heads), :].astype(jnp.bfloat16)


def far_attention(queries, state, keys, axis_size):
    rows, steps, heads, width = queries.shape
    pairs = rows * steps
    block_rows = 2
    per = block_rows * steps * heads
    chunks = heads // axis_size // CHUNK_HEADS
    whole = pl.BlockSpec(memory_space=pltpu.VMEM)
    return pl.pallas_call(
        functools.partial(far_kernel, len(keys), axis_size, pairs),
        grid=(rows // block_rows,),
        in_specs=[
            pl.BlockSpec((block_rows, steps, heads, width), lambda r: (r, 0, 0, 0)),
            pl.BlockSpec((per, 128), lambda r: (r, 0)),
            pl.BlockSpec((per, 128), lambda r: (r, 0)),
            pl.BlockSpec((per, LATENT), lambda r: (r, 0)),
        ]
        + [whole] * len(keys),
        out_specs=[whole] * (chunks * axis_size),
        out_shape=[
            jax.ShapeDtypeStruct((CHUNK_HEADS * pairs, LATENT), jnp.bfloat16)
        ]
        * (chunks * axis_size),
        scratch_shapes=[pltpu.VMEM((LATENT // 128, (pairs + 1) * heads, 128), jnp.float32)],
        compiler_params=pltpu.CompilerParams(vmem_limit_bytes=24 * MIB),
        cost_estimate=pl.CostEstimate(
            flops=2 * pairs * heads * 1100 * 512, bytes_accessed=8 * MIB, transcendentals=pairs * heads * 512
        ),
        name="far_attention",
    )(queries, *state, *keys)


def project_kernel(chunk, first_col, n_pieces, has_acc, last, block, *refs):
    piece_refs, refs = refs[:n_pieces], refs[n_pieces:]
    if has_acc:
        acc_ref, refs = refs[0], refs[1:]
    uv_ref, w_ref = refs[:2]
    if last:
        keep_ref, send_ref = refs[2:4]
    else:
        out_ref = refs[2]
    uv_buf, w_buf, uv_sem, w_sem = refs[-4:]
    depth, cols = w_buf.shape
    heads = uv_buf.shape[0]
    pairs = piece_refs[0].shape[0] // heads
    uv_copy = pltpu.make_async_copy(uv_ref.at[pl.ds(chunk * heads, heads)], uv_buf, uv_sem)
    uv_copy.start()
    copies = []
    for b in range(cols // block):
        here = pl.ds(b * block, block)
        copies.append(
            pltpu.make_async_copy(
                w_ref.at[pl.ds(chunk * depth, depth), pl.ds(first_col + b * block, block)],
                w_buf.at[:, here],
                w_sem.at[b],
            )
        )
        copies[-1].start()
    uv_copy.wait()
    head_out = []
    for i in range(heads):
        rows = jnp.concatenate([p[i * pairs : (i + 1) * pairs, :] for p in piece_refs], axis=0)
        head_out.append(dot_nn(rows, uv_buf[i]).astype(jnp.bfloat16))
    head_out = jnp.concatenate(head_out, axis=1)
    for b, copy in enumerate(copies):
        here = slice(b * block, (b + 1) * block)
        copy.wait()
        total = dot_nn(head_out, w_buf[:, here])
        if has_acc:
            total += acc_ref[:, here]
        if last:
            for k in range(n_pieces):
                to = send_ref if k % 2 else keep_ref
                to[k // 2 * pairs : (k // 2 + 1) * pairs, here] = total[
                    k * pairs : (k + 1) * pairs
                ].astype(jnp.bfloat16)
        else:
            out_ref[:, here] = total


def project(chunk, pieces, acc, w_uv, w_out, last, first_col, cols):
    head_v = w_uv.shape[2]
    depth = CHUNK_HEADS * head_v
    total_rows = sum(p.shape[0] for p in pieces) // CHUNK_HEADS
    block = next(b for b in (1024, 896, 512, 128) if cols % b == 0)
    vmem, hbm = pl.BlockSpec(memory_space=pltpu.VMEM), pl.BlockSpec(memory_space=pl.ANY)
    has_acc = acc is not None
    operands = list(pieces) + ([acc] if has_acc else []) + [w_uv, w_out]
    if last:
        out_shape = [jax.ShapeDtypeStruct((total_rows // 2, cols), jnp.bfloat16)] * 2
    else:
        out_shape = [jax.ShapeDtypeStruct((total_rows, cols), jnp.float32)]
    acc_spec = [vmem]
    if has_acc and acc.shape[1] != cols:
        part = first_col // cols
        acc_spec = [pl.BlockSpec((total_rows, cols), lambda i: (0, part))]
    out = pl.pallas_call(
        functools.partial(project_kernel, chunk, first_col, len(pieces), has_acc, last, block),
        grid=(1,),
        in_specs=[vmem] * len(pieces) + (acc_spec if has_acc else []) + [hbm, hbm],
        out_specs=[vmem] * len(out_shape),
        out_shape=out_shape,
        scratch_shapes=[
            pltpu.VMEM((CHUNK_HEADS,) + w_uv.shape[1:], jnp.bfloat16),
            pltpu.VMEM((depth, cols), jnp.bfloat16),
            pltpu.SemaphoreType.DMA,
            pltpu.SemaphoreType.DMA((cols // block,)),
        ],
        compiler_params=pltpu.CompilerParams(vmem_limit_bytes=32 * MIB),
        cost_estimate=pl.CostEstimate(
            flops=2 * total_rows * depth * cols, bytes_accessed=2 * depth * cols, transcendentals=0
        ),
        input_output_aliases={len(pieces): 0} if has_acc and not last else {},
        name="project",
    )(*operands)
    return out if last else out[0]


def on_device(prefix_latent, suffix_latent, suffix_len, new_latent, queries, w_uv, w_out):
    n = lax.axis_size("roll")
    rows, steps, heads, _ = queries.shape
    pairs = rows * steps
    width = w_out.shape[1]

    def swap(x, k):
        return lax.ppermute(x, "roll", [(i, i ^ k) for i in range(n)])

    own = prefix_latent.T.astype(jnp.bfloat16)
    across = [swap(own, k) for k in range(2, n, 2)]
    beside = swap(own, 1)
    forwarded = [swap(x, 1) for x in across]
    state = near_attention(
        suffix_len, queries, jnp.swapaxes(suffix_latent, 1, 2), new_latent, [own, beside]
    )
    pieces = far_attention(queries, state, across + forwarded, n)
    chunks = len(pieces) // n
    order = list(range(2, n)) + [1]
    acc = None
    for c in range(chunks):
        mine = pieces[c * n : (c + 1) * n]
        got = [mine[0]] + [None] * (n - 1)
        for k in order:
            got[k] = swap(mine[k], k)
        if c < chunks - 1:
            acc = project(c, got, acc, w_uv, w_out, False, 0, width)
    cols = width // OUT_PARTS
    outs = []
    for part in range(OUT_PARTS):
        keep, send = project(
            chunks - 1, got, acc, w_uv, w_out, True, part * cols, cols
        )
        recv = swap(send, 1)
        total = keep.astype(jnp.float32) + recv.astype(jnp.float32)
        result = total[:pairs]
        for k in range(2, n, 2):
            piece = total[k // 2 * pairs : (k // 2 + 1) * pairs].astype(jnp.bfloat16)
            result = result + swap(piece, k).astype(jnp.float32)
        outs.append(result.astype(jnp.bfloat16))
    return jnp.concatenate(outs, axis=1).reshape(rows, steps, width)


def solution(mesh):
    in_specs = (
        P(("group", "roll"), None),
        P(("group", "roll"), None, None),
        P(("group", "roll")),
        P(("group", "roll"), None, None),
        P(("group", "roll"), None, None, None),
        P("roll", None, None),
        P("roll", None),
    )
    out_specs = P(("group", "roll"), None, None)
    return jax.shard_map(
        on_device, mesh=mesh, in_specs=in_specs, out_specs=out_specs, check_vma=False
    )
```

time: 103 us -> 63.1 us (0.61)
  Pallas kernels: 0 us -> 27.6 us
  waiting for transfers between devices: 39.3 us -> 13 us
  matrix products: 24.5 us -> 0 us
  blocking collectives: 16.9 us -> 0 us
  starting transfers between devices: 0.04 us -> 15.6 us
  between operations: 13.5 us -> 0.2 us
  other arithmetic: 4.22 us -> 1.26 us
  local copies, waits for them, and re-layouts: 4.13 us -> 5.18 us
    pallas_call x0 -> x7, Pallas kernels: none -> 27.6 us  [the longest x5 15.6 us: project(): pl.pallas_call(functools.partial(project_kernel, chunk, first_col, len(pi...]
    dot_general x8 -> x0, matrix products: 24.5 us -> none  [the longest x1 12.2 us: on_device(): result = jnp.dot(flat_rows, w_out, preferred_element_type=jnp.float32)]
    unnamed x3 -> x0, waiting for transfers between devices: 24.3 us -> none
    all_to_all x1 -> x0, blocking collectives: 16.9 us -> none  [on_device(): lax.all_to_all(attended, 'roll', split_axis=2, concat_axis=0, tiled=True)]
    ppermute x0 -> x19, starting transfers between devices: none -> 15.6 us  [swap(): return lax.ppermute(x, 'roll', [(i, i ^ k) for i in range(n)])]
    all_gather x1 -> x0, waiting for transfers between devices: 15.1 us -> none  [on_device(): lax.all_gather(prefix_latent.astype(jnp.bfloat16), 'roll', axis=0, tiled=...]
    ppermute x0 -> x19, waiting for transfers between devices: none -> 13 us  [swap(): return lax.ppermute(x, 'roll', [(i, i ^ k) for i in range(n)])]
    unnamed x9 -> x12, local copies, waits for them, and re-layouts: 1.19 us -> 4.37 us
  transfers between devices with their start and end apart: 2 -> 19, of which waited for: 2 -> 5; matrix products, arithmetic and copies ran while one was open for 5% -> 0% of each run, Pallas kernels for 0% -> 33%
where the time goes in v1:
time: 63.1 us; the launch traced here: 62.7 us
  Pallas kernels  27.6 us (44%)
  starting transfers between devices  15.6 us (25%)
  waiting for transfers between devices  13 us (21%)
  local copies, waits for them, and re-layouts  5.18 us (8%)
  other arithmetic  1.26 us (2%)
    pallas_call x5, Pallas kernels, project(): pl.pallas_call(functools.partial(project_kernel, chunk, first_col, len(pi...  15.6 us
    ppermute x19, starting transfers between devices, swap(): return lax.ppermute(x, 'roll', [(i, i ^ k) for i in range(n)])  15.6 us
    ppermute x19, waiting for transfers between devices, swap(): return lax.ppermute(x, 'roll', [(i, i ^ k) for i in range(n)])  13 us
    pallas_call x1, Pallas kernels, near_attention(): pl.pallas_call(near_kernel, grid=(rows,), in_specs=[pl.BlockSpec(memory_s...  7.6 us
    unnamed x12, local copies, waits for them, and re-layouts  4.37 us
    pallas_call x1, Pallas kernels, far_attention(): pl.pallas_call(functools.partial(far_kernel, len(keys), axis_size, pairs)...  4.34 us
  transfers between devices with their start and end apart: 19, of which 5 were waited for; matrix products, arithmetic and copies ran while one was open for 0% of the time, Pallas kernels for 33%

profile of v1, /device:TPU:0, one launch (start us, length us, event | category | flops | bytes accessed | tf_op | source)
XLA Modules:
  0.0 62.7 jit_solution(14959239358745656888)
XLA Ops:
  0.0 1.1 %convert_bitcast_fusion.refs_0_ = bf16[576,256]{1,0:T(8,128)(2,1)S(1)} fusion(f32[256,576]{0,1:T(8,128)} %param.7), kind=kLoop, calls=%fused_computation.2 | loop fusion | flops 147456 | bytes 884736 | tf_op jit(solution)/shard_map/convert_element_type | solution.py:257
  1.1 3.0 %collective-permute-start.1 = (bf16[576,256]{1,0:T(8,128)(2,1)S(1)}, bf16[576,256]{1,0:T(8,128)(2,1)S(1)}, u32[]{:S(2)}, u32[]{:S(2)}) collective-permute-start(bf16[576,256]{1,0:T(8,128)(2,1)S(1)} %convert_bitcast_fusion.refs_0_), channel_id=1, source_target_pairs={{0,2},{1,3},{2,0},{3,1},{4,6},{5,7},{6,4},{7,5},{8,10},{9,11},{10,... | collective-permute-start | bytes 884744 | tf_op jit(solution)/shard_map/ppermute | solution.py:255
  4.1 7.0 %collective-permute-done.1.refs_0_ = bf16[576,256]{1,0:T(8,128)(2,1)S(1)} collective-permute-done((bf16[576,256]{1,0:T(8,128)(2,1)S(1)}, bf16[576,256]{1,0:T(8,128)(2,1)S(1)}, u32[]{:S(2)}, u32[]{:S(2)}) %collective-permute-start.1) | collective-permute-done | bytes 294944 | tf_op jit(solution)/shard_map/ppermute | solution.py:255
  11.1 1.3 %copy-done.1 = bf16[8,2,64,576]{3,2,1,0:T(8,128)(2,1)S(1)} copy-done((bf16[8,2,64,576]{3,2,1,0:T(8,128)(2,1)S(1)}, bf16[8,2,64,576]{3,2,1,0:T(8,128)(2,1)}, u32[]{:S(2)}) %copy-start.1) | copy-done | bytes 1179672
  12.4 1.7 %copy-done.3 = bf16[8,256,576]{1,2,0:T(8,128)(2,1)S(1)} copy-done((bf16[8,256,576]{1,2,0:T(8,128)(2,1)S(1)}, bf16[8,256,576]{1,2,0:T(8,128)(2,1)}, u32[]{:S(2)}) %copy-start.3) | copy-done | bytes 2359320
  14.1 0.7 %copy-done.4 = bf16[8,2,576]{2,1,0:T(2,128)(2,1)S(1)} copy-done((bf16[8,2,576]{2,1,0:T(2,128)(2,1)S(1)}, bf16[8,2,576]{2,1,0:T(2,128)(2,1)}, u32[]{:S(2)}) %copy-start.4) | copy-done | bytes 18456
  14.8 0.7 %copy-done.5 = s32[8]{0:T(128)S(1)} copy-done((s32[8]{0:T(128)S(1)}, s32[8]{0:T(128)}, u32[]{:S(2)}) %copy-start.5) | copy-done | bytes 56
  15.5 7.6 %near_attention.1 = (f32[1024,128]{1,0:T(8,128)S(1)}, f32[1024,128]{1,0:T(8,128)S(1)}, f32[1024,512]{1,0:T(8,128)S(1)}) custom-call(s32[8]{0:T(128)S(1)} %copy-done.5, bf16[8,2,64,576]{3,2,1,0:T(8,128)(2,1)S(1)} %copy-done.1, bf16[8,576,256]{2,1,0:T(8,128)(2,1)S(1)} %bitcast.3, bf16[8,2,576]{2,1,0:T(2,128)(2,1)S(1)} %copy-done.4, ...), custom_call_target="tpu_custom_call" | custom-call | flops 1730150400 | bytes 8388608 | tf_op jit(solution)/shard_map/near_attention/pallas_call | solution.py:66
  23.1 4.3 %far_attention.1 = (bf16[64,512]{1,0:T(8,128)(2,1)S(1)}, bf16[64,512]{1,0:T(8,128)(2,1)S(1)}, bf16[64,512]{1,0:T(8,128)(2,1)S(1)}, bf16[64,512]{1,0:T(8,128)(2,1...) custom-call(bf16[8,2,64,576]{3,2,1,0:T(8,128)(2,1)S(1)} %copy-done.2, ...), custom_call_target="tpu_custom_call" | custom-call | flops 1153433600 | bytes 8388608 | tf_op jit(solution)/shard_map/far_attention/pallas_call | solution.py:138
  28.1 1.7 %collective-permute-start.13 = (bf16[64,512]{1,0:T(8,128)(2,1)S(1)}, bf16[64,512]{1,0:T(8,128)(2,1)S(1)}, u32[]{:S(2)}, u32[]{:S(2)}) collective-permute-start(bf16[64,512]{1,0:T(8,128)(2,1)S(1)} %get-tuple-element.45), channel_id=1, source_target_pairs={{0,2},{1,3},{2,0},{3,1},{4,6},{5,7},{6,4},{7,5},{8,10},{9,11},{10,... | collective-permute-start | bytes 196616 | tf_op jit(solution)/shard_map/ppermute | solution.py:255
  30.3 1.7 %collective-permute-start.10 = (bf16[64,512]{1,0:T(8,128)(2,1)S(1)}, bf16[64,512]{1,0:T(8,128)(2,1)S(1)}, u32[]{:S(2)}, u32[]{:S(2)}) collective-permute-start(bf16[64,512]{1,0:T(8,128)(2,1)S(1)} %get-tuple-element.41), channel_id=1, source_target_pairs={{0,2},{1,3},{2,0},{3,1},{4,6},{5,7},{6,4},{7,5},{8,10},{9,11},{10,... | collective-permute-start | bytes 196616 | tf_op jit(solution)/shard_map/ppermute | solution.py:255
  32.6 2.2 %collective-permute-start.7 = (bf16[64,512]{1,0:T(8,128)(2,1)S(1)}, bf16[64,512]{1,0:T(8,128)(2,1)S(1)}, u32[]{:S(2)}, u32[]{:S(2)}) collective-permute-start(bf16[64,512]{1,0:T(8,128)(2,1)S(1)} %get-tuple-element.37), channel_id=1, source_target_pairs={{0,2},{1,3},{2,0},{3,1},{4,6},{5,7},{6,4},{7,5},{8,10},{9,11},{10,... | collective-permute-start | bytes 196616 | tf_op jit(solution)/shard_map/ppermute | solution.py:255
  34.8 0.8 %collective-permute-start.8 = (bf16[64,512]{1,0:T(8,128)(2,1)S(1)}, bf16[64,512]{1,0:T(8,128)(2,1)S(1)}, u32[]{:S(2)}, u32[]{:S(2)}) collective-permute-start(bf16[64,512]{1,0:T(8,128)(2,1)S(1)} %get-tuple-element.38), channel_id=1, source_target_pairs={{0,3},{1,2},{2,1},{3,0},{4,7},{5,6},{6,5},{7,4},{8,11},{9,10},{10,... | collective-permute-start | bytes 196616 | tf_op jit(solution)/shard_map/ppermute | solution.py:255
  35.6 3.5 %project.5.refs_4_ = f32[64,7168]{1,0:T(8,128)S(1)} custom-call(bf16[64,512]{1,0:T(8,128)(2,1)S(1)} %get-tuple-element.43.refs_0_, bf16[64,512]{1,0:T(8,128)(2,1)S(1)} %collective-permute-done.12.refs_1_, bf16[64,512]{1,0:T(8,128)(2,1)S(1)} %collective-permute-done.13.refs_2_, bf16[64,512]{1,0:T(8,128)(2,1)S(1)} %collective-permute-done.14.refs_3_, ...), custom_call_target="tpu_custom_call" | custom-call | flops 469762048 | bytes 7340032 | tf_op jit(solution)/shard_map/project/pallas_call | solution.py:226
  39.2 1.3 %collective-permute-start.4 = (bf16[64,512]{1,0:T(8,128)(2,1)S(1)}, bf16[64,512]{1,0:T(8,128)(2,1)S(1)}, u32[]{:S(2)}, u32[]{:S(2)}) collective-permute-start(bf16[64,512]{1,0:T(8,128)(2,1)S(1)} %get-tuple-element.33), channel_id=1, source_target_pairs={{0,2},{1,3},{2,0},{3,1},{4,6},{5,7},{6,4},{7,5},{8,10},{9,11},{10,... | collective-permute-start | bytes 196616 | tf_op jit(solution)/shard_map/ppermute | solution.py:255
  41.1 3.5 %project.6.refs_4_ = f32[64,7168]{1,0:T(8,128)S(1)} custom-call(bf16[64,512]{1,0:T(8,128)(2,1)S(1)} %get-tuple-element.39.refs_0_, bf16[64,512]{1,0:T(8,128)(2,1)S(1)} %collective-permute-done.9.refs_1_, bf16[64,512]{1,0:T(8,128)(2,1)S(1)} %collective-permute-done.10.refs_2_, ...), custom_call_target="tpu_custom_call", output_to_operand_aliasing={{}: (4, {})} | custom-call | flops 469762048 | bytes 7340032 | tf_op jit(solution)/shard_map/project/pallas_call | solution.py:226
  44.7 3.5 %project.7.refs_4_ = f32[64,7168]{1,0:T(8,128)S(1)} custom-call(bf16[64,512]{1,0:T(8,128)(2,1)S(1)} %get-tuple-element.35.refs_0_, bf16[64,512]{1,0:T(8,128)(2,1)S(1)} %collective-permute-done.6.refs_1_, bf16[64,512]{1,0:T(8,128)(2,1)S(1)} %collective-permute-done.7.refs_2_, ...), custom_call_target="tpu_custom_call", output_to_operand_aliasing={{}: (4, {})} | custom-call | flops 469762048 | bytes 7340032 | tf_op jit(solution)/shard_map/project/pallas_call | solution.py:226
  48.3 2.5 %project.9 = (bf16[32,3584]{1,0:T(8,128)(2,1)S(1)}, bf16[32,3584]{1,0:T(8,128)(2,1)S(1)}) custom-call(bf16[64,512]{1,0:T(8,128)(2,1)S(1)} %get-tuple-element.31.refs_0_, bf16[64,512]{1,0:T(8,128)(2,1)S(1)} %collective-permute-done.3.refs_1_, bf16[64,512]{1,0:T(8,128)(2,1)S(1)} %collective-permute-done.4.refs_2_, ...), custom_call_target="tpu_custom_call" | custom-call | flops 234881024 | bytes 3670016 | tf_op jit(solution)/shard_map/project/pallas_call | solution.py:226
  51.2 2.5 %project.8 = (bf16[32,3584]{1,0:T(8,128)(2,1)S(1)}, bf16[32,3584]{1,0:T(8,128)(2,1)S(1)}) custom-call(bf16[64,512]{1,0:T(8,128)(2,1)S(1)} %get-tuple-element.31.refs_0_, bf16[64,512]{1,0:T(8,128)(2,1)S(1)} %collective-permute-done.3.refs_1_, bf16[64,512]{1,0:T(8,128)(2,1)S(1)} %collective-permute-done.4.refs_2_, ...), custom_call_target="tpu_custom_call" | custom-call | flops 234881024 | bytes 3670016 | tf_op jit(solution)/shard_map/project/pallas_call | solution.py:226
  54.0 1.2 %collective-permute-start.18 = (bf16[16,3584]{1,0:T(8,128)(2,1)S(1)}, bf16[16,3584]{1,0:T(8,128)(2,1)S(1)}, u32[]{:S(2)}, u32[]{:S(2)}) collective-permute-start(bf16[16,3584]{1,0:T(8,128)(2,1)S(1)} %slice.30), channel_id=1, source_target_pairs={{0,2},{1,3},{2,0},{3,1},{4,6},{5,7},{6,4},{7,5},{8,10},{9,11},{10,... | collective-permute-start | bytes 344072 | tf_op jit(solution)/shard_map/ppermute | solution.py:255
  55.3 1.3 %collective-permute-start.16 = (bf16[16,3584]{1,0:T(8,128)(2,1)S(1)}, bf16[16,3584]{1,0:T(8,128)(2,1)S(1)}, u32[]{:S(2)}, u32[]{:S(2)}) collective-permute-start(bf16[16,3584]{1,0:T(8,128)(2,1)S(1)} %slice.31), channel_id=1, source_target_pairs={{0,2},{1,3},{2,0},{3,1},{4,6},{5,7},{6,4},{7,5},{8,10},{9,11},{10,... | collective-permute-start | bytes 344072 | tf_op jit(solution)/shard_map/ppermute | solution.py:255
  56.6 3.4 %collective-permute-done.18 = bf16[16,3584]{1,0:T(8,128)(2,1)S(1)} collective-permute-done((bf16[16,3584]{1,0:T(8,128)(2,1)S(1)}, bf16[16,3584]{1,0:T(8,128)(2,1)S(1)}, u32[]{:S(2)}, u32[]{:S(2)}) %collective-permute-start.18) | collective-permute-done | bytes 114720 | tf_op jit(solution)/shard_map/ppermute | solution.py:255
  60.1 1.9 %collective-permute-done.16 = bf16[16,3584]{1,0:T(8,128)(2,1)S(1)} collective-permute-done((bf16[16,3584]{1,0:T(8,128)(2,1)S(1)}, bf16[16,3584]{1,0:T(8,128)(2,1)S(1)}, u32[]{:S(2)}, u32[]{:S(2)}) %collective-permute-start.16) | collective-permute-done | bytes 114720 | tf_op jit(solution)/shard_map/ppermute | solution.py:255
  62.0 0.8 %reshape.3 = bf16[8,2,7168]{2,1,0:T(2,128)(2,1)} reshape(bf16[16,7168]{1,0:T(8,128)(2,1)S(1)} %pad_maximum_fusion) | data formatting | bytes 458752 | tf_op jit(solution)/shard_map/reshape | solution.py:288
  (42 shorter events, 3.2 us)
Async XLA Ops:
  1.1 10.0 %collective-permute-start.1 = (bf16[576,256]{1,0:T(8,128)(2,1)S(1)}, bf16[576,256]{1,0:T(8,128)(2,1)S(1)}, u32[]{:S(2)}, u32[]{:S(2)}) collective-permute-start(bf16[576,256]{1,0:T(8,128)(2,1)S(1)} %convert_bitcast_fusion.refs_0_), channel_id=1, source_target_pairs={{0,2},{1,3},{2,0},{3,1},{4,6},{5,7},{6,4},{7,5},{8,10},{9,11},{10,... | collective-permute-start | bytes 884744 | tf_op jit(solution)/shard_map/ppermute | solution.py:255
  4.1 7.0 %collective-permute-start = (bf16[576,256]{1,0:T(8,128)(2,1)S(1)}, bf16[576,256]{1,0:T(8,128)(2,1)S(1)}, u32[]{:S(2)}, u32[]{:S(2)}) collective-permute-start(bf16[576,256]{1,0:T(8,128)(2,1)S(1)} %convert_bitcast_fusion.refs_0_), channel_id=1, source_target_pairs={{0,1},{1,0},{2,3},{3,2},{4,5},{5,4},{6,7},{7,6},{8,9},{9,8},{10,11... | collective-permute-start | bytes 884744 | tf_op jit(solution)/shard_map/ppermute | solution.py:255
  11.1 12.0 %collective-permute-start.2 = (bf16[576,256]{1,0:T(8,128)(2,1)S(1)}, bf16[576,256]{1,0:T(8,128)(2,1)S(1)}, u32[]{:S(2)}, u32[]{:S(2)}) collective-permute-start(bf16[576,256]{1,0:T(8,128)(2,1)S(1)} %collective-permute-done.1.refs_0_), channel_id=1, source_target_pairs={{0,1},{1,0},{2,3},{3,2},{4,5},{5,4},{6,7},{7,6},{8,9},{9,8},{10,11... | collective-permute-start | bytes 884744 | tf_op jit(solution)/shard_map/ppermute | solution.py:255
  11.1 1.3 %copy-start.1 = (bf16[8,2,64,576]{3,2,1,0:T(8,128)(2,1)S(1)}, bf16[8,2,64,576]{3,2,1,0:T(8,128)(2,1)}, u32[]{:S(2)}) copy-start(bf16[8,2,64,576]{3,2,1,0:T(8,128)(2,1)} %q_ref.3) | copy-start | bytes 3538948
  12.4 1.7 %copy-start.3 = (bf16[8,256,576]{1,2,0:T(8,128)(2,1)S(1)}, bf16[8,256,576]{1,2,0:T(8,128)(2,1)}, u32[]{:S(2)}) copy-start(bf16[8,256,576]{1,2,0:T(8,128)(2,1)} %param.8) | copy-start | bytes 7077892
  14.1 0.7 %copy-start.4 = (bf16[8,2,576]{2,1,0:T(2,128)(2,1)S(1)}, bf16[8,2,576]{2,1,0:T(2,128)(2,1)}, u32[]{:S(2)}) copy-start(bf16[8,2,576]{2,1,0:T(2,128)(2,1)} %new_ref.1) | copy-start | bytes 55300
  15.5 7.6 %copy-start.2 = (bf16[8,2,64,576]{3,2,1,0:T(8,128)(2,1)S(1)}, bf16[8,2,64,576]{3,2,1,0:T(8,128)(2,1)}, u32[]{:S(2)}) copy-start(bf16[8,2,64,576]{3,2,1,0:T(8,128)(2,1)} %q_ref.3) | copy-start | bytes 3538948
  23.1 12.5 %copy-start = (bf16[16,512,128]{2,1,0:T(8,128)(2,1)S(1)}, bf16[16,512,128]{2,1,0:T(8,128)(2,1)}, u32[]{:S(2)}) copy-start(bf16[16,512,128]{2,1,0:T(8,128)(2,1)} %refs_5_.9) | copy-start | bytes 6291460
  27.5 2.8 %collective-permute-start.6 = (bf16[64,512]{1,0:T(8,128)(2,1)S(1)}, bf16[64,512]{1,0:T(8,128)(2,1)S(1)}, u32[]{:S(2)}, u32[]{:S(2)}) collective-permute-start(bf16[64,512]{1,0:T(8,128)(2,1)S(1)} %get-tuple-element.36), channel_id=1, source_target_pairs={{0,1},{1,0},{2,3},{3,2},{4,5},{5,4},{6,7},{7,6},{8,9},{9,8},{10,11... | collective-permute-start | bytes 196616 | tf_op jit(solution)/shard_map/ppermute | solution.py:255
  28.0 4.0 %collective-permute-start.12 = (bf16[64,512]{1,0:T(8,128)(2,1)S(1)}, bf16[64,512]{1,0:T(8,128)(2,1)S(1)}, u32[]{:S(2)}, u32[]{:S(2)}) collective-permute-start(bf16[64,512]{1,0:T(8,128)(2,1)S(1)} %get-tuple-element.44), channel_id=1, source_target_pairs={{0,1},{1,0},{2,3},{3,2},{4,5},{5,4},{6,7},{7,6},{8,9},{9,8},{10,11... | collective-permute-start | bytes 196616 | tf_op jit(solution)/shard_map/ppermute | solution.py:255
  28.1 4.4 %collective-permute-start.13 = (bf16[64,512]{1,0:T(8,128)(2,1)S(1)}, bf16[64,512]{1,0:T(8,128)(2,1)S(1)}, u32[]{:S(2)}, u32[]{:S(2)}) collective-permute-start(bf16[64,512]{1,0:T(8,128)(2,1)S(1)} %get-tuple-element.45), channel_id=1, source_target_pairs={{0,2},{1,3},{2,0},{3,1},{4,6},{5,7},{6,4},{7,5},{8,10},{9,11},{10,... | collective-permute-start | bytes 196616 | tf_op jit(solution)/shard_map/ppermute | solution.py:255
  29.9 4.9 %collective-permute-start.14 = (bf16[64,512]{1,0:T(8,128)(2,1)S(1)}, bf16[64,512]{1,0:T(8,128)(2,1)S(1)}, u32[]{:S(2)}, u32[]{:S(2)}) collective-permute-start(bf16[64,512]{1,0:T(8,128)(2,1)S(1)} %get-tuple-element.46), channel_id=1, source_target_pairs={{0,3},{1,2},{2,1},{3,0},{4,7},{5,6},{6,5},{7,4},{8,11},{9,10},{10,... | collective-permute-start | bytes 196616 | tf_op jit(solution)/shard_map/ppermute | solution.py:255
  29.9 9.2 %collective-permute-start.9 = (bf16[64,512]{1,0:T(8,128)(2,1)S(1)}, bf16[64,512]{1,0:T(8,128)(2,1)S(1)}, u32[]{:S(2)}, u32[]{:S(2)}) collective-permute-start(bf16[64,512]{1,0:T(8,128)(2,1)S(1)} %get-tuple-element.40), channel_id=1, source_target_pairs={{0,1},{1,0},{2,3},{3,2},{4,5},{5,4},{6,7},{7,6},{8,9},{9,8},{10,11... | collective-permute-start | bytes 196616 | tf_op jit(solution)/shard_map/ppermute | solution.py:255
  30.3 9.0 %collective-permute-start.10 = (bf16[64,512]{1,0:T(8,128)(2,1)S(1)}, bf16[64,512]{1,0:T(8,128)(2,1)S(1)}, u32[]{:S(2)}, u32[]{:S(2)}) collective-permute-start(bf16[64,512]{1,0:T(8,128)(2,1)S(1)} %get-tuple-element.41), channel_id=1, source_target_pairs={{0,2},{1,3},{2,0},{3,1},{4,6},{5,7},{6,4},{7,5},{8,10},{9,11},{10,... | collective-permute-start | bytes 196616 | tf_op jit(solution)/shard_map/ppermute | solution.py:255
  32.0 8.5 %collective-permute-start.11 = (bf16[64,512]{1,0:T(8,128)(2,1)S(1)}, bf16[64,512]{1,0:T(8,128)(2,1)S(1)}, u32[]{:S(2)}, u32[]{:S(2)}) collective-permute-start(bf16[64,512]{1,0:T(8,128)(2,1)S(1)} %get-tuple-element.42), channel_id=1, source_target_pairs={{0,3},{1,2},{2,1},{3,0},{4,7},{5,6},{6,5},{7,4},{8,11},{9,10},{10,... | collective-permute-start | bytes 196616 | tf_op jit(solution)/shard_map/ppermute | solution.py:255
  32.6 12.1 %collective-permute-start.7 = (bf16[64,512]{1,0:T(8,128)(2,1)S(1)}, bf16[64,512]{1,0:T(8,128)(2,1)S(1)}, u32[]{:S(2)}, u32[]{:S(2)}) collective-permute-start(bf16[64,512]{1,0:T(8,128)(2,1)S(1)} %get-tuple-element.37), channel_id=1, source_target_pairs={{0,2},{1,3},{2,0},{3,1},{4,6},{5,7},{6,4},{7,5},{8,10},{9,11},{10,... | collective-permute-start | bytes 196616 | tf_op jit(solution)/shard_map/ppermute | solution.py:255
  34.8 9.9 %collective-permute-start.8 = (bf16[64,512]{1,0:T(8,128)(2,1)S(1)}, bf16[64,512]{1,0:T(8,128)(2,1)S(1)}, u32[]{:S(2)}, u32[]{:S(2)}) collective-permute-start(bf16[64,512]{1,0:T(8,128)(2,1)S(1)} %get-tuple-element.38), channel_id=1, source_target_pairs={{0,3},{1,2},{2,1},{3,0},{4,7},{5,6},{6,5},{7,4},{8,11},{9,10},{10,... | collective-permute-start | bytes 196616 | tf_op jit(solution)/shard_map/ppermute | solution.py:255
  39.1 9.1 %collective-permute-start.3 = (bf16[64,512]{1,0:T(8,128)(2,1)S(1)}, bf16[64,512]{1,0:T(8,128)(2,1)S(1)}, u32[]{:S(2)}, u32[]{:S(2)}) collective-permute-start(bf16[64,512]{1,0:T(8,128)(2,1)S(1)} %get-tuple-element.32), channel_id=1, source_target_pairs={{0,1},{1,0},{2,3},{3,2},{4,5},{5,4},{6,7},{7,6},{8,9},{9,8},{10,11... | collective-permute-start | bytes 196616 | tf_op jit(solution)/shard_map/ppermute | solution.py:255
  39.2 9.0 %collective-permute-start.4 = (bf16[64,512]{1,0:T(8,128)(2,1)S(1)}, bf16[64,512]{1,0:T(8,128)(2,1)S(1)}, u32[]{:S(2)}, u32[]{:S(2)}) collective-permute-start(bf16[64,512]{1,0:T(8,128)(2,1)S(1)} %get-tuple-element.33), channel_id=1, source_target_pairs={{0,2},{1,3},{2,0},{3,1},{4,6},{5,7},{6,4},{7,5},{8,10},{9,11},{10,... | collective-permute-start | bytes 196616 | tf_op jit(solution)/shard_map/ppermute | solution.py:255
  40.5 7.7 %collective-permute-start.5 = (bf16[64,512]{1,0:T(8,128)(2,1)S(1)}, bf16[64,512]{1,0:T(8,128)(2,1)S(1)}, u32[]{:S(2)}, u32[]{:S(2)}) collective-permute-start(bf16[64,512]{1,0:T(8,128)(2,1)S(1)} %get-tuple-element.34), channel_id=1, source_target_pairs={{0,3},{1,2},{2,1},{3,0},{4,7},{5,6},{6,5},{7,4},{8,11},{9,10},{10,... | collective-permute-start | bytes 196616 | tf_op jit(solution)/shard_map/ppermute | solution.py:255
  50.8 3.2 %collective-permute-start.17 = (bf16[32,3584]{1,0:T(8,128)(2,1)S(1)}, bf16[32,3584]{1,0:T(8,128)(2,1)S(1)}, u32[]{:S(2)}, u32[]{:S(2)}) collective-permute-start(bf16[32,3584]{1,0:T(8,128)(2,1)S(1)} %get-tuple-element.50), channel_id=1, source_target_pairs={{0,1},{1,0},{2,3},{3,2},{4,5},{5,4},{6,7},{7,6},{8,9},{9,8},{10,11... | collective-permute-start | bytes 688136 | tf_op jit(solution)/shard_map/ppermute | solution.py:255
  53.7 1.6 %collective-permute-start.15 = (bf16[32,3584]{1,0:T(8,128)(2,1)S(1)}, bf16[32,3584]{1,0:T(8,128)(2,1)S(1)}, u32[]{:S(2)}, u32[]{:S(2)}) collective-permute-start(bf16[32,3584]{1,0:T(8,128)(2,1)S(1)} %get-tuple-element.48), channel_id=1, source_target_pairs={{0,1},{1,0},{2,3},{3,2},{4,5},{5,4},{6,7},{7,6},{8,9},{9,8},{10,11... | collective-permute-start | bytes 688136 | tf_op jit(solution)/shard_map/ppermute | solution.py:255
  54.0 6.0 %collective-permute-start.18 = (bf16[16,3584]{1,0:T(8,128)(2,1)S(1)}, bf16[16,3584]{1,0:T(8,128)(2,1)S(1)}, u32[]{:S(2)}, u32[]{:S(2)}) collective-permute-start(bf16[16,3584]{1,0:T(8,128)(2,1)S(1)} %slice.30), channel_id=1, source_target_pairs={{0,2},{1,3},{2,0},{3,1},{4,6},{5,7},{6,4},{7,5},{8,10},{9,11},{10,... | collective-permute-start | bytes 344072 | tf_op jit(solution)/shard_map/ppermute | solution.py:255
  55.3 6.6 %collective-permute-start.16 = (bf16[16,3584]{1,0:T(8,128)(2,1)S(1)}, bf16[16,3584]{1,0:T(8,128)(2,1)S(1)}, u32[]{:S(2)}, u32[]{:S(2)}) collective-permute-start(bf16[16,3584]{1,0:T(8,128)(2,1)S(1)} %slice.31), channel_id=1, source_target_pairs={{0,2},{1,3},{2,0},{3,1},{4,6},{5,7},{6,4},{7,5},{8,10},{9,11},{10,... | collective-permute-start | bytes 344072 | tf_op jit(solution)/shard_map/ppermute | solution.py:255
  (1 other events, 0.7 us)

commit v2 on v0

v2 whole, which is shorter than its diff:
```python
import functools
import math

import jax
import jax.numpy as jnp
from jax import lax
from jax.experimental import pallas as pl
from jax.experimental.pallas import tpu as pltpu
from jax.sharding import PartitionSpec as P

LATENT = 512
QK_HEAD = 192
SCALE2 = QK_HEAD**-0.5 * math.log2(math.e)
NEG = -1e30
CHUNK_HEADS = 4
OUT_PARTS = 2
BLOCK = 256
MIB = 2**20
NEAR_VMEM = 12 * MIB


def dot_nt(a, b):
    return lax.dot_general(a, b, (((1,), (1,)), ((), ())), preferred_element_type=jnp.float32)


def dot_nn(a, b):
    return jnp.dot(a, b, preferred_element_type=jnp.float32)


def update(scores, m, l, acc, probs_into):
    new_m = m
    for s in scores:
        new_m = jnp.maximum(new_m, jnp.max(s, axis=1, keepdims=True))
    shrink = jnp.exp2((m - new_m) * SCALE2)
    weights = [jnp.exp2((s - new_m) * SCALE2) for s in scores]
    l = l * shrink
    for p in weights:
        l += jnp.sum(p, axis=1, keepdims=True)
    return new_m, l, probs_into(acc * shrink, [p.astype(jnp.bfloat16) for p in weights])


def in_turn(tasks, score, finish):
    before = None
    for task in tasks:
        now = score(task)
        if before is not None:
            finish(*before)
        before = (task, now)
    finish(*before)


def near_call(suffix_len, queries, suffix_t, new_latent, own, beside, w_out, ahead, unit_rows, units, axis_size):
    rows, steps, heads, width = queries.shape
    tile = heads // units
    share = heads // axis_size
    per = steps * heads
    small = (queries, suffix_len, new_latent)

    def kernel(len_ref, q_ref, suf_ref, new_ref, own_ref, beside_ref, w_ref, *refs):
        w_ahead, (qs_ref, m_ref, l_ref, acc_ref) = refs[:ahead], refs[ahead : ahead + 4]
        q_buf, len_buf, new_buf, suf_buf, sems, suf_sems, w_sems = refs[ahead + 4 :]
        pairs = [(q_ref, q_buf), (len_ref, len_buf), (new_ref, new_buf)]
        copies = [pltpu.make_async_copy(x, y, sems.at[i]) for i, (x, y) in enumerate(pairs)]
        suf_copies = [
            pltpu.make_async_copy(suf_ref.at[r], suf_buf.at[r], suf_sems.at[r]) for r in range(rows)
        ]
        w_copies = [
            pltpu.make_async_copy(w_ref.at[pl.ds(i * unit_rows, unit_rows)], to, w_sems.at[i])
            for i, to in enumerate(w_ahead)
        ]
        for copy in copies + suf_copies + w_copies:
            copy.start()
        for copy in copies:
            copy.wait()
        keys = [own_ref[...], beside_ref[...]]

        def sort(r):
            by_unit = [[] for _ in range(units)]
            for s in range(steps):
                q = q_buf[r, s].astype(jnp.float32)
                for u in range(units):
                    picked = [
                        q[j * share + u * CHUNK_HEADS : j * share + (u + 1) * CHUNK_HEADS]
                        for j in range(axis_size)
                    ]
                    by_unit[u].append(jnp.concatenate(picked, axis=0).astype(jnp.bfloat16))
            for u in range(units):
                for s in range(steps):
                    qs_ref[u, r * steps + s] = by_unit[u][s]
            return jnp.concatenate([x for unit in by_unit for x in unit], axis=0)

        def score(first):
            q = [sort(first + i) for i in range(BLOCK // per)]
            both = jnp.concatenate(q, axis=0)
            scores = [dot_nn(both, k) for k in keys]
            old, new = [], []
            for i, x in enumerate(q):
                suf_copies[first + i].wait()
                s = dot_nn(x, suf_buf[first + i])
                at = lax.broadcasted_iota(jnp.int32, s.shape, 1)
                old.append(jnp.where(at < len_buf[first + i], s, NEG))
                s = dot_nt(x, new_buf[first + i])
                step = lax.broadcasted_iota(jnp.int32, s.shape, 0) // tile % steps
                token = lax.broadcasted_iota(jnp.int32, s.shape, 1)
                new.append(jnp.where(token <= step, s, NEG))
            return scores + [jnp.concatenate(x, axis=0) for x in (old, new)]

        def finish(first, scores):
            m = functools.reduce(
                jnp.maximum, [jnp.max(s, axis=1, keepdims=True) for s in scores]
            )
            weights = [jnp.exp2((s - m) * SCALE2) for s in scores]
            l = sum(jnp.sum(p, axis=1, keepdims=True) for p in weights)
            probs = [p.astype(jnp.bfloat16) for p in weights]
            acc = dot_nt(probs[0], keys[0][:LATENT]) + dot_nt(probs[1], keys[1][:LATENT])
            new_probs = probs[3].astype(jnp.float32)
            for i in range(BLOCK // per):
                here = slice(i * per, (i + 1) * per)
                part = acc[here] + dot_nt(probs[2][here], suf_buf[first + i, :LATENT])
                values = new_buf[first + i][:, :LATENT].astype(jnp.float32)
                for t in range(steps):
                    part += new_probs[here, t : t + 1] * values[t : t + 1]
                there = slice((first + i) * steps, (first + i + 1) * steps)
                lead = (units, steps, tile)
                m_ref[:, there] = jnp.broadcast_to(m[here], (per, 128)).reshape(lead + (128,))
                l_ref[:, there] = jnp.broadcast_to(l[here], (per, 128)).reshape(lead + (128,))
                acc_ref[:, there] = part.reshape(lead + (LATENT,))

        in_turn(range(0, rows, BLOCK // per), score, finish)
        for copy in w_copies:
            copy.wait()

    vmem, hbm = pl.BlockSpec(memory_space=pltpu.VMEM), pl.BlockSpec(memory_space=pltpu.HBM)
    lead = (units, rows * steps, tile)
    f32 = jnp.float32
    return pl.pallas_call(
        kernel,
        in_specs=[hbm, hbm, hbm, hbm, vmem, vmem, hbm],
        out_specs=[vmem] * (ahead + 4),
        out_shape=[pltpu.VMEM((unit_rows, w_out.shape[1]), w_out.dtype)] * ahead
        + [
            jax.ShapeDtypeStruct(lead + (width,), queries.dtype),
            jax.ShapeDtypeStruct(lead + (128,), f32),
            jax.ShapeDtypeStruct(lead + (128,), f32),
            jax.ShapeDtypeStruct(lead + (LATENT,), f32),
        ],
        scratch_shapes=[
            pltpu.VMEM(queries.shape, queries.dtype),
            pltpu.SMEM(suffix_len.shape, jnp.int32),
            pltpu.VMEM(new_latent.shape, jnp.bfloat16),
            pltpu.VMEM(suffix_t.shape, jnp.bfloat16),
            pltpu.SemaphoreType.DMA((len(small),)),
            pltpu.SemaphoreType.DMA((rows,)),
            pltpu.SemaphoreType.DMA((ahead,)),
        ],
        compiler_params=pltpu.CompilerParams(vmem_limit_bytes=NEAR_VMEM),
        cost_estimate=pl.CostEstimate(
            flops=4 * rows * per * 1100 * 768,
            bytes_accessed=4 * MIB + 2 * ahead * unit_rows * w_out.shape[1],
            transcendentals=rows * per * 768,
        ),
        name="near_attention",
    )(suffix_len, queries, suffix_t, new_latent, own, beside, w_out)


def merge(units, keys, q_ref, m_ref, l_ref, acc_ref, store):
    _, pairs, tile, width = q_ref.shape
    step = BLOCK // tile
    tasks = [(u, slice(first, first + step)) for u in units for first in range(0, pairs, step)]

    def score(here):
        q = q_ref[here].reshape(BLOCK, width)
        return [dot_nn(q, k) for k in keys]

    def finish(here, scores):
        store(
            here,
            *update(
                scores,
                m_ref[here].reshape(BLOCK, 128)[:, 0:1],
                l_ref[here].reshape(BLOCK, 128)[:, 0:1],
                acc_ref[here].reshape(BLOCK, LATENT),
                lambda acc, ps: acc + sum(dot_nt(p, k[:LATENT]) for p, k in zip(ps, keys)),
            ),
        )

    in_turn(tasks, score, finish)


def middle_call(queries, state, keys):
    units, pairs, tile, _ = queries.shape

    def kernel(q_ref, m_ref, l_ref, acc_ref, *refs):
        key_refs, (m_out, l_out, acc_out) = refs[: len(keys)], refs[len(keys) :]

        def store(here, m, l, acc):
            lead = (BLOCK // tile, tile)
            m_out[here] = jnp.broadcast_to(m, (BLOCK, 128)).reshape(lead + (128,))
            l_out[here] = jnp.broadcast_to(l, (BLOCK, 128)).reshape(lead + (128,))
            acc_out[here] = acc.reshape(lead + (LATENT,))

        merge(range(units), [k[...] for k in key_refs], q_ref, m_ref, l_ref, acc_ref, store)

    vmem = pl.BlockSpec(memory_space=pltpu.VMEM)
    return pl.pallas_call(
        kernel,
        in_specs=[vmem] * (4 + len(keys)),
        out_specs=[vmem] * 3,
        out_shape=[jax.ShapeDtypeStruct(x.shape, x.dtype) for x in state],
        compiler_params=pltpu.CompilerParams(vmem_limit_bytes=10 * MIB),
        cost_estimate=pl.CostEstimate(
            flops=2 * units * pairs * tile * 1100 * 256 * len(keys),
            bytes_accessed=4 * MIB,
            transcendentals=0,
        ),
        name="middle_attention",
    )(queries, *state, *keys)


def far_call(first, size, queries, state, keys, axis_size):
    _, pairs, tile, _ = queries.shape
    per_unit = pairs * tile

    def kernel(q_ref, m_ref, l_ref, acc_ref, *refs):
        key_refs, out_refs, done = refs[: len(keys)], refs[len(keys) : -1], refs[-1]

        def store(here, m, l, acc):
            attended = acc / l
            at = (here[0] - first) * per_unit + here[1].start * tile
            for g in range(LATENT // 128):
                done[g, at : at + BLOCK, :] = attended[:, g * 128 : (g + 1) * 128]

        keys_now = [k[...] for k in key_refs]
        merge(range(first, first + size), keys_now, q_ref, m_ref, l_ref, acc_ref, store)
        me = lax.axis_index("roll")
        for k in range(axis_size):
            there = jnp.bitwise_xor(me, k) * CHUNK_HEADS
            for u in range(size):
                for i in range(CHUNK_HEADS):
                    at = (u * CHUNK_HEADS + i) * pairs
                    for g in range(LATENT // 128):
                        out_refs[k][at : at + pairs, g * 128 : (g + 1) * 128] = done[
                            g, pl.ds(u * per_unit + there + i, pairs, stride=tile), :
                        ].astype(jnp.bfloat16)

    vmem = pl.BlockSpec(memory_space=pltpu.VMEM)
    return pl.pallas_call(
        kernel,
        in_specs=[vmem] * (4 + len(keys)),
        out_specs=[vmem] * axis_size,
        out_shape=[jax.ShapeDtypeStruct((size * CHUNK_HEADS * pairs, LATENT), jnp.bfloat16)]
        * axis_size,
        scratch_shapes=[pltpu.VMEM((LATENT // 128, size * per_unit + tile, 128), jnp.float32)],
        compiler_params=pltpu.CompilerParams(vmem_limit_bytes=10 * MIB),
        cost_estimate=pl.CostEstimate(
            flops=2 * size * per_unit * 1100 * 256 * len(keys), bytes_accessed=MIB, transcendentals=0
        ),
        name="far_attention",
    )(queries, *state, *keys)


def project(first_head, heads, pieces, acc, w_uv, w_units, kept=None, first_col=0, cols=None, bring=(None, ())):
    n_pieces = len(pieces)
    pairs = pieces[0].shape[0] // heads
    total_rows = n_pieces * pairs
    unit_rows, width = w_units[0].shape
    cols = width if cols is None else cols
    block = next(b for b in (1792, 1024, 896, 512, 128) if cols % b == 0)
    w_all, missing = bring

    def kernel(*refs):
        refs = list(refs)
        piece_refs = [refs.pop(0) for _ in pieces]
        acc_ref = refs.pop(0) if acc is not None else None
        uv_ref = refs.pop(0)
        w_refs = [refs.pop(0) for _ in w_units]
        copies = []
        if missing:
            all_ref, sem = refs.pop(0), refs[-1]
            for i, u in enumerate(missing):
                rows = pl.ds(u * unit_rows, unit_rows)
                copies.append(pltpu.make_async_copy(all_ref.at[rows], refs[1 + i], sem.at[i]))
                copies[-1].start()
        head_out = []
        for i in range(heads):
            rows = jnp.concatenate([p[i * pairs : (i + 1) * pairs, :] for p in piece_refs], axis=0)
            head_out.append(dot_nn(rows, uv_ref[first_head + i]).astype(jnp.bfloat16))
        head_out = jnp.concatenate(head_out, axis=1)
        for b in range(cols // block):
            here = slice(b * block, (b + 1) * block)
            there = slice(first_col + b * block, first_col + (b + 1) * block)
            total = sum(
                dot_nn(head_out[:, u * unit_rows : (u + 1) * unit_rows], w_ref[:, there])
                for u, w_ref in enumerate(w_refs)
            )
            if acc_ref is not None:
                total += acc_ref[:, there]
            if kept is None:
                refs[0][:, here] = total
                continue
            at = [0, 0]
            for k in range(n_pieces):
                side = 0 if k in kept else 1
                refs[side][at[side] * pairs : (at[side] + 1) * pairs, here] = total[
                    k * pairs : (k + 1) * pairs
                ].astype(jnp.bfloat16)
                at[side] += 1
        for copy in copies:
            copy.wait()

    vmem, hbm = pl.BlockSpec(memory_space=pltpu.VMEM), pl.BlockSpec(memory_space=pltpu.HBM)
    operands = list(pieces) + ([acc] if acc is not None else []) + [w_uv, *w_units]
    in_specs = [vmem] * len(operands)
    scratch = []
    if kept is not None:
        out_shape = [jax.ShapeDtypeStruct((total_rows // 2, cols), jnp.bfloat16)] * 2
    else:
        out_shape = [jax.ShapeDtypeStruct((total_rows, cols), jnp.float32)]
    if missing:
        operands.append(w_all)
        in_specs.append(hbm)
        out_shape += [pltpu.VMEM(w_units[0].shape, w_all.dtype)] * len(missing)
        scratch = [pltpu.SemaphoreType.DMA((len(missing),))]
    depth = heads * w_uv.shape[2]
    return pl.pallas_call(
        kernel,
        in_specs=in_specs,
        out_specs=[vmem] * len(out_shape),
        out_shape=out_shape,
        scratch_shapes=scratch,
        compiler_params=pltpu.CompilerParams(vmem_limit_bytes=8 * MIB),
        cost_estimate=pl.CostEstimate(
            flops=8 * total_rows * depth * cols, bytes_accessed=2 * depth * cols, transcendentals=0
        ),
        input_output_aliases={n_pieces: 0} if acc is not None and kept is None else {},
        name="project",
    )(*operands)


def last_sums(rows, steps, width, parts):
    pairs = rows * steps
    flat = [x for part in parts for x in part]
    cols = width // len(parts)

    def kernel(*refs):
        refs, out_ref = list(refs[:-1]), refs[-1]
        for i, part in enumerate(parts):
            total = None
            for _, first in part:
                x = refs.pop(0)[first : first + pairs, :].astype(jnp.float32)
                total = x if total is None else total + x
            out_ref[:, :, i * cols : (i + 1) * cols] = total.astype(jnp.bfloat16).reshape(
                rows, steps, cols
            )

    vmem = pl.BlockSpec(memory_space=pltpu.VMEM)
    return pl.pallas_call(
        kernel,
        in_specs=[vmem] * len(flat),
        out_specs=vmem,
        out_shape=jax.ShapeDtypeStruct((rows, steps, width), jnp.bfloat16),
        compiler_params=pltpu.CompilerParams(vmem_limit_bytes=8 * MIB),
        name="last_sums",
    )(*[x for x, _ in flat])


def on_device(prefix_latent, suffix_latent, suffix_len, new_latent, queries, w_uv, w_out):
    n = lax.axis_size("roll")
    rows, steps, heads, _ = queries.shape
    pairs = rows * steps
    width = w_out.shape[1]
    share = heads // n
    units = share // CHUNK_HEADS
    unit_rows = CHUNK_HEADS * w_uv.shape[2]
    chunks = [(0, 1), (1, units - 2), (units - 1, 1)] if units > 2 else [(u, 1) for u in range(units)]
    ahead = max(1, units // 2)

    def swap(x, k):
        return lax.ppermute(x, "roll", [(i, i ^ k) for i in range(n)])

    own = prefix_latent.T.astype(jnp.bfloat16)
    across = [swap(own, k) for k in range(2, n, 2)]
    beside = swap(own, 1)
    *w_units, queries, m, l, acc = near_call(
        suffix_len,
        queries,
        jnp.swapaxes(suffix_latent, 1, 2),
        new_latent,
        own,
        beside,
        w_out,
        ahead,
        unit_rows,
        units,
        n,
    )
    *across, m = lax.optimization_barrier((*across, m))
    forwarded = [swap(x, 1) for x in across]
    state = middle_call(queries, (m, l, acc), across)
    got = []
    for first, size in chunks:
        mine = far_call(first, size, queries, state, forwarded, n)
        there = [mine[0]] + [None] * (n - 1)
        for k in list(range(2, n)) + [1]:
            there[k] = swap(mine[k], k)
        got.append(there)
    acc = None
    for c, (first, size) in enumerate(chunks[:-1]):
        missing = range(len(w_units), units) if c == 0 else ()
        acc, *brought = project(
            first * CHUNK_HEADS,
            size * CHUNK_HEADS,
            got[c],
            acc,
            w_uv,
            w_units[first : first + size],
            bring=(w_out, missing),
        )
        w_units += brought
    first, size = chunks[-1]
    cols = width // OUT_PARTS
    parts = []
    for part in range(OUT_PARTS):
        odd = part % 2
        kept = tuple(k for k in range(n) if k == 0 or (k != 1 and k % 2 == odd))
        keep, send = project(
            first * CHUNK_HEADS,
            size * CHUNK_HEADS,
            got[-1],
            acc,
            w_uv,
            w_units[first : first + size],
            kept=kept,
            first_col=part * cols,
            cols=cols,
        )
        left = [k for k in range(n) if k not in kept]
        recv = swap(send, 1)

        def piece(x, i):
            return x[i * pairs : (i + 1) * pairs].astype(jnp.float32)

        terms = [(keep, 0), (recv, left.index(1) * pairs)]
        for i, k in enumerate(kept[1:]):
            both = piece(keep, i + 1) + piece(recv, left.index(k ^ 1))
            terms.append((swap(both.astype(jnp.bfloat16), k), 0))
        parts.append(terms)
    return last_sums(rows, steps, width, parts)


def solution(mesh):
    in_specs = (
        P(("group", "roll"), None),
        P(("group", "roll"), None, None),
        P(("group", "roll")),
        P(("group", "roll"), None, None),
        P(("group", "roll"), None, None, None),
        P("roll", None, None),
        P("roll", None),
    )
    out_specs = P(("group", "roll"), None, None)
    return jax.shard_map(
        on_device, mesh=mesh, in_specs=in_specs, out_specs=out_specs, check_vma=False
    )
```

time: 103 us -> 46.4 us (0.45)
  waiting for transfers between devices: 39.3 us -> 6.86 us
  matrix products: 24.5 us -> 0 us
  Pallas kernels: 0 us -> 21.3 us
  blocking collectives: 16.9 us -> 0 us
  between operations: 13.5 us -> 0.16 us
  starting transfers between devices: 0.04 us -> 12.2 us
  other arithmetic: 4.22 us -> 1.15 us
    dot_general x8 -> x0, matrix products: 24.5 us -> none  [the longest x1 12.2 us: on_device(): result = jnp.dot(flat_rows, w_out, preferred_element_type=jnp.float32)]
    unnamed x3 -> x0, waiting for transfers between devices: 24.3 us -> none
    pallas_call x0 -> x10, Pallas kernels: none -> 21.3 us  [the longest x4 10 us: project(): pl.pallas_call(kernel, in_specs=in_specs, out_specs=[vmem] * len(out_shap...]
    all_to_all x1 -> x0, blocking collectives: 16.9 us -> none  [on_device(): lax.all_to_all(attended, 'roll', split_axis=2, concat_axis=0, tiled=True)]
    all_gather x1 -> x0, waiting for transfers between devices: 15.1 us -> none  [on_device(): lax.all_gather(prefix_latent.astype(jnp.bfloat16), 'roll', axis=0, tiled=...]
    ppermute x0 -> x16, starting transfers between devices: none -> 12.2 us  [swap(): return lax.ppermute(x, 'roll', [(i, i ^ k) for i in range(n)])]
    ppermute x0 -> x16, waiting for transfers between devices: none -> 6.86 us  [swap(): return lax.ppermute(x, 'roll', [(i, i ^ k) for i in range(n)])]
    unnamed x9 -> x10, local copies, waits for them, and re-layouts: 1.19 us -> 4.37 us
  transfers between devices with their start and end apart: 2 -> 16, of which waited for: 2 -> 4; matrix products, arithmetic and copies ran while one was open for 5% -> 0% of each run, Pallas kernels for 0% -> 41%
where the time goes in v2:
time: 46.4 us; the launch traced here: 46.1 us
  Pallas kernels  21.3 us (46%)
  starting transfers between devices  12.2 us (26%)
  waiting for transfers between devices  6.86 us (15%)
  local copies, waits for them, and re-layouts  4.37 us (9%)
  other arithmetic  1.15 us (2%)
    ppermute x16, starting transfers between devices, swap(): return lax.ppermute(x, 'roll', [(i, i ^ k) for i in range(n)])  12.2 us
    pallas_call x4, Pallas kernels, project(): pl.pallas_call(kernel, in_specs=in_specs, out_specs=[vmem] * len(out_shap...  10 us
    ppermute x16, waiting for transfers between devices, swap(): return lax.ppermute(x, 'roll', [(i, i ^ k) for i in range(n)])  6.86 us
    pallas_call x1, Pallas kernels, near_call(): pl.pallas_call(kernel, in_specs=[hbm, hbm, hbm, hbm, vmem, vmem, hbm], ou...  5.88 us
    unnamed x10, local copies, waits for them, and re-layouts  4.37 us
    pallas_call x3, Pallas kernels, far_call(): pl.pallas_call(kernel, in_specs=[vmem] * (4 + len(keys)), out_specs=[vmem...  2.96 us
    pallas_call x1, Pallas kernels, middle_call(): pl.pallas_call(kernel, in_specs=[vmem] * (4 + len(keys)), out_specs=[vmem...  1.63 us
    convert_element_type x1, other arithmetic, on_device(): own = prefix_latent.T.astype(jnp.bfloat16)  1.09 us
  transfers between devices with their start and end apart: 16, of which 4 were waited for; matrix products, arithmetic and copies ran while one was open for 0% of the time, Pallas kernels for 41%

profile of v2, /device:TPU:0, one launch (start us, length us, event | category | flops | bytes accessed | tf_op | source)
XLA Modules:
  0.0 46.1 jit_solution(12408048981755005880)
XLA Ops:
  0.0 1.1 %convert_bitcast_fusion.own_ref = bf16[576,256]{1,0:T(8,128)(2,1)S(1)} fusion(f32[256,576]{0,1:T(8,128)} %param.7), kind=kLoop, calls=%fused_computation | loop fusion | flops 147456 | bytes 884736 | tf_op jit(solution)/shard_map/convert_element_type | solution.py:381
  1.6 2.6 %collective-permute-start.1 = (bf16[576,256]{1,0:T(8,128)(2,1)S(1)}, bf16[576,256]{1,0:T(8,128)(2,1)S(1)}, u32[]{:S(2)}, u32[]{:S(2)}) collective-permute-start(bf16[576,256]{1,0:T(8,128)(2,1)S(1)} %convert_bitcast_fusion.own_ref), channel_id=1, source_target_pairs={{0,2},{1,3},{2,0},{3,1},{4,6},{5,7},{6,4},{7,5},{8,10},{9,11},{10,... | collective-permute-start | bytes 884744 | tf_op jit(solution)/shard_map/ppermute | solution.py:379
  4.2 1.7 %copy-done.1 = bf16[8,256,576]{1,2,0:T(8,128)(2,1)S(1)} copy-done((bf16[8,256,576]{1,2,0:T(8,128)(2,1)S(1)}, bf16[8,256,576]{1,2,0:T(8,128)(2,1)}, u32[]{:S(2)}) %copy-start.1) | copy-done | bytes 2359320
  5.9 1.3 %copy-done.2 = bf16[8,2,64,576]{3,2,1,0:T(8,128)(2,1)S(1)} copy-done((bf16[8,2,64,576]{3,2,1,0:T(8,128)(2,1)S(1)}, bf16[8,2,64,576]{3,2,1,0:T(8,128)(2,1)}, u32[]{:S(2)}) %copy-start.2) | copy-done | bytes 1179672
  7.2 0.7 %copy-done.3 = bf16[8,2,576]{2,1,0:T(2,128)(2,1)S(1)} copy-done((bf16[8,2,576]{2,1,0:T(2,128)(2,1)S(1)}, bf16[8,2,576]{2,1,0:T(2,128)(2,1)}, u32[]{:S(2)}) %copy-start.3) | copy-done | bytes 18456
  7.9 0.7 %copy-done.4 = s32[8]{0:T(128)S(1)} copy-done((s32[8]{0:T(128)S(1)}, s32[8]{0:T(128)}, u32[]{:S(2)}) %copy-start.4) | copy-done | bytes 56
  8.6 5.9 %near_attention.1 = (bf16[512,7168]{1,0:T(8,128)(2,1)S(1)}, bf16[512,7168]{1,0:T(8,128)(2,1)S(1)}, bf16[4,16,16,576]{3,2,1,0:T(8,128)(2,1)S(1)}, f32[4,16,16,128...) custom-call(s32[8]{0:T(128)S(1)} %copy-done.4, ...), custom_call_target="tpu_custom_call" | custom-call | flops 3460300800 | bytes 18874368 | tf_op jit(solution)/shard_map/near_attention/pallas_call | solution.py:136
  14.7 1.6 %middle_attention.1 = (f32[4,16,16,128]{3,2,1,0:T(8,128)S(1)}, f32[4,16,16,128]{3,2,1,0:T(8,128)S(1)}, f32[4,16,16,512]{3,2,1,0:T(8,128)S(1)}) custom-call(bf16[4,16,16,576]{3,2,1,0:T(8,128)(2,1)S(1)} %get-tuple-element.35.q_ref, f32[4,16,16,128]{3,2,1,0:T(8,128)S(1)} %get-tuple-element.37.m_ref, f32[4,16,16,128]{3,2,1,0:T(8,128)S(1)} %get-tuple-element.38.l_ref, ...), custom_call_target="tpu_custom_call" | custom-call | flops 576716800 | bytes 4194304 | tf_op jit(solution)/shard_map/middle_attention/pallas_call | solution.py:205
  16.3 0.9 %far_attention.5 = (bf16[64,512]{1,0:T(8,128)(2,1)S(1)}, bf16[64,512]{1,0:T(8,128)(2,1)S(1)}, bf16[64,512]{1,0:T(8,128)(2,1)S(1)}, bf16[64,512]{1,0:T(8,128)(2,1)S(1)}) custom-call(bf16[4,16,16,576]{3,2,1,0:T(8,128)(2,1)S(1)} %get-tuple-element.35.q_ref, f32[4,16,16,128]{3,2,1,0:T(8,128)S(1)} %get-tuple-element.41.m_ref, ...), custom_call_target="tpu_custom_call" | custom-call | flops 144179200 | bytes 1048576 | tf_op jit(solution)/shard_map/far_attention/pallas_call | solution.py:247
  17.6 1.5 %collective-permute-start.10 = (bf16[64,512]{1,0:T(8,128)(2,1)S(1)}, bf16[64,512]{1,0:T(8,128)(2,1)S(1)}, u32[]{:S(2)}, u32[]{:S(2)}) collective-permute-start(bf16[64,512]{1,0:T(8,128)(2,1)S(1)} %get-tuple-element.54), channel_id=1, source_target_pairs={{0,2},{1,3},{2,0},{3,1},{4,6},{5,7},{6,4},{7,5},{8,10},{9,11},{10,... | collective-permute-start | bytes 196616 | tf_op jit(solution)/shard_map/ppermute | solution.py:379
  19.1 0.9 %far_attention.3 = (bf16[64,512]{1,0:T(8,128)(2,1)S(1)}, bf16[64,512]{1,0:T(8,128)(2,1)S(1)}, bf16[64,512]{1,0:T(8,128)(2,1)S(1)}, bf16[64,512]{1,0:T(8,128)(2,1)S(1)}) custom-call(bf16[4,16,16,576]{3,2,1,0:T(8,128)(2,1)S(1)} %get-tuple-element.35.q_ref, f32[4,16,16,128]{3,2,1,0:T(8,128)S(1)} %get-tuple-element.41.m_ref, ...), custom_call_target="tpu_custom_call" | custom-call | flops 144179200 | bytes 1048576 | tf_op jit(solution)/shard_map/far_attention/pallas_call | solution.py:247
  20.0 0.7 %collective-permute-start.3 = (bf16[64,512]{1,0:T(8,128)(2,1)S(1)}, bf16[64,512]{1,0:T(8,128)(2,1)S(1)}, u32[]{:S(2)}, u32[]{:S(2)}) collective-permute-start(bf16[64,512]{1,0:T(8,128)(2,1)S(1)} %get-tuple-element.45), channel_id=1, source_target_pairs={{0,1},{1,0},{2,3},{3,2},{4,5},{5,4},{6,7},{7,6},{8,9},{9,8},{10,11... | collective-permute-start | bytes 196616 | tf_op jit(solution)/shard_map/ppermute | solution.py:379
  20.7 1.5 %collective-permute-start.4 = (bf16[64,512]{1,0:T(8,128)(2,1)S(1)}, bf16[64,512]{1,0:T(8,128)(2,1)S(1)}, u32[]{:S(2)}, u32[]{:S(2)}) collective-permute-start(bf16[64,512]{1,0:T(8,128)(2,1)S(1)} %get-tuple-element.46), channel_id=1, source_target_pairs={{0,2},{1,3},{2,0},{3,1},{4,6},{5,7},{6,4},{7,5},{8,10},{9,11},{10,... | collective-permute-start | bytes 196616 | tf_op jit(solution)/shard_map/ppermute | solution.py:379
  22.2 1.2 %far_attention.4 = (bf16[128,512]{1,0:T(8,128)(2,1)S(1)}, bf16[128,512]{1,0:T(8,128)(2,1)S(1)}, bf16[128,512]{1,0:T(8,128)(2,1)S(1)}, bf16[128,512]{1,0:T(8,128)(2,1)S(1)}) custom-call(bf16[4,16,16,576]{3,2,1,0:T(8,128)(2,1)S(1)} %get-tuple-element.35.q_ref, f32[4,16,16,128]{3,2,1,0:T(8,128)S(1)} %get-tuple-element.41.m_ref, ...), custom_call_target="tpu_custom_call" | custom-call | flops 288358400 | bytes 1048576 | tf_op jit(solution)/shard_map/far_attention/pallas_call | solution.py:247
  24.1 1.3 %collective-permute-start.8 = (bf16[128,512]{1,0:T(8,128)(2,1)S(1)}, bf16[128,512]{1,0:T(8,128)(2,1)S(1)}, u32[]{:S(2)}, u32[]{:S(2)}) collective-permute-start(bf16[128,512]{1,0:T(8,128)(2,1)S(1)} %get-tuple-element.51), channel_id=1, source_target_pairs={{0,3},{1,2},{2,1},{3,0},{4,7},{5,6},{6,5},{7,4},{8,11},{9,10},{10,... | collective-permute-start | bytes 393224 | tf_op jit(solution)/shard_map/ppermute | solution.py:379
  25.4 5.3 %project.4 = (f32[64,7168]{1,0:T(8,128)S(1)}, bf16[512,7168]{1,0:T(8,128)(2,1)S(1)}, bf16[512,7168]{1,0:T(8,128)(2,1)S(1)}) custom-call(bf16[64,512]{1,0:T(8,128)(2,1)S(1)} %get-tuple-element.52.refs_0_, bf16[64,512]{1,0:T(8,128)(2,1)S(1)} %collective-permute-done.9.refs_1_, bf16[64,512]{1,0:T(8,128)(2,1)S(1)} %collective-permute-done.10.refs_2_, ...), custom_call_target="tpu_custom_call" | custom-call | flops 1879048192 | bytes 7340032 | tf_op jit(solution)/shard_map/project/pallas_call | solution.py:325
  31.8 3.0 %project.5.refs_4_ = f32[64,7168]{1,0:T(8,128)S(1)} custom-call(bf16[128,512]{1,0:T(8,128)(2,1)S(1)} %get-tuple-element.48.refs_0_, bf16[128,512]{1,0:T(8,128)(2,1)S(1)} %collective-permute-done.6.refs_1_, bf16[128,512]{1,0:T(8,128)(2,1)S(1)} %collective-permute-done.7.refs_2_, ...), custom_call_target="tpu_custom_call", output_to_operand_aliasing={{}: (4, {})} | custom-call | flops 3758096384 | bytes 14680064 | tf_op jit(solution)/shard_map/project/pallas_call | solution.py:325
  34.8 0.9 %project.7 = (bf16[32,3584]{1,0:T(8,128)(2,1)S(1)}, bf16[32,3584]{1,0:T(8,128)(2,1)S(1)}) custom-call(bf16[64,512]{1,0:T(8,128)(2,1)S(1)} %get-tuple-element.44.refs_0_, bf16[64,512]{1,0:T(8,128)(2,1)S(1)} %collective-permute-done.3.refs_1_, bf16[64,512]{1,0:T(8,128)(2,1)S(1)} %collective-permute-done.4.refs_2_, ...), custom_call_target="tpu_custom_call" | custom-call | flops 939524096 | bytes 3670016 | tf_op jit(solution)/shard_map/project/pallas_call | solution.py:325
  36.1 0.9 %project.6 = (bf16[32,3584]{1,0:T(8,128)(2,1)S(1)}, bf16[32,3584]{1,0:T(8,128)(2,1)S(1)}) custom-call(bf16[64,512]{1,0:T(8,128)(2,1)S(1)} %get-tuple-element.44.refs_0_, bf16[64,512]{1,0:T(8,128)(2,1)S(1)} %collective-permute-done.3.refs_1_, bf16[64,512]{1,0:T(8,128)(2,1)S(1)} %collective-permute-done.4.refs_2_, ...), custom_call_target="tpu_custom_call" | custom-call | flops 939524096 | bytes 3670016 | tf_op jit(solution)/shard_map/project/pallas_call | solution.py:325
  37.3 0.8 %collective-permute-start.15 = (bf16[16,3584]{1,0:T(8,128)(2,1)S(1)}, bf16[16,3584]{1,0:T(8,128)(2,1)S(1)}, u32[]{:S(2)}, u32[]{:S(2)}) collective-permute-start(bf16[16,3584]{1,0:T(8,128)(2,1)S(1)} %add_convert_fusion), channel_id=1, source_target_pairs={{0,3},{1,2},{2,1},{3,0},{4,7},{5,6},{6,5},{7,4},{8,11},{9,10},{10,... | collective-permute-start | bytes 344072 | tf_op jit(solution)/shard_map/ppermute | solution.py:379
  38.5 0.9 %collective-permute-start.13 = (bf16[16,3584]{1,0:T(8,128)(2,1)S(1)}, bf16[16,3584]{1,0:T(8,128)(2,1)S(1)}, u32[]{:S(2)}, u32[]{:S(2)}) collective-permute-start(bf16[16,3584]{1,0:T(8,128)(2,1)S(1)} %add_convert_fusion.1), channel_id=1, source_target_pairs={{0,2},{1,3},{2,0},{3,1},{4,6},{5,7},{6,4},{7,5},{8,10},{9,11},{10,... | collective-permute-start | bytes 344072 | tf_op jit(solution)/shard_map/ppermute | solution.py:379
  39.4 3.0 %collective-permute-done.15.refs_5_ = bf16[16,3584]{1,0:T(8,128)(2,1)S(1)} collective-permute-done((bf16[16,3584]{1,0:T(8,128)(2,1)S(1)}, bf16[16,3584]{1,0:T(8,128)(2,1)S(1)}, u32[]{:S(2)}, u32[]{:S(2)}) %collective-permute-start.15) | collective-permute-done | bytes 114720 | tf_op jit(solution)/shard_map/ppermute | solution.py:379
  42.4 2.8 %collective-permute-done.13.refs_2_ = bf16[16,3584]{1,0:T(8,128)(2,1)S(1)} collective-permute-done((bf16[16,3584]{1,0:T(8,128)(2,1)S(1)}, bf16[16,3584]{1,0:T(8,128)(2,1)S(1)}, u32[]{:S(2)}, u32[]{:S(2)}) %collective-permute-start.13) | collective-permute-done | bytes 114720 | tf_op jit(solution)/shard_map/ppermute | solution.py:379
  45.3 0.8 %last_sums.1 = bf16[8,2,7168]{2,1,0:T(2,128)(2,1)} custom-call(bf16[32,3584]{1,0:T(8,128)(2,1)S(1)} %get-tuple-element.61.refs_0_, bf16[32,3584]{1,0:T(8,128)(2,1)S(1)} %collective-permute-done.12.refs_1_, bf16[16,3584]{1,0:T(8,128)(2,1)S(1)} %collective-permute-done.13.refs_2_, bf16[32,3584]{1,0:T(8,128)(2,1)S(1)} %get-tuple-element.63.refs_3_, ...), custom_call_target="tpu_custom_call" | custom-call | tf_op jit(solution)/shard_map/last_sums/pallas_call | solution.py:357
  (31 shorter events, 4.1 us)
Async XLA Ops:
  1.1 3.1 %collective-permute-start = (bf16[576,256]{1,0:T(8,128)(2,1)S(1)}, bf16[576,256]{1,0:T(8,128)(2,1)S(1)}, u32[]{:S(2)}, u32[]{:S(2)}) collective-permute-start(bf16[576,256]{1,0:T(8,128)(2,1)S(1)} %convert_bitcast_fusion.own_ref), channel_id=1, source_target_pairs={{0,1},{1,0},{2,3},{3,2},{4,5},{5,4},{6,7},{7,6},{8,9},{9,8},{10,11... | collective-permute-start | bytes 884744 | tf_op jit(solution)/shard_map/ppermute | solution.py:379
  1.6 12.8 %collective-permute-start.1 = (bf16[576,256]{1,0:T(8,128)(2,1)S(1)}, bf16[576,256]{1,0:T(8,128)(2,1)S(1)}, u32[]{:S(2)}, u32[]{:S(2)}) collective-permute-start(bf16[576,256]{1,0:T(8,128)(2,1)S(1)} %convert_bitcast_fusion.own_ref), channel_id=1, source_target_pairs={{0,2},{1,3},{2,0},{3,1},{4,6},{5,7},{6,4},{7,5},{8,10},{9,11},{10,... | collective-permute-start | bytes 884744 | tf_op jit(solution)/shard_map/ppermute | solution.py:379
  4.2 1.7 %copy-start.1 = (bf16[8,256,576]{1,2,0:T(8,128)(2,1)S(1)}, bf16[8,256,576]{1,2,0:T(8,128)(2,1)}, u32[]{:S(2)}) copy-start(bf16[8,256,576]{1,2,0:T(8,128)(2,1)} %param.8) | copy-start | bytes 7077892
  5.9 1.3 %copy-start.2 = (bf16[8,2,64,576]{3,2,1,0:T(8,128)(2,1)S(1)}, bf16[8,2,64,576]{3,2,1,0:T(8,128)(2,1)}, u32[]{:S(2)}) copy-start(bf16[8,2,64,576]{3,2,1,0:T(8,128)(2,1)} %q_ref.1) | copy-start | bytes 3538948
  7.2 0.7 %copy-start.3 = (bf16[8,2,576]{2,1,0:T(2,128)(2,1)S(1)}, bf16[8,2,576]{2,1,0:T(2,128)(2,1)}, u32[]{:S(2)}) copy-start(bf16[8,2,576]{2,1,0:T(2,128)(2,1)} %new_ref.1) | copy-start | bytes 55300
  7.9 0.7 %copy-start.4 = (s32[8]{0:T(128)S(1)}, s32[8]{0:T(128)}, u32[]{:S(2)}) copy-start(s32[8]{0:T(128)} %len_ref.1) | copy-start | bytes 100
  14.4 1.9 %collective-permute-start.2 = (bf16[576,256]{1,0:T(8,128)(2,1)S(1)}, bf16[576,256]{1,0:T(8,128)(2,1)S(1)}, u32[]{:S(2)}, u32[]{:S(2)}) collective-permute-start(bf16[576,256]{1,0:T(8,128)(2,1)S(1)} %collective-permute-done.1.refs_0_), channel_id=1, source_target_pairs={{0,1},{1,0},{2,3},{3,2},{4,5},{5,4},{6,7},{7,6},{8,9},{9,8},{10,11... | collective-permute-start | bytes 884744 | tf_op jit(solution)/shard_map/ppermute | solution.py:379
  17.2 6.2 %collective-permute-start.9 = (bf16[64,512]{1,0:T(8,128)(2,1)S(1)}, bf16[64,512]{1,0:T(8,128)(2,1)S(1)}, u32[]{:S(2)}, u32[]{:S(2)}) collective-permute-start(bf16[64,512]{1,0:T(8,128)(2,1)S(1)} %get-tuple-element.53), channel_id=1, source_target_pairs={{0,1},{1,0},{2,3},{3,2},{4,5},{5,4},{6,7},{7,6},{8,9},{9,8},{10,11... | collective-permute-start | bytes 196616 | tf_op jit(solution)/shard_map/ppermute | solution.py:379
  17.6 5.9 %collective-permute-start.10 = (bf16[64,512]{1,0:T(8,128)(2,1)S(1)}, bf16[64,512]{1,0:T(8,128)(2,1)S(1)}, u32[]{:S(2)}, u32[]{:S(2)}) collective-permute-start(bf16[64,512]{1,0:T(8,128)(2,1)S(1)} %get-tuple-element.54), channel_id=1, source_target_pairs={{0,2},{1,3},{2,0},{3,1},{4,6},{5,7},{6,4},{7,5},{8,10},{9,11},{10,... | collective-permute-start | bytes 196616 | tf_op jit(solution)/shard_map/ppermute | solution.py:379
  19.1 5.0 %collective-permute-start.11 = (bf16[64,512]{1,0:T(8,128)(2,1)S(1)}, bf16[64,512]{1,0:T(8,128)(2,1)S(1)}, u32[]{:S(2)}, u32[]{:S(2)}) collective-permute-start(bf16[64,512]{1,0:T(8,128)(2,1)S(1)} %get-tuple-element.55), channel_id=1, source_target_pairs={{0,3},{1,2},{2,1},{3,0},{4,7},{5,6},{6,5},{7,4},{8,11},{9,10},{10,... | collective-permute-start | bytes 196616 | tf_op jit(solution)/shard_map/ppermute | solution.py:379
  20.0 14.8 %collective-permute-start.3 = (bf16[64,512]{1,0:T(8,128)(2,1)S(1)}, bf16[64,512]{1,0:T(8,128)(2,1)S(1)}, u32[]{:S(2)}, u32[]{:S(2)}) collective-permute-start(bf16[64,512]{1,0:T(8,128)(2,1)S(1)} %get-tuple-element.45), channel_id=1, source_target_pairs={{0,1},{1,0},{2,3},{3,2},{4,5},{5,4},{6,7},{7,6},{8,9},{9,8},{10,11... | collective-permute-start | bytes 196616 | tf_op jit(solution)/shard_map/ppermute | solution.py:379
  20.7 4.7 %copy-start = (bf16[16,512,128]{2,1,0:T(8,128)(2,1)S(1)}, bf16[16,512,128]{2,1,0:T(8,128)(2,1)}, u32[]{:S(2)}) copy-start(bf16[16,512,128]{2,1,0:T(8,128)(2,1)} %refs_5_.5) | copy-start | bytes 6291460
  20.7 14.1 %collective-permute-start.4 = (bf16[64,512]{1,0:T(8,128)(2,1)S(1)}, bf16[64,512]{1,0:T(8,128)(2,1)S(1)}, u32[]{:S(2)}, u32[]{:S(2)}) collective-permute-start(bf16[64,512]{1,0:T(8,128)(2,1)S(1)} %get-tuple-element.46), channel_id=1, source_target_pairs={{0,2},{1,3},{2,0},{3,1},{4,6},{5,7},{6,4},{7,5},{8,10},{9,11},{10,... | collective-permute-start | bytes 196616 | tf_op jit(solution)/shard_map/ppermute | solution.py:379
  23.4 7.2 %collective-permute-start.6 = (bf16[128,512]{1,0:T(8,128)(2,1)S(1)}, bf16[128,512]{1,0:T(8,128)(2,1)S(1)}, u32[]{:S(2)}, u32[]{:S(2)}) collective-permute-start(bf16[128,512]{1,0:T(8,128)(2,1)S(1)} %get-tuple-element.49), channel_id=1, source_target_pairs={{0,1},{1,0},{2,3},{3,2},{4,5},{5,4},{6,7},{7,6},{8,9},{9,8},{10,11... | collective-permute-start | bytes 393224 | tf_op jit(solution)/shard_map/ppermute | solution.py:379
  23.5 7.7 %collective-permute-start.7 = (bf16[128,512]{1,0:T(8,128)(2,1)S(1)}, bf16[128,512]{1,0:T(8,128)(2,1)S(1)}, u32[]{:S(2)}, u32[]{:S(2)}) collective-permute-start(bf16[128,512]{1,0:T(8,128)(2,1)S(1)} %get-tuple-element.50), channel_id=1, source_target_pairs={{0,2},{1,3},{2,0},{3,1},{4,6},{5,7},{6,4},{7,5},{8,10},{9,11},{10,... | collective-permute-start | bytes 393224 | tf_op jit(solution)/shard_map/ppermute | solution.py:379
  24.1 7.7 %collective-permute-start.8 = (bf16[128,512]{1,0:T(8,128)(2,1)S(1)}, bf16[128,512]{1,0:T(8,128)(2,1)S(1)}, u32[]{:S(2)}, u32[]{:S(2)}) collective-permute-start(bf16[128,512]{1,0:T(8,128)(2,1)S(1)} %get-tuple-element.51), channel_id=1, source_target_pairs={{0,3},{1,2},{2,1},{3,0},{4,7},{5,6},{6,5},{7,4},{8,11},{9,10},{10,... | collective-permute-start | bytes 393224 | tf_op jit(solution)/shard_map/ppermute | solution.py:379
  30.7 4.1 %collective-permute-start.5 = (bf16[64,512]{1,0:T(8,128)(2,1)S(1)}, bf16[64,512]{1,0:T(8,128)(2,1)S(1)}, u32[]{:S(2)}, u32[]{:S(2)}) collective-permute-start(bf16[64,512]{1,0:T(8,128)(2,1)S(1)} %get-tuple-element.47), channel_id=1, source_target_pairs={{0,3},{1,2},{2,1},{3,0},{4,7},{5,6},{6,5},{7,4},{8,11},{9,10},{10,... | collective-permute-start | bytes 196616 | tf_op jit(solution)/shard_map/ppermute | solution.py:379
  35.7 1.6 %collective-permute-start.14 = (bf16[32,3584]{1,0:T(8,128)(2,1)S(1)}, bf16[32,3584]{1,0:T(8,128)(2,1)S(1)}, u32[]{:S(2)}, u32[]{:S(2)}) collective-permute-start(bf16[32,3584]{1,0:T(8,128)(2,1)S(1)} %get-tuple-element.64), channel_id=1, source_target_pairs={{0,1},{1,0},{2,3},{3,2},{4,5},{5,4},{6,7},{7,6},{8,9},{9,8},{10,11... | collective-permute-start | bytes 688136 | tf_op jit(solution)/shard_map/ppermute | solution.py:379
  37.0 1.6 %collective-permute-start.12 = (bf16[32,3584]{1,0:T(8,128)(2,1)S(1)}, bf16[32,3584]{1,0:T(8,128)(2,1)S(1)}, u32[]{:S(2)}, u32[]{:S(2)}) collective-permute-start(bf16[32,3584]{1,0:T(8,128)(2,1)S(1)} %get-tuple-element.62), channel_id=1, source_target_pairs={{0,1},{1,0},{2,3},{3,2},{4,5},{5,4},{6,7},{7,6},{8,9},{9,8},{10,11... | collective-permute-start | bytes 688136 | tf_op jit(solution)/shard_map/ppermute | solution.py:379
  37.3 5.1 %collective-permute-start.15 = (bf16[16,3584]{1,0:T(8,128)(2,1)S(1)}, bf16[16,3584]{1,0:T(8,128)(2,1)S(1)}, u32[]{:S(2)}, u32[]{:S(2)}) collective-permute-start(bf16[16,3584]{1,0:T(8,128)(2,1)S(1)} %add_convert_fusion), channel_id=1, source_target_pairs={{0,3},{1,2},{2,1},{3,0},{4,7},{5,6},{6,5},{7,4},{8,11},{9,10},{10,... | collective-permute-start | bytes 344072 | tf_op jit(solution)/shard_map/ppermute | solution.py:379
  38.5 6.7 %collective-permute-start.13 = (bf16[16,3584]{1,0:T(8,128)(2,1)S(1)}, bf16[16,3584]{1,0:T(8,128)(2,1)S(1)}, u32[]{:S(2)}, u32[]{:S(2)}) collective-permute-start(bf16[16,3584]{1,0:T(8,128)(2,1)S(1)} %add_convert_fusion.1), channel_id=1, source_target_pairs={{0,2},{1,3},{2,0},{3,1},{4,6},{5,7},{6,4},{7,5},{8,10},{9,11},{10,... | collective-permute-start | bytes 344072 | tf_op jit(solution)/shard_map/ppermute | solution.py:379

commit v3 on v2

v3 whole, which is shorter than its diff:
```python
import functools
import math

import jax
import jax.numpy as jnp
from jax import lax
from jax.experimental import pallas as pl
from jax.experimental.pallas import tpu as pltpu
from jax.sharding import PartitionSpec as P

LATENT = 512
QK_HEAD = 192
SCALE2 = QK_HEAD**-0.5 * math.log2(math.e)
NEG = -1e30
CHUNK_HEADS = 4
OUT_PARTS = 2
BLOCK = 256
MIB = 2**20
W_PIECES = 2
PAUSE_FLOPS = 10**10
PAUSE_BYTES = 30 * MIB


def dot_nt(a, b):
    return lax.dot_general(a, b, (((1,), (1,)), ((), ())), preferred_element_type=jnp.float32)


def dot_nn(a, b):
    return jnp.dot(a, b, preferred_element_type=jnp.float32)


def pause():
    def kernel(out_ref):
        out_ref[...] = jnp.zeros_like(out_ref)

    return pl.pallas_call(
        kernel,
        out_specs=pl.BlockSpec(memory_space=pltpu.VMEM),
        out_shape=pltpu.VMEM((8, 128), jnp.float32),
        cost_estimate=pl.CostEstimate(
            flops=PAUSE_FLOPS, bytes_accessed=PAUSE_BYTES, transcendentals=0
        ),
        name="pause",
    )()


def call(body, operands, in_specs, out_shape, scratch, bring, limit, flops, name, aliases=None):
    w_out, piece_rows, pieces = bring
    vmem, hbm = pl.BlockSpec(memory_space=pltpu.VMEM), pl.BlockSpec(memory_space=pltpu.HBM)
    n_in, n_out = len(operands), len(out_shape)
    copied = 0
    if pieces:
        operands, in_specs = [*operands, w_out], [*in_specs, hbm]
        out_shape = [*out_shape] + [pltpu.VMEM((piece_rows, w_out.shape[1]), w_out.dtype)] * len(pieces)
        scratch = [*scratch, pltpu.SemaphoreType.DMA((len(pieces),))]
        copied = 2 * len(pieces) * piece_rows * w_out.shape[1]

    def kernel(*refs):
        ins, rest = refs[: len(operands)], refs[len(operands) :]
        outs, rest = rest[: len(out_shape)], rest[len(out_shape) :]
        copies = []
        for i, piece in enumerate(pieces):
            rows = pl.ds(piece * piece_rows, piece_rows)
            copies.append(pltpu.make_async_copy(ins[-1].at[rows], outs[n_out + i], rest[-1].at[i]))
        for copy in copies:
            copy.start()
        body(ins[:n_in], outs[:n_out], rest[: len(scratch) - bool(pieces)])
        for copy in copies:
            copy.wait()

    out = pl.pallas_call(
        kernel,
        in_specs=in_specs,
        out_specs=[vmem] * len(out_shape),
        out_shape=out_shape,
        scratch_shapes=scratch,
        compiler_params=pltpu.CompilerParams(vmem_limit_bytes=limit * MIB),
        cost_estimate=pl.CostEstimate(
            flops=flops, bytes_accessed=4 * MIB + copied, transcendentals=0
        ),
        input_output_aliases=aliases or {},
        name=name,
    )(*operands)
    return out[:n_out], list(out[n_out:])


def update(scores, m, l, acc, probs_into):
    new_m = m
    for s in scores:
        new_m = jnp.maximum(new_m, jnp.max(s, axis=1, keepdims=True))
    shrink = jnp.exp2((m - new_m) * SCALE2)
    weights = [jnp.exp2((s - new_m) * SCALE2) for s in scores]
    l = l * shrink
    for p in weights:
        l += jnp.sum(p, axis=1, keepdims=True)
    return new_m, l, probs_into(acc * shrink, [p.astype(jnp.bfloat16) for p in weights])


def in_turn(tasks, score, finish):
    def some(first, count):
        before = None
        for i in range(count):
            task = first + i
            now = score(task)
            if before is not None:
                finish(*before)
            before = (task, now)
        finish(*before)

    if tasks % 2 or tasks < 4:
        some(0, tasks)
    else:

        @pl.loop(0, 2)
        def _(i):
            some(i * (tasks // 2), tasks // 2)


def near_call(paused, suffix_len, queries, suffix_t, new_latent, own, beside, units, axis_size, bring):
    rows, steps, heads, width = queries.shape
    tile = heads // units
    share = heads // axis_size
    per = steps * heads

    def body(ins, outs, _):
        _, len_buf, q_buf, suf_buf, new_buf, own_ref, beside_ref = ins
        qs_ref, m_ref, l_ref, acc_ref = outs
        keys = [own_ref[...], beside_ref[...]]

        def sort(r):
            by_unit = [[] for _ in range(units)]
            for s in range(steps):
                q = q_buf[r, s].astype(jnp.float32)
                for u in range(units):
                    picked = [
                        q[j * share + u * CHUNK_HEADS : j * share + (u + 1) * CHUNK_HEADS]
                        for j in range(axis_size)
                    ]
                    by_unit[u].append(jnp.concatenate(picked, axis=0).astype(jnp.bfloat16))
            for u in range(units):
                for s in range(steps):
                    qs_ref[u, r * steps + s] = by_unit[u][s]
            return jnp.concatenate([x for unit in by_unit for x in unit], axis=0)

        def score(task):
            first = task * (BLOCK // per)
            q = [sort(first + i) for i in range(BLOCK // per)]
            both = jnp.concatenate(q, axis=0)
            scores = [dot_nn(both, k) for k in keys]
            old, new = [], []
            for i, x in enumerate(q):
                s = dot_nn(x, suf_buf[first + i])
                at = lax.broadcasted_iota(jnp.int32, s.shape, 1)
                old.append(jnp.where(at < len_buf[first + i], s, NEG))
                s = dot_nt(x, new_buf[first + i])
                step = lax.broadcasted_iota(jnp.int32, s.shape, 0) // tile % steps
                token = lax.broadcasted_iota(jnp.int32, s.shape, 1)
                new.append(jnp.where(token <= step, s, NEG))
            return scores + [jnp.concatenate(x, axis=0) for x in (old, new)]

        def finish(task, scores):
            first = task * (BLOCK // per)
            m = functools.reduce(
                jnp.maximum, [jnp.max(s, axis=1, keepdims=True) for s in scores]
            )
            weights = [jnp.exp2((s - m) * SCALE2) for s in scores]
            l = sum(jnp.sum(p, axis=1, keepdims=True) for p in weights)
            probs = [p.astype(jnp.bfloat16) for p in weights]
            acc = dot_nt(probs[0], keys[0][:LATENT]) + dot_nt(probs[1], keys[1][:LATENT])
            new_probs = probs[3].astype(jnp.float32)
            for i in range(BLOCK // per):
                here = slice(i * per, (i + 1) * per)
                part = acc[here] + dot_nt(probs[2][here], suf_buf[first + i, :LATENT])
                values = new_buf[first + i][:, :LATENT].astype(jnp.float32)
                for t in range(steps):
                    part += new_probs[here, t : t + 1] * values[t : t + 1]
                there = pl.ds((first + i) * steps, steps)
                lead = (units, steps, tile)
                m_ref[:, there] = jnp.broadcast_to(m[here], (per, 128)).reshape(lead + (128,))
                l_ref[:, there] = jnp.broadcast_to(l[here], (per, 128)).reshape(lead + (128,))
                acc_ref[:, there] = part.reshape(lead + (LATENT,))

        in_turn(rows * per // BLOCK, score, finish)

    vmem, smem = pl.BlockSpec(memory_space=pltpu.VMEM), pl.BlockSpec(memory_space=pltpu.SMEM)
    lead = (units, rows * steps, tile)
    f32 = jnp.float32
    return call(
        body,
        [paused, suffix_len, queries, suffix_t, new_latent, own, beside],
        [vmem, smem] + [vmem] * 5,
        [
            jax.ShapeDtypeStruct(lead + (width,), queries.dtype),
            jax.ShapeDtypeStruct(lead + (128,), f32),
            jax.ShapeDtypeStruct(lead + (128,), f32),
            jax.ShapeDtypeStruct(lead + (LATENT,), f32),
        ],
        [],
        bring,
        24,
        4 * rows * per * 1100 * 768,
        "near_attention",
    )


def merge(first, size, keys, q_ref, m_ref, l_ref, acc_ref, store):
    _, pairs, tile, width = q_ref.shape
    step = BLOCK // tile
    blocks = pairs // step

    def at(task):
        return first + task // blocks, pl.ds(task % blocks * step, step)

    def score(task):
        here = at(task)
        q = q_ref[here].reshape(BLOCK, width)
        return [dot_nn(q, k) for k in keys]

    def finish(task, scores):
        here = at(task)
        store(
            task,
            here,
            *update(
                scores,
                m_ref[here].reshape(BLOCK, 128)[:, 0:1],
                l_ref[here].reshape(BLOCK, 128)[:, 0:1],
                acc_ref[here].reshape(BLOCK, LATENT),
                lambda acc, ps: acc + sum(dot_nt(p, k[:LATENT]) for p, k in zip(ps, keys)),
            ),
        )

    in_turn(size * blocks, score, finish)


def middle_call(queries, state, keys, bring):
    units, pairs, tile, _ = queries.shape

    def body(ins, outs, _):
        q_ref, m_ref, l_ref, acc_ref, *key_refs = ins
        m_out, l_out, acc_out = outs

        def store(task, here, m, l, acc):
            lead = (BLOCK // tile, tile)
            m_out[here] = jnp.broadcast_to(m, (BLOCK, 128)).reshape(lead + (128,))
            l_out[here] = jnp.broadcast_to(l, (BLOCK, 128)).reshape(lead + (128,))
            acc_out[here] = acc.reshape(lead + (LATENT,))

        merge(0, units, [k[...] for k in key_refs], q_ref, m_ref, l_ref, acc_ref, store)

    operands = [queries, *state, *keys]
    return call(
        body,
        operands,
        [pl.BlockSpec(memory_space=pltpu.VMEM)] * len(operands),
        [jax.ShapeDtypeStruct(x.shape, x.dtype) for x in state],
        [],
        bring,
        28 if bring[2] else 10,
        2 * units * pairs * tile * 1100 * 256 * len(keys),
        "middle_attention",
    )


def far_call(first, size, queries, state, keys, axis_size, bring):
    _, pairs, tile, _ = queries.shape
    per_unit = pairs * tile

    def body(ins, out_refs, scratch):
        q_ref, m_ref, l_ref, acc_ref, *key_refs = ins
        (done,) = scratch

        def store(task, here, m, l, acc):
            attended = acc / l
            rows = pl.ds(task * BLOCK, BLOCK)
            for g in range(LATENT // 128):
                done[g, rows, :] = attended[:, g * 128 : (g + 1) * 128]

        keys_now = [k[...] for k in key_refs]
        merge(first, size, keys_now, q_ref, m_ref, l_ref, acc_ref, store)
        me = lax.axis_index("roll")
        for k in range(axis_size):
            there = jnp.bitwise_xor(me, k) * CHUNK_HEADS
            for u in range(size):
                for i in range(CHUNK_HEADS):
                    at = (u * CHUNK_HEADS + i) * pairs
                    for g in range(LATENT // 128):
                        out_refs[k][at : at + pairs, g * 128 : (g + 1) * 128] = done[
                            g, pl.ds(u * per_unit + there + i, pairs, stride=tile), :
                        ].astype(jnp.bfloat16)

    operands = [queries, *state, *keys]
    return call(
        body,
        operands,
        [pl.BlockSpec(memory_space=pltpu.VMEM)] * len(operands),
        [jax.ShapeDtypeStruct((size * CHUNK_HEADS * pairs, LATENT), jnp.bfloat16)] * axis_size,
        [pltpu.VMEM((LATENT // 128, size * per_unit + tile, 128), jnp.float32)],
        bring,
        24 if bring[2] else 10,
        2 * size * per_unit * 1100 * 256 * len(keys),
        "far_attention",
    )


def project(first_head, heads, pieces, acc, w_uv, w_pieces, bring, kept=None, first_col=0, cols=None):
    pairs = pieces[0].shape[0] // heads
    total_rows = len(pieces) * pairs
    piece_rows, width = w_pieces[0].shape
    cols = width if cols is None else cols
    block = next(b for b in (1792, 1024, 896, 512, 128) if cols % b == 0)

    def body(ins, outs, _):
        ins = list(ins)
        piece_refs = [ins.pop(0) for _ in pieces]
        acc_ref = ins.pop(0) if acc is not None else None
        uv_ref, *w_refs = ins
        head_out = []
        for i in range(heads):
            rows = jnp.concatenate([p[i * pairs : (i + 1) * pairs, :] for p in piece_refs], axis=0)
            head_out.append(dot_nn(rows, uv_ref[first_head + i]).astype(jnp.bfloat16))
        head_out = jnp.concatenate(head_out, axis=1)

        def block_of(b):
            here = pl.ds(b * block, block)
            there = pl.ds(first_col + b * block, block)
            total = sum(
                dot_nn(head_out[:, i * piece_rows : (i + 1) * piece_rows], w_ref[:, there])
                for i, w_ref in enumerate(w_refs)
            )
            if acc_ref is not None:
                total += acc_ref[:, there]
            if kept is None:
                outs[0][:, here] = total
                return
            at = [0, 0]
            for k in range(len(pieces)):
                side = 0 if k in kept else 1
                outs[side][at[side] * pairs : (at[side] + 1) * pairs, here] = total[
                    k * pairs : (k + 1) * pairs
                ].astype(jnp.bfloat16)
                at[side] += 1

        if bring[2]:
            pl.loop(0, cols // block)(block_of)
        else:
            for b in range(cols // block):
                block_of(b)

    operands = [*pieces] + ([acc] if acc is not None else []) + [w_uv, *w_pieces]
    if kept is not None:
        out_shape = [jax.ShapeDtypeStruct((total_rows // 2, cols), jnp.bfloat16)] * 2
    else:
        out_shape = [jax.ShapeDtypeStruct((total_rows, cols), jnp.float32)]
    return call(
        body,
        operands,
        [pl.BlockSpec(memory_space=pltpu.VMEM)] * len(operands),
        out_shape,
        [],
        bring,
        14 if bring[2] else 8,
        8 * total_rows * heads * w_uv.shape[2] * cols,
        "project",
        {len(pieces): 0} if acc is not None and kept is None else {},
    )


def last_sums(rows, steps, width, parts):
    pairs = rows * steps
    flat = [x for part in parts for x in part]
    cols = width // len(parts)

    def kernel(*refs):
        refs, out_ref = list(refs[:-1]), refs[-1]
        for i, part in enumerate(parts):
            total = None
            for _, first in part:
                x = refs.pop(0)[first : first + pairs, :].astype(jnp.float32)
                total = x if total is None else total + x
            out_ref[:, :, i * cols : (i + 1) * cols] = total.astype(jnp.bfloat16).reshape(
                rows, steps, cols
            )

    vmem = pl.BlockSpec(memory_space=pltpu.VMEM)
    return pl.pallas_call(
        kernel,
        in_specs=[vmem] * len(flat),
        out_specs=vmem,
        out_shape=jax.ShapeDtypeStruct((rows, steps, width), jnp.bfloat16),
        compiler_params=pltpu.CompilerParams(vmem_limit_bytes=8 * MIB),
        name="last_sums",
    )(*[x for x, _ in flat])


def on_device(prefix_latent, suffix_latent, suffix_len, new_latent, queries, w_uv, w_out):
    n = lax.axis_size("roll")
    rows, steps, heads, _ = queries.shape
    pairs = rows * steps
    width = w_out.shape[1]
    share = heads // n
    units = share // CHUNK_HEADS
    chunks = [(0, 1), (1, units - 2), (units - 1, 1)] if units > 2 else [(u, 1) for u in range(units)]
    piece_rows = CHUNK_HEADS * w_uv.shape[2] // W_PIECES
    n_pieces = units * W_PIECES
    if len(chunks) == 3 and n_pieces == 8:
        brings = {
            "near": [0, 1, 2, 3],
            "middle": [4],
            ("project", 0): [5],
            ("project", 1): [6, 7],
        }
    else:
        half = n_pieces // 2
        brings = {"near": list(range(half)), "middle": list(range(half, n_pieces))}
    held = {}

    def bring(who):
        return (w_out, piece_rows, brings.get(who, []))

    def keep(who, result):
        out, brought = result
        held.update(zip(brings.get(who, []), brought))
        return out

    def swap(x, k):
        return lax.ppermute(x, "roll", [(i, i ^ k) for i in range(n)])

    own = prefix_latent.T.astype(jnp.bfloat16)
    own, paused = lax.optimization_barrier((own, pause()))
    across = [swap(own, k) for k in range(2, n, 2)]
    beside = swap(own, 1)
    queries, m, l, acc = keep(
        "near",
        near_call(
            paused,
            suffix_len,
            queries,
            jnp.swapaxes(suffix_latent, 1, 2),
            new_latent,
            own,
            beside,
            units,
            n,
            bring("near"),
        ),
    )
    *across, m = lax.optimization_barrier((*across, m))
    forwarded = [swap(x, 1) for x in across]
    state = keep("middle", middle_call(queries, (m, l, acc), across, bring("middle")))
    got = []
    for c, (first, size) in enumerate(chunks):
        if c >= 2:
            queries, *got[c - 2] = lax.optimization_barrier((queries, *got[c - 2]))
        who = ("far", c)
        mine = keep(who, far_call(first, size, queries, state, forwarded, n, bring(who)))
        if c >= 2:
            *mine, got[c - 2] = lax.optimization_barrier((*mine, got[c - 2]))
        *mine, queries = lax.optimization_barrier((*mine, queries))
        there = [mine[0]] + [None] * (n - 1)
        for k in range(1, n):
            there[k] = swap(mine[k], k)
        got.append(there)
    acc = None

    def pieces_of(first, size):
        return [held[i] for i in range(first * W_PIECES, (first + size) * W_PIECES)]

    for c, (first, size) in enumerate(chunks[:-1]):
        who = ("project", c)
        (acc,) = keep(
            who,
            project(
                first * CHUNK_HEADS,
                size * CHUNK_HEADS,
                got[c],
                acc,
                w_uv,
                pieces_of(first, size),
                bring(who),
            ),
        )
    first, size = chunks[-1]
    cols = width // OUT_PARTS
    parts = []
    for part in range(OUT_PARTS):
        odd = part % 2
        kept = tuple(k for k in range(n) if k == 0 or (k != 1 and k % 2 == odd))
        (stay, send), _ = project(
            first * CHUNK_HEADS,
            size * CHUNK_HEADS,
            got[-1],
            acc,
            w_uv,
            pieces_of(first, size),
            bring(None),
            kept,
            part * cols,
            cols,
        )
        left = [k for k in range(n) if k not in kept]
        recv = swap(send, 1)

        def piece(x, i):
            return x[i * pairs : (i + 1) * pairs].astype(jnp.float32)

        terms = [(stay, 0), (recv, left.index(1) * pairs)]
        for i, k in enumerate(kept[1:]):
            both = piece(stay, i + 1) + piece(recv, left.index(k ^ 1))
            terms.append((swap(both.astype(jnp.bfloat16), k), 0))
        parts.append(terms)
    return last_sums(rows, steps, width, parts)


def solution(mesh):
    in_specs = (
        P(("group", "roll"), None),
        P(("group", "roll"), None, None),
        P(("group", "roll")),
        P(("group", "roll"), None, None),
        P(("group", "roll"), None, None, None),
        P("roll", None, None),
        P("roll", None),
    )
    out_specs = P(("group", "roll"), None, None)
    return jax.shard_map(
        on_device, mesh=mesh, in_specs=in_specs, out_specs=out_specs, check_vma=False
    )
```

time: 46.4 us -> 41.8 us (0.901)
  Pallas kernels: 21.3 us -> 19 us
  local copies, waits for them, and re-layouts: 4.37 us -> 2.38 us
  other arithmetic: 1.15 us -> 0.09 us
  starting transfers between devices: 12.2 us -> 13.2 us
    pallas_call x9 -> x10, Pallas kernels: 20.5 us -> 18.2 us  [the longest x9 18.2 us: call(): pl.pallas_call(kernel, in_specs=in_specs, out_specs=[vmem] * len(out_shap...]
    unnamed x10 -> x12, local copies, waits for them, and re-layouts: 4.37 us -> 2.38 us
    convert_element_type x1, other arithmetic: 1.09 us -> 0.03 us  [on_device(): own = prefix_latent.T.astype(jnp.bfloat16)]
    ppermute x16, starting transfers between devices: 12.2 us -> 13.2 us  [swap(): return lax.ppermute(x, 'roll', [(i, i ^ k) for i in range(n)])]
  transfers between devices with their start and end apart: 16 -> 16, of which waited for: 4 -> 6; matrix products, arithmetic and copies ran while one was open for 0% -> 0% of each run, Pallas kernels for 41% -> 39%
where the time goes in v3:
time: 41.8 us; the launch traced here: 41.5 us
  Pallas kernels  19 us (45%)
  starting transfers between devices  13.2 us (32%)
  waiting for transfers between devices  6.67 us (16%)
  local copies, waits for them, and re-layouts  2.38 us (6%)
    pallas_call x9, Pallas kernels, call(): pl.pallas_call(kernel, in_specs=in_specs, out_specs=[vmem] * len(out_shap...  18.2 us
    ppermute x16, starting transfers between devices, swap(): return lax.ppermute(x, 'roll', [(i, i ^ k) for i in range(n)])  13.2 us
    ppermute x16, waiting for transfers between devices, swap(): return lax.ppermute(x, 'roll', [(i, i ^ k) for i in range(n)])  6.67 us
    unnamed x12, local copies, waits for them, and re-layouts  2.38 us
  transfers between devices with their start and end apart: 16, of which 6 were waited for; matrix products, arithmetic and copies ran while one was open for 0% of the time, Pallas kernels for 39%

profile of v3, /device:TPU:0, one launch (start us, length us, event | category | flops | bytes accessed | tf_op | source)
XLA Modules:
  0.0 41.5 jit_solution(7353604594435462996)
XLA Ops:
  0.0 1.1 %copy-done.5 = f32[256,576]{0,1:T(8,128)S(1)} copy-done((f32[256,576]{0,1:T(8,128)S(1)}, f32[256,576]{0,1:T(8,128)}, u32[]{:S(2)}) %copy-start.5) | copy-done | bytes 589848
  1.6 2.6 %collective-permute-start.1 = (bf16[576,256]{1,0:T(8,128)(2,1)S(1)}, bf16[576,256]{1,0:T(8,128)(2,1)S(1)}, u32[]{:S(2)}, u32[]{:S(2)}) collective-permute-start(bf16[576,256]{1,0:T(8,128)(2,1)S(1)} %convert_bitcast_fusion.refs_5_), channel_id=1, source_target_pairs={{0,2},{1,3},{2,0},{3,1},{4,6},{5,7},{6,4},{7,5},{8,10},{9,11},{10,... | collective-permute-start | bytes 884744 | tf_op jit(solution)/shard_map/ppermute | solution.py:427
  4.2 1.3 %copy-done.2 = bf16[8,2,64,576]{3,2,1,0:T(8,128)(2,1)S(1)} copy-done((bf16[8,2,64,576]{3,2,1,0:T(8,128)(2,1)S(1)}, bf16[8,2,64,576]{3,2,1,0:T(8,128)(2,1)}, u32[]{:S(2)}) %copy-start.2) | copy-done | bytes 1179672
  5.5 5.8 %near_attention.1 = (bf16[4,16,16,576]{3,2,1,0:T(8,128)(2,1)S(1)}, f32[4,16,16,128]{3,2,1,0:T(8,128)S(1)}, f32[4,16,16,128]{3,2,1,0:T(8,128)S(1)}, f32[4,16,16,5...) custom-call(f32[8,128]{1,0:T(8,128)S(1)} %pause.1.refs_0_, ...), custom_call_target="tpu_custom_call" | custom-call | flops 3460300800 | bytes 18874368 | tf_op jit(solution)/shard_map/near_attention/pallas_call | solution.py:71
  11.8 2.0 %middle_attention.1 = (f32[4,16,16,128]{3,2,1,0:T(8,128)S(1)}, f32[4,16,16,128]{3,2,1,0:T(8,128)S(1)}, f32[4,16,16,512]{3,2,1,0:T(8,128)S(1)}, bf16[256,7168]{1,0:T(8,128)(2,1)S(1)}) custom-call(bf16[4,16,16,576]{3,2,1,0:T(8,128)(2,1)S(1)} %get-tuple-element.94.refs_0_, f32[4,16,16,128]{3,2,1,0:T(8,128)S(1)} %get-tuple-element.73.refs_1_, ...), custom_call_target="tpu_custom_call" | custom-call | flops 576716800 | bytes 7864320 | tf_op jit(solution)/shard_map/middle_attention/pallas_call | solution.py:71
  13.9 0.9 %far_attention.3 = (bf16[64,512]{1,0:T(8,128)(2,1)S(1)}, bf16[64,512]{1,0:T(8,128)(2,1)S(1)}, bf16[64,512]{1,0:T(8,128)(2,1)S(1)}, bf16[64,512]{1,0:T(8,128)(2,1)S(1)}) custom-call(bf16[4,16,16,576]{3,2,1,0:T(8,128)(2,1)S(1)} %get-tuple-element.94.refs_0_, f32[4,16,16,128]{3,2,1,0:T(8,128)S(1)} %get-tuple-element.77.refs_1_, ...), custom_call_target="tpu_custom_call" | custom-call | flops 144179200 | bytes 4194304 | tf_op jit(solution)/shard_map/far_attention/pallas_call | solution.py:71
  14.7 0.6 %collective-permute-start.3 = (bf16[64,512]{1,0:T(8,128)(2,1)S(1)}, bf16[64,512]{1,0:T(8,128)(2,1)S(1)}, u32[]{:S(2)}, u32[]{:S(2)}) collective-permute-start(bf16[64,512]{1,0:T(8,128)(2,1)S(1)} %get-tuple-element.91), channel_id=1, source_target_pairs={{0,1},{1,0},{2,3},{3,2},{4,5},{5,4},{6,7},{7,6},{8,9},{9,8},{10,11... | collective-permute-start | bytes 196616 | tf_op jit(solution)/shard_map/ppermute | solution.py:427
  15.3 1.8 %collective-permute-start.4 = (bf16[64,512]{1,0:T(8,128)(2,1)S(1)}, bf16[64,512]{1,0:T(8,128)(2,1)S(1)}, u32[]{:S(2)}, u32[]{:S(2)}) collective-permute-start(bf16[64,512]{1,0:T(8,128)(2,1)S(1)} %get-tuple-element.92), channel_id=1, source_target_pairs={{0,2},{1,3},{2,0},{3,1},{4,6},{5,7},{6,4},{7,5},{8,10},{9,11},{10,... | collective-permute-start | bytes 196616 | tf_op jit(solution)/shard_map/ppermute | solution.py:427
  17.1 1.2 %far_attention.4 = (bf16[128,512]{1,0:T(8,128)(2,1)S(1)}, bf16[128,512]{1,0:T(8,128)(2,1)S(1)}, bf16[128,512]{1,0:T(8,128)(2,1)S(1)}, bf16[128,512]{1,0:T(8,128)(2,1)S(1)}) custom-call(bf16[4,16,16,576]{3,2,1,0:T(8,128)(2,1)S(1)} %get-tuple-element.94.refs_0_, f32[4,16,16,128]{3,2,1,0:T(8,128)S(1)} %get-tuple-element.77.refs_1_, ...), custom_call_target="tpu_custom_call" | custom-call | flops 288358400 | bytes 4194304 | tf_op jit(solution)/shard_map/far_attention/pallas_call | solution.py:71
  18.7 1.8 %collective-permute-start.10 = (bf16[128,512]{1,0:T(8,128)(2,1)S(1)}, bf16[128,512]{1,0:T(8,128)(2,1)S(1)}, u32[]{:S(2)}, u32[]{:S(2)}) collective-permute-start(bf16[128,512]{1,0:T(8,128)(2,1)S(1)} %get-tuple-element.113), channel_id=1, source_target_pairs={{0,2},{1,3},{2,0},{3,1},{4,6},{5,7},{6,4},{7,5},{8,10},{9,11},{10,... | collective-permute-start | bytes 393224 | tf_op jit(solution)/shard_map/ppermute | solution.py:427
  20.5 0.9 %collective-permute-done.5.refs_3_ = bf16[64,512]{1,0:T(8,128)(2,1)S(1)} collective-permute-done((bf16[64,512]{1,0:T(8,128)(2,1)S(1)}, bf16[64,512]{1,0:T(8,128)(2,1)S(1)}, u32[]{:S(2)}, u32[]{:S(2)}) %collective-permute-start.5) | collective-permute-done | bytes 65568 | tf_op jit(solution)/shard_map/ppermute | solution.py:427
  21.4 0.9 %far_attention.5 = (bf16[64,512]{1,0:T(8,128)(2,1)S(1)}, bf16[64,512]{1,0:T(8,128)(2,1)S(1)}, bf16[64,512]{1,0:T(8,128)(2,1)S(1)}, bf16[64,512]{1,0:T(8,128)(2,1)S(1)}) custom-call(bf16[4,16,16,576]{3,2,1,0:T(8,128)(2,1)S(1)} %get-tuple-element.94.refs_0_, f32[4,16,16,128]{3,2,1,0:T(8,128)S(1)} %get-tuple-element.77.refs_1_, ...), custom_call_target="tpu_custom_call" | custom-call | flops 144179200 | bytes 4194304 | tf_op jit(solution)/shard_map/far_attention/pallas_call | solution.py:71
  22.5 1.1 %collective-permute-start.7 = (bf16[64,512]{1,0:T(8,128)(2,1)S(1)}, bf16[64,512]{1,0:T(8,128)(2,1)S(1)}, u32[]{:S(2)}, u32[]{:S(2)}) collective-permute-start(bf16[64,512]{1,0:T(8,128)(2,1)S(1)} %get-tuple-element.109), channel_id=1, source_target_pairs={{0,2},{1,3},{2,0},{3,1},{4,6},{5,7},{6,4},{7,5},{8,10},{9,11},{10,... | collective-permute-start | bytes 196616 | tf_op jit(solution)/shard_map/ppermute | solution.py:427
  23.6 2.1 %project.4 = (f32[64,7168]{1,0:T(8,128)S(1)}, bf16[256,7168]{1,0:T(8,128)(2,1)S(1)}) custom-call(bf16[64,512]{1,0:T(8,128)(2,1)S(1)} %get-tuple-element.115.refs_0_, bf16[64,512]{1,0:T(8,128)(2,1)S(1)} %collective-permute-done.3.refs_1_, bf16[64,512]{1,0:T(8,128)(2,1)S(1)} %collective-permute-done.4.refs_2_, ...), custom_call_target="tpu_custom_call" | custom-call | flops 1879048192 | bytes 7864320 | tf_op jit(solution)/shard_map/project/pallas_call | solution.py:71
  25.7 0.7 %collective-permute-start.8 = (bf16[64,512]{1,0:T(8,128)(2,1)S(1)}, bf16[64,512]{1,0:T(8,128)(2,1)S(1)}, u32[]{:S(2)}, u32[]{:S(2)}) collective-permute-start(bf16[64,512]{1,0:T(8,128)(2,1)S(1)} %get-tuple-element.110), channel_id=1, source_target_pairs={{0,3},{1,2},{2,1},{3,0},{4,7},{5,6},{6,5},{7,4},{8,11},{9,10},{10,... | collective-permute-start | bytes 196616 | tf_op jit(solution)/shard_map/ppermute | solution.py:427
  27.0 3.4 %project.5 = (f32[64,7168]{1,0:T(8,128)S(1)}, bf16[256,7168]{1,0:T(8,128)(2,1)S(1)}, bf16[256,7168]{1,0:T(8,128)(2,1)S(1)}) custom-call(bf16[128,512]{1,0:T(8,128)(2,1)S(1)} %get-tuple-element.111.refs_0_, bf16[128,512]{1,0:T(8,128)(2,1)S(1)} %collective-permute-done.9.refs_1_, ...), custom_call_target="tpu_custom_call", output_to_operand_aliasing={{0}: (4, {})} | custom-call | flops 3758096384 | bytes 11534336 | tf_op jit(solution)/shard_map/project/pallas_call | solution.py:71
  30.5 0.9 %project.6 = (bf16[32,3584]{1,0:T(8,128)(2,1)S(1)}, bf16[32,3584]{1,0:T(8,128)(2,1)S(1)}) custom-call(bf16[64,512]{1,0:T(8,128)(2,1)S(1)} %get-tuple-element.107.refs_0_, bf16[64,512]{1,0:T(8,128)(2,1)S(1)} %collective-permute-done.6.refs_1_, bf16[64,512]{1,0:T(8,128)(2,1)S(1)} %collective-permute-done.7.refs_2_, ...), custom_call_target="tpu_custom_call" | custom-call | flops 939524096 | bytes 4194304 | tf_op jit(solution)/shard_map/project/pallas_call | solution.py:71
  31.4 0.7 %collective-permute-start.12 = (bf16[32,3584]{1,0:T(8,128)(2,1)S(1)}, bf16[32,3584]{1,0:T(8,128)(2,1)S(1)}, u32[]{:S(2)}, u32[]{:S(2)}) collective-permute-start(bf16[32,3584]{1,0:T(8,128)(2,1)S(1)} %get-tuple-element.130), channel_id=1, source_target_pairs={{0,1},{1,0},{2,3},{3,2},{4,5},{5,4},{6,7},{7,6},{8,9},{9,8},{10,11... | collective-permute-start | bytes 688136 | tf_op jit(solution)/shard_map/ppermute | solution.py:427
  32.1 0.9 %project.7 = (bf16[32,3584]{1,0:T(8,128)(2,1)S(1)}, bf16[32,3584]{1,0:T(8,128)(2,1)S(1)}) custom-call(bf16[64,512]{1,0:T(8,128)(2,1)S(1)} %get-tuple-element.107.refs_0_, bf16[64,512]{1,0:T(8,128)(2,1)S(1)} %collective-permute-done.6.refs_1_, bf16[64,512]{1,0:T(8,128)(2,1)S(1)} %collective-permute-done.7.refs_2_, ...), custom_call_target="tpu_custom_call" | custom-call | flops 939524096 | bytes 4194304 | tf_op jit(solution)/shard_map/project/pallas_call | solution.py:71
  33.2 1.8 %collective-permute-start.13 = (bf16[16,3584]{1,0:T(8,128)(2,1)S(1)}, bf16[16,3584]{1,0:T(8,128)(2,1)S(1)}, u32[]{:S(2)}, u32[]{:S(2)}) collective-permute-start(bf16[16,3584]{1,0:T(8,128)(2,1)S(1)} %add_convert_fusion.1), channel_id=1, source_target_pairs={{0,2},{1,3},{2,0},{3,1},{4,6},{5,7},{6,4},{7,5},{8,10},{9,11},{10,... | collective-permute-start | bytes 344072 | tf_op jit(solution)/shard_map/ppermute | solution.py:427
  35.0 1.1 %collective-permute-start.15 = (bf16[16,3584]{1,0:T(8,128)(2,1)S(1)}, bf16[16,3584]{1,0:T(8,128)(2,1)S(1)}, u32[]{:S(2)}, u32[]{:S(2)}) collective-permute-start(bf16[16,3584]{1,0:T(8,128)(2,1)S(1)} %add_convert_fusion), channel_id=1, source_target_pairs={{0,3},{1,2},{2,1},{3,0},{4,7},{5,6},{6,5},{7,4},{8,11},{9,10},{10,... | collective-permute-start | bytes 344072 | tf_op jit(solution)/shard_map/ppermute | solution.py:427
  36.1 3.1 %collective-permute-done.13.refs_2_ = bf16[16,3584]{1,0:T(8,128)(2,1)S(1)} collective-permute-done((bf16[16,3584]{1,0:T(8,128)(2,1)S(1)}, bf16[16,3584]{1,0:T(8,128)(2,1)S(1)}, u32[]{:S(2)}, u32[]{:S(2)}) %collective-permute-start.13) | collective-permute-done | bytes 114720 | tf_op jit(solution)/shard_map/ppermute | solution.py:427
  39.2 1.5 %collective-permute-done.15.refs_5_ = bf16[16,3584]{1,0:T(8,128)(2,1)S(1)} collective-permute-done((bf16[16,3584]{1,0:T(8,128)(2,1)S(1)}, bf16[16,3584]{1,0:T(8,128)(2,1)S(1)}, u32[]{:S(2)}, u32[]{:S(2)}) %collective-permute-start.15) | collective-permute-done | bytes 114720 | tf_op jit(solution)/shard_map/ppermute | solution.py:427
  40.7 0.8 %last_sums.1 = bf16[8,2,7168]{2,1,0:T(2,128)(2,1)} custom-call(bf16[32,3584]{1,0:T(8,128)(2,1)S(1)} %get-tuple-element.129.refs_0_, bf16[32,3584]{1,0:T(8,128)(2,1)S(1)} %collective-permute-done.12.refs_1_, bf16[16,3584]{1,0:T(8,128)(2,1)S(1)} %collective-permute-done.13.refs_2_, bf16[32,3584]{1,0:T(8,128)(2,1)S(1)} %get-tuple-element.131.refs_3_, ...), custom_call_target="tpu_custom_call" | custom-call | tf_op jit(solution)/shard_map/last_sums/pallas_call | solution.py:386
  (34 shorter events, 2.4 us)
Async XLA Ops:
  0.0 1.1 %copy-start.5 = (f32[256,576]{0,1:T(8,128)S(1)}, f32[256,576]{0,1:T(8,128)}, u32[]{:S(2)}) copy-start(f32[256,576]{0,1:T(8,128)} %param.7) | copy-start | bytes 1769476
  0.0 4.2 %copy-start.4 = (s32[8]{0:T(128)S(1)}, s32[8]{0:T(128)}, u32[]{:S(2)}) copy-start(s32[8]{0:T(128)} %refs_1_.1) | copy-start | bytes 100
  0.0 4.2 %copy-start.1 = (bf16[8,256,576]{1,2,0:T(8,128)(2,1)S(1)}, bf16[8,256,576]{1,2,0:T(8,128)(2,1)}, u32[]{:S(2)}) copy-start(bf16[8,256,576]{1,2,0:T(8,128)(2,1)} %param.8) | copy-start | bytes 7077892
  0.0 4.2 %copy-start.3 = (bf16[8,2,576]{2,1,0:T(2,128)(2,1)S(1)}, bf16[8,2,576]{2,1,0:T(2,128)(2,1)}, u32[]{:S(2)}) copy-start(bf16[8,2,576]{2,1,0:T(2,128)(2,1)} %refs_4_.2) | copy-start | bytes 55300
  1.1 3.1 %collective-permute-start = (bf16[576,256]{1,0:T(8,128)(2,1)S(1)}, bf16[576,256]{1,0:T(8,128)(2,1)S(1)}, u32[]{:S(2)}, u32[]{:S(2)}) collective-permute-start(bf16[576,256]{1,0:T(8,128)(2,1)S(1)} %convert_bitcast_fusion.refs_5_), channel_id=1, source_target_pairs={{0,1},{1,0},{2,3},{3,2},{4,5},{5,4},{6,7},{7,6},{8,9},{9,8},{10,11... | collective-permute-start | bytes 884744 | tf_op jit(solution)/shard_map/ppermute | solution.py:427
  1.6 10.2 %collective-permute-start.1 = (bf16[576,256]{1,0:T(8,128)(2,1)S(1)}, bf16[576,256]{1,0:T(8,128)(2,1)S(1)}, u32[]{:S(2)}, u32[]{:S(2)}) collective-permute-start(bf16[576,256]{1,0:T(8,128)(2,1)S(1)} %convert_bitcast_fusion.refs_5_), channel_id=1, source_target_pairs={{0,2},{1,3},{2,0},{3,1},{4,6},{5,7},{6,4},{7,5},{8,10},{9,11},{10,... | collective-permute-start | bytes 884744 | tf_op jit(solution)/shard_map/ppermute | solution.py:427
  4.2 1.3 %copy-start.2 = (bf16[8,2,64,576]{3,2,1,0:T(8,128)(2,1)S(1)}, bf16[8,2,64,576]{3,2,1,0:T(8,128)(2,1)}, u32[]{:S(2)}) copy-start(bf16[8,2,64,576]{3,2,1,0:T(8,128)(2,1)} %refs_2_.1) | copy-start | bytes 3538948
  11.8 2.1 %collective-permute-start.2 = (bf16[576,256]{1,0:T(8,128)(2,1)S(1)}, bf16[576,256]{1,0:T(8,128)(2,1)S(1)}, u32[]{:S(2)}, u32[]{:S(2)}) collective-permute-start(bf16[576,256]{1,0:T(8,128)(2,1)S(1)} %collective-permute-done.1.refs_4_), channel_id=1, source_target_pairs={{0,1},{1,0},{2,3},{3,2},{4,5},{5,4},{6,7},{7,6},{8,9},{9,8},{10,11... | collective-permute-start | bytes 884744 | tf_op jit(solution)/shard_map/ppermute | solution.py:427
  14.7 8.9 %copy-start = (bf16[16,512,128]{2,1,0:T(8,128)(2,1)S(1)}, bf16[16,512,128]{2,1,0:T(8,128)(2,1)}, u32[]{:S(2)}) copy-start(bf16[16,512,128]{2,1,0:T(8,128)(2,1)} %refs_5_.7) | copy-start | bytes 6291460
  14.7 5.8 %collective-permute-start.3 = (bf16[64,512]{1,0:T(8,128)(2,1)S(1)}, bf16[64,512]{1,0:T(8,128)(2,1)S(1)}, u32[]{:S(2)}, u32[]{:S(2)}) collective-permute-start(bf16[64,512]{1,0:T(8,128)(2,1)S(1)} %get-tuple-element.91), channel_id=1, source_target_pairs={{0,1},{1,0},{2,3},{3,2},{4,5},{5,4},{6,7},{7,6},{8,9},{9,8},{10,11... | collective-permute-start | bytes 196616 | tf_op jit(solution)/shard_map/ppermute | solution.py:427
  15.3 5.2 %collective-permute-start.4 = (bf16[64,512]{1,0:T(8,128)(2,1)S(1)}, bf16[64,512]{1,0:T(8,128)(2,1)S(1)}, u32[]{:S(2)}, u32[]{:S(2)}) collective-permute-start(bf16[64,512]{1,0:T(8,128)(2,1)S(1)} %get-tuple-element.92), channel_id=1, source_target_pairs={{0,2},{1,3},{2,0},{3,1},{4,6},{5,7},{6,4},{7,5},{8,10},{9,11},{10,... | collective-permute-start | bytes 196616 | tf_op jit(solution)/shard_map/ppermute | solution.py:427
  17.1 4.4 %collective-permute-start.5 = (bf16[64,512]{1,0:T(8,128)(2,1)S(1)}, bf16[64,512]{1,0:T(8,128)(2,1)S(1)}, u32[]{:S(2)}, u32[]{:S(2)}) collective-permute-start(bf16[64,512]{1,0:T(8,128)(2,1)S(1)} %get-tuple-element.93), channel_id=1, source_target_pairs={{0,3},{1,2},{2,1},{3,0},{4,7},{5,6},{6,5},{7,4},{8,11},{9,10},{10,... | collective-permute-start | bytes 196616 | tf_op jit(solution)/shard_map/ppermute | solution.py:427
  18.3 7.4 %collective-permute-start.9 = (bf16[128,512]{1,0:T(8,128)(2,1)S(1)}, bf16[128,512]{1,0:T(8,128)(2,1)S(1)}, u32[]{:S(2)}, u32[]{:S(2)}) collective-permute-start(bf16[128,512]{1,0:T(8,128)(2,1)S(1)} %get-tuple-element.112), channel_id=1, source_target_pairs={{0,1},{1,0},{2,3},{3,2},{4,5},{5,4},{6,7},{7,6},{8,9},{9,8},{10,11... | collective-permute-start | bytes 393224 | tf_op jit(solution)/shard_map/ppermute | solution.py:427
  18.7 7.7 %collective-permute-start.10 = (bf16[128,512]{1,0:T(8,128)(2,1)S(1)}, bf16[128,512]{1,0:T(8,128)(2,1)S(1)}, u32[]{:S(2)}, u32[]{:S(2)}) collective-permute-start(bf16[128,512]{1,0:T(8,128)(2,1)S(1)} %get-tuple-element.113), channel_id=1, source_target_pairs={{0,2},{1,3},{2,0},{3,1},{4,6},{5,7},{6,4},{7,5},{8,10},{9,11},{10,... | collective-permute-start | bytes 393224 | tf_op jit(solution)/shard_map/ppermute | solution.py:427
  20.5 6.5 %collective-permute-start.11 = (bf16[128,512]{1,0:T(8,128)(2,1)S(1)}, bf16[128,512]{1,0:T(8,128)(2,1)S(1)}, u32[]{:S(2)}, u32[]{:S(2)}) collective-permute-start(bf16[128,512]{1,0:T(8,128)(2,1)S(1)} %get-tuple-element.114), channel_id=1, source_target_pairs={{0,3},{1,2},{2,1},{3,0},{4,7},{5,6},{6,5},{7,4},{8,11},{9,10},{10,... | collective-permute-start | bytes 393224 | tf_op jit(solution)/shard_map/ppermute | solution.py:427
  22.3 8.1 %collective-permute-start.6 = (bf16[64,512]{1,0:T(8,128)(2,1)S(1)}, bf16[64,512]{1,0:T(8,128)(2,1)S(1)}, u32[]{:S(2)}, u32[]{:S(2)}) collective-permute-start(bf16[64,512]{1,0:T(8,128)(2,1)S(1)} %get-tuple-element.108), channel_id=1, source_target_pairs={{0,1},{1,0},{2,3},{3,2},{4,5},{5,4},{6,7},{7,6},{8,9},{9,8},{10,11... | collective-permute-start | bytes 196616 | tf_op jit(solution)/shard_map/ppermute | solution.py:427
  22.5 8.0 %collective-permute-start.7 = (bf16[64,512]{1,0:T(8,128)(2,1)S(1)}, bf16[64,512]{1,0:T(8,128)(2,1)S(1)}, u32[]{:S(2)}, u32[]{:S(2)}) collective-permute-start(bf16[64,512]{1,0:T(8,128)(2,1)S(1)} %get-tuple-element.109), channel_id=1, source_target_pairs={{0,2},{1,3},{2,0},{3,1},{4,6},{5,7},{6,4},{7,5},{8,10},{9,11},{10,... | collective-permute-start | bytes 196616 | tf_op jit(solution)/shard_map/ppermute | solution.py:427
  25.7 4.7 %collective-permute-start.8 = (bf16[64,512]{1,0:T(8,128)(2,1)S(1)}, bf16[64,512]{1,0:T(8,128)(2,1)S(1)}, u32[]{:S(2)}, u32[]{:S(2)}) collective-permute-start(bf16[64,512]{1,0:T(8,128)(2,1)S(1)} %get-tuple-element.110), channel_id=1, source_target_pairs={{0,3},{1,2},{2,1},{3,0},{4,7},{5,6},{6,5},{7,4},{8,11},{9,10},{10,... | collective-permute-start | bytes 196616 | tf_op jit(solution)/shard_map/ppermute | solution.py:427
  31.4 1.8 %collective-permute-start.12 = (bf16[32,3584]{1,0:T(8,128)(2,1)S(1)}, bf16[32,3584]{1,0:T(8,128)(2,1)S(1)}, u32[]{:S(2)}, u32[]{:S(2)}) collective-permute-start(bf16[32,3584]{1,0:T(8,128)(2,1)S(1)} %get-tuple-element.130), channel_id=1, source_target_pairs={{0,1},{1,0},{2,3},{3,2},{4,5},{5,4},{6,7},{7,6},{8,9},{9,8},{10,11... | collective-permute-start | bytes 688136 | tf_op jit(solution)/shard_map/ppermute | solution.py:427
  33.0 2.0 %collective-permute-start.14 = (bf16[32,3584]{1,0:T(8,128)(2,1)S(1)}, bf16[32,3584]{1,0:T(8,128)(2,1)S(1)}, u32[]{:S(2)}, u32[]{:S(2)}) collective-permute-start(bf16[32,3584]{1,0:T(8,128)(2,1)S(1)} %get-tuple-element.132), channel_id=1, source_target_pairs={{0,1},{1,0},{2,3},{3,2},{4,5},{5,4},{6,7},{7,6},{8,9},{9,8},{10,11... | collective-permute-start | bytes 688136 | tf_op jit(solution)/shard_map/ppermute | solution.py:427
  33.2 6.0 %collective-permute-start.13 = (bf16[16,3584]{1,0:T(8,128)(2,1)S(1)}, bf16[16,3584]{1,0:T(8,128)(2,1)S(1)}, u32[]{:S(2)}, u32[]{:S(2)}) collective-permute-start(bf16[16,3584]{1,0:T(8,128)(2,1)S(1)} %add_convert_fusion.1), channel_id=1, source_target_pairs={{0,2},{1,3},{2,0},{3,1},{4,6},{5,7},{6,4},{7,5},{8,10},{9,11},{10,... | collective-permute-start | bytes 344072 | tf_op jit(solution)/shard_map/ppermute | solution.py:427
  35.0 5.7 %collective-permute-start.15 = (bf16[16,3584]{1,0:T(8,128)(2,1)S(1)}, bf16[16,3584]{1,0:T(8,128)(2,1)S(1)}, u32[]{:S(2)}, u32[]{:S(2)}) collective-permute-start(bf16[16,3584]{1,0:T(8,128)(2,1)S(1)} %add_convert_fusion), channel_id=1, source_target_pairs={{0,3},{1,2},{2,1},{3,0},{4,7},{5,6},{6,5},{7,4},{8,11},{9,10},{10,... | collective-permute-start | bytes 344072 | tf_op jit(solution)/shard_map/ppermute | solution.py:427

commit v4 on v3

--- a/solution.py
+++ b/solution.py
@@ -17,6 +17,9 @@
 BLOCK = 256
 MIB = 2**20
 W_PIECES = 2
+NEAR_LIMIT = 20
+FAR_LIMIT = 20
+PROJECT_LIMIT = 10
 PAUSE_FLOPS = 10**10
 PAUSE_BYTES = 30 * MIB
 
@@ -96,7 +99,7 @@
     return new_m, l, probs_into(acc * shrink, [p.astype(jnp.bfloat16) for p in weights])
 
 
-def in_turn(tasks, score, finish):
+def in_turn(tasks, score, finish, looped):
     def some(first, count):
         before = None
         for i in range(count):
@@ -107,7 +110,7 @@
             before = (task, now)
         finish(*before)
 
-    if tasks % 2 or tasks < 4:
+    if tasks % 2 or not looped:
         some(0, tasks)
     else:
 
@@ -180,7 +183,7 @@
                 l_ref[:, there] = jnp.broadcast_to(l[here], (per, 128)).reshape(lead + (128,))
                 acc_ref[:, there] = part.reshape(lead + (LATENT,))
 
-        in_turn(rows * per // BLOCK, score, finish)
+        in_turn(rows * per // BLOCK, score, finish, True)
 
     vmem, smem = pl.BlockSpec(memory_space=pltpu.VMEM), pl.BlockSpec(memory_space=pltpu.SMEM)
     lead = (units, rows * steps, tile)
@@ -197,13 +200,13 @@
         ],
         [],
         bring,
-        24,
+        NEAR_LIMIT,
         4 * rows * per * 1100 * 768,
         "near_attention",
     )
 
 
-def merge(first, size, keys, q_ref, m_ref, l_ref, acc_ref, store):
+def merge(first, size, keys, q_ref, m_ref, l_ref, acc_ref, store, looped):
     _, pairs, tile, width = q_ref.shape
     step = BLOCK // tile
     blocks = pairs // step
@@ -230,7 +233,7 @@
             ),
         )
 
-    in_turn(size * blocks, score, finish)
+    in_turn(size * blocks, score, finish, looped)
 
 
 def middle_call(queries, state, keys, bring):
@@ -246,7 +249,7 @@
             l_out[here] = jnp.broadcast_to(l, (BLOCK, 128)).reshape(lead + (128,))
             acc_out[here] = acc.reshape(lead + (LATENT,))
 
-        merge(0, units, [k[...] for k in key_refs], q_ref, m_ref, l_ref, acc_ref, store)
+        merge(0, units, [k[...] for k in key_refs], q_ref, m_ref, l_ref, acc_ref, store, True)
 
     operands = [queries, *state, *keys]
     return call(
@@ -277,7 +280,7 @@
                 done[g, rows, :] = attended[:, g * 128 : (g + 1) * 128]
 
         keys_now = [k[...] for k in key_refs]
-        merge(first, size, keys_now, q_ref, m_ref, l_ref, acc_ref, store)
+        merge(first, size, keys_now, q_ref, m_ref, l_ref, acc_ref, store, bool(bring[2]))
         me = lax.axis_index("roll")
         for k in range(axis_size):
             there = jnp.bitwise_xor(me, k) * CHUNK_HEADS
@@ -297,7 +300,7 @@
         [jax.ShapeDtypeStruct((size * CHUNK_HEADS * pairs, LATENT), jnp.bfloat16)] * axis_size,
         [pltpu.VMEM((LATENT // 128, size * per_unit + tile, 128), jnp.float32)],
         bring,
-        24 if bring[2] else 10,
+        FAR_LIMIT if bring[2] else 8,
         2 * size * per_unit * 1100 * 256 * len(keys),
         "far_attention",
     )
@@ -359,7 +362,7 @@
         out_shape,
         [],
         bring,
-        14 if bring[2] else 8,
+        PROJECT_LIMIT if bring[2] else 8,
         8 * total_rows * heads * w_uv.shape[2] * cols,
         "project",
         {len(pieces): 0} if acc is not None and kept is None else {},
@@ -400,19 +403,16 @@
     width = w_out.shape[1]
     share = heads // n
     units = share // CHUNK_HEADS
-    chunks = [(0, 1), (1, units - 2), (units - 1, 1)] if units > 2 else [(u, 1) for u in range(units)]
+    chunks = [(0, units // 2), (units // 2, units - units // 2)] if units > 1 else [(0, 1)]
     piece_rows = CHUNK_HEADS * w_uv.shape[2] // W_PIECES
     n_pieces = units * W_PIECES
-    if len(chunks) == 3 and n_pieces == 8:
-        brings = {
-            "near": [0, 1, 2, 3],
-            "middle": [4],
-            ("project", 0): [5],
-            ("project", 1): [6, 7],
-        }
+    half = n_pieces // 2
+    brings = {"near": list(range(half))}
+    if len(chunks) > 1:
+        brings["far", 1] = list(range(half, half + half // 4))
+        brings["project", 0] = list(range(half + half // 4, n_pieces))
     else:
-        half = n_pieces // 2
-        brings = {"near": list(range(half)), "middle": list(range(half, n_pieces))}
+        brings["middle"] = list(range(half, n_pieces))
     held = {}
 
     def bring(who):
@@ -450,15 +450,11 @@
     state = keep("middle", middle_call(queries, (m, l, acc), across, bring("middle")))
     got = []
     for c, (first, size) in enumerate(chunks):
-        if c >= 2:
-            queries, *got[c - 2] = lax.optimization_barrier((queries, *got[c - 2]))
         who = ("far", c)
         mine = keep(who, far_call(first, size, queries, state, forwarded, n, bring(who)))
-        if c >= 2:
-            *mine, got[c - 2] = lax.optimization_barrier((*mine, got[c - 2]))
         *mine, queries = lax.optimization_barrier((*mine, queries))
         there = [mine[0]] + [None] * (n - 1)
-        for k in range(1, n):
+        for k in [*range(2, n), 1]:
             there[k] = swap(mine[k], k)
         got.append(there)
     acc = None

time: 41.8 us -> 40.4 us (0.967)
  starting transfers between devices: 13.2 us -> 11.3 us
  waiting for transfers between devices: 6.67 us -> 7.83 us
  Pallas kernels: 19 us -> 18.5 us
    ppermute x16 -> x13, starting transfers between devices: 13.2 us -> 11.3 us  [swap(): return lax.ppermute(x, 'roll', [(i, i ^ k) for i in range(n)])]
    ppermute x16 -> x13, waiting for transfers between devices: 6.67 us -> 7.83 us  [swap(): return lax.ppermute(x, 'roll', [(i, i ^ k) for i in range(n)])]
    pallas_call x9 -> x7, Pallas kernels: 18.2 us -> 17.6 us  [call(): pl.pallas_call(kernel, in_specs=in_specs, out_specs=[vmem] * len(out_shap...]
  transfers between devices with their start and end apart: 16 -> 13, of which waited for: 6 -> 6; matrix products, arithmetic and copies ran while one was open for 0% -> 0% of each run, Pallas kernels for 39% -> 38%
where the time goes in v4:
time: 40.4 us; the launch traced here: 40.2 us
  Pallas kernels  18.5 us (46%)
  starting transfers between devices  11.3 us (28%)
  waiting for transfers between devices  7.83 us (19%)
  local copies, waits for them, and re-layouts  2.38 us (6%)
    pallas_call x7, Pallas kernels, call(): pl.pallas_call(kernel, in_specs=in_specs, out_specs=[vmem] * len(out_shap...  17.6 us
    ppermute x13, starting transfers between devices, swap(): return lax.ppermute(x, 'roll', [(i, i ^ k) for i in range(n)])  11.3 us
    ppermute x13, waiting for transfers between devices, swap(): return lax.ppermute(x, 'roll', [(i, i ^ k) for i in range(n)])  7.83 us
    unnamed x12, local copies, waits for them, and re-layouts  2.38 us
  transfers between devices with their start and end apart: 13, of which 6 were waited for; matrix products, arithmetic and copies ran while one was open for 0% of the time, Pallas kernels for 38%

profile of v4, /device:TPU:0, one launch (start us, length us, event | category | flops | bytes accessed | tf_op | source)
XLA Modules:
  0.0 40.2 jit_solution(11168873814240909286)
XLA Ops:
  0.0 1.1 %copy-done.5 = f32[256,576]{0,1:T(8,128)S(1)} copy-done((f32[256,576]{0,1:T(8,128)S(1)}, f32[256,576]{0,1:T(8,128)}, u32[]{:S(2)}) %copy-start.5) | copy-done | bytes 589848
  1.1 0.5 %collective-permute-start = (bf16[576,256]{1,0:T(8,128)(2,1)S(1)}, bf16[576,256]{1,0:T(8,128)(2,1)S(1)}, u32[]{:S(2)}, u32[]{:S(2)}) collective-permute-start(bf16[576,256]{1,0:T(8,128)(2,1)S(1)} %convert_bitcast_fusion.refs_5_), channel_id=1, source_target_pairs={{0,1},{1,0},{2,3},{3,2},{4,5},{5,4},{6,7},{7,6},{8,9},{9,8},{10,11... | collective-permute-start | bytes 884744 | tf_op jit(solution)/shard_map/ppermute | solution.py:427
  1.6 2.6 %collective-permute-start.1 = (bf16[576,256]{1,0:T(8,128)(2,1)S(1)}, bf16[576,256]{1,0:T(8,128)(2,1)S(1)}, u32[]{:S(2)}, u32[]{:S(2)}) collective-permute-start(bf16[576,256]{1,0:T(8,128)(2,1)S(1)} %convert_bitcast_fusion.refs_5_), channel_id=1, source_target_pairs={{0,2},{1,3},{2,0},{3,1},{4,6},{5,7},{6,4},{7,5},{8,10},{9,11},{10,... | collective-permute-start | bytes 884744 | tf_op jit(solution)/shard_map/ppermute | solution.py:427
  4.2 1.3 %copy-done.2 = bf16[8,2,64,576]{3,2,1,0:T(8,128)(2,1)S(1)} copy-done((bf16[8,2,64,576]{3,2,1,0:T(8,128)(2,1)S(1)}, bf16[8,2,64,576]{3,2,1,0:T(8,128)(2,1)}, u32[]{:S(2)}) %copy-start.2) | copy-done | bytes 1179672
  5.5 5.8 %near_attention.1 = (bf16[4,16,16,576]{3,2,1,0:T(8,128)(2,1)S(1)}, f32[4,16,16,128]{3,2,1,0:T(8,128)S(1)}, f32[4,16,16,128]{3,2,1,0:T(8,128)S(1)}, f32[4,16,16,5...) custom-call(f32[8,128]{1,0:T(8,128)S(1)} %pause.1.refs_0_, ...), custom_call_target="tpu_custom_call" | custom-call | flops 3460300800 | bytes 18874368 | tf_op jit(solution)/shard_map/near_attention/pallas_call | solution.py:74
  11.4 0.4 %collective-permute-done.1.refs_4_ = bf16[576,256]{1,0:T(8,128)(2,1)S(1)} collective-permute-done((bf16[576,256]{1,0:T(8,128)(2,1)S(1)}, bf16[576,256]{1,0:T(8,128)(2,1)S(1)}, u32[]{:S(2)}, u32[]{:S(2)}) %collective-permute-start.1) | collective-permute-done | bytes 294944 | tf_op jit(solution)/shard_map/ppermute | solution.py:427
  11.8 1.6 %middle_attention.1 = (f32[4,16,16,128]{3,2,1,0:T(8,128)S(1)}, f32[4,16,16,128]{3,2,1,0:T(8,128)S(1)}, f32[4,16,16,512]{3,2,1,0:T(8,128)S(1)}) custom-call(bf16[4,16,16,576]{3,2,1,0:T(8,128)(2,1)S(1)} %get-tuple-element.61.refs_0_, f32[4,16,16,128]{3,2,1,0:T(8,128)S(1)} %get-tuple-element.50.refs_1_, f32[4,16,16,128]{3,2,1,0:T(8,128)S(1)} %get-tuple-element.51.refs_2_, ...), custom_call_target="tpu_custom_call" | custom-call | flops 576716800 | bytes 4194304 | tf_op jit(solution)/shard_map/middle_attention/pallas_call | solution.py:74
  13.4 1.2 %far_attention.2 = (bf16[128,512]{1,0:T(8,128)(2,1)S(1)}, bf16[128,512]{1,0:T(8,128)(2,1)S(1)}, bf16[128,512]{1,0:T(8,128)(2,1)S(1)}, bf16[128,512]{1,0:T(8,128)(2,1)S(1)}) custom-call(bf16[4,16,16,576]{3,2,1,0:T(8,128)(2,1)S(1)} %get-tuple-element.61.refs_0_, f32[4,16,16,128]{3,2,1,0:T(8,128)S(1)} %get-tuple-element.54.refs_1_, ...), custom_call_target="tpu_custom_call" | custom-call | flops 288358400 | bytes 4194304 | tf_op jit(solution)/shard_map/far_attention/pallas_call | solution.py:74
  14.7 0.6 %collective-permute-start.6 = (bf16[128,512]{1,0:T(8,128)(2,1)S(1)}, bf16[128,512]{1,0:T(8,128)(2,1)S(1)}, u32[]{:S(2)}, u32[]{:S(2)}) collective-permute-start(bf16[128,512]{1,0:T(8,128)(2,1)S(1)} %get-tuple-element.71), channel_id=1, source_target_pairs={{0,1},{1,0},{2,3},{3,2},{4,5},{5,4},{6,7},{7,6},{8,9},{9,8},{10,11... | collective-permute-start | bytes 393224 | tf_op jit(solution)/shard_map/ppermute | solution.py:427
  15.2 1.8 %collective-permute-start.7 = (bf16[128,512]{1,0:T(8,128)(2,1)S(1)}, bf16[128,512]{1,0:T(8,128)(2,1)S(1)}, u32[]{:S(2)}, u32[]{:S(2)}) collective-permute-start(bf16[128,512]{1,0:T(8,128)(2,1)S(1)} %get-tuple-element.72), channel_id=1, source_target_pairs={{0,2},{1,3},{2,0},{3,1},{4,6},{5,7},{6,4},{7,5},{8,10},{9,11},{10,... | collective-permute-start | bytes 393224 | tf_op jit(solution)/shard_map/ppermute | solution.py:427
  17.0 2.0 %far_attention.3 = (bf16[128,512]{1,0:T(8,128)(2,1)S(1)}, bf16[128,512]{1,0:T(8,128)(2,1)S(1)}, bf16[128,512]{1,0:T(8,128)(2,1)S(1)}, bf16[128,512]{1,0:T(8,128)(2,1)S(1)}, bf16[256,7168]{1,0:T(8,128)(2,1)S(1)}) custom-call(bf16[4,16,16,576]{3,2,1,0:T(8,128)(2,1)S(1)} %get-tuple-element.61.refs_0_, f32[4,16,16,128]{3,2,1,0:T(8,128)S(1)} %get-tuple-element.54.refs_1_, ...), custom_call_target="tpu_custom_call" | custom-call | flops 288358400 | bytes 7864320 | tf_op jit(solution)/shard_map/far_attention/pallas_call | solution.py:74
  19.0 0.4 %collective-permute-start.3 = (bf16[128,512]{1,0:T(8,128)(2,1)S(1)}, bf16[128,512]{1,0:T(8,128)(2,1)S(1)}, u32[]{:S(2)}, u32[]{:S(2)}) collective-permute-start(bf16[128,512]{1,0:T(8,128)(2,1)S(1)} %get-tuple-element.67), channel_id=1, source_target_pairs={{0,1},{1,0},{2,3},{3,2},{4,5},{5,4},{6,7},{7,6},{8,9},{9,8},{10,11... | collective-permute-start | bytes 393224 | tf_op jit(solution)/shard_map/ppermute | solution.py:427
  19.5 1.8 %collective-permute-start.4 = (bf16[128,512]{1,0:T(8,128)(2,1)S(1)}, bf16[128,512]{1,0:T(8,128)(2,1)S(1)}, u32[]{:S(2)}, u32[]{:S(2)}) collective-permute-start(bf16[128,512]{1,0:T(8,128)(2,1)S(1)} %get-tuple-element.68), channel_id=1, source_target_pairs={{0,2},{1,3},{2,0},{3,1},{4,6},{5,7},{6,4},{7,5},{8,10},{9,11},{10,... | collective-permute-start | bytes 393224 | tf_op jit(solution)/shard_map/ppermute | solution.py:427
  21.5 2.2 %collective-permute-done.8.refs_3_ = bf16[128,512]{1,0:T(8,128)(2,1)S(1)} collective-permute-done((bf16[128,512]{1,0:T(8,128)(2,1)S(1)}, bf16[128,512]{1,0:T(8,128)(2,1)S(1)}, u32[]{:S(2)}, u32[]{:S(2)}) %collective-permute-start.8) | collective-permute-done | bytes 131104 | tf_op jit(solution)/shard_map/ppermute | solution.py:427
  23.7 4.4 %project.3 = (f32[64,7168]{1,0:T(8,128)S(1)}, bf16[256,7168]{1,0:T(8,128)(2,1)S(1)}, bf16[256,7168]{1,0:T(8,128)(2,1)S(1)}, bf16[256,7168]{1,0:T(8,128)(2,1)S(1)}) custom-call(bf16[128,512]{1,0:T(8,128)(2,1)S(1)} %get-tuple-element.70.refs_0_, bf16[128,512]{1,0:T(8,128)(2,1)S(1)} %collective-permute-done.6.refs_1_, ...), custom_call_target="tpu_custom_call" | custom-call | flops 3758096384 | bytes 15204352 | tf_op jit(solution)/shard_map/project/pallas_call | solution.py:74
  28.1 0.3 collective-permute-done.5.refs_3_
  28.4 1.3 %project.4 = (bf16[32,3584]{1,0:T(8,128)(2,1)S(1)}, bf16[32,3584]{1,0:T(8,128)(2,1)S(1)}) custom-call(bf16[128,512]{1,0:T(8,128)(2,1)S(1)} %get-tuple-element.66.refs_0_, bf16[128,512]{1,0:T(8,128)(2,1)S(1)} %collective-permute-done.3.refs_1_, bf16[128,512]{1,0:T(8,128)(2,1)S(1)} %collective-permute-done.4.refs_2_, ...), custom_call_target="tpu_custom_call" | custom-call | flops 1879048192 | bytes 4194304 | tf_op jit(solution)/shard_map/project/pallas_call | solution.py:74
  29.7 0.6 %collective-permute-start.9 = (bf16[32,3584]{1,0:T(8,128)(2,1)S(1)}, bf16[32,3584]{1,0:T(8,128)(2,1)S(1)}, u32[]{:S(2)}, u32[]{:S(2)}) collective-permute-start(bf16[32,3584]{1,0:T(8,128)(2,1)S(1)} %get-tuple-element.84), channel_id=1, source_target_pairs={{0,1},{1,0},{2,3},{3,2},{4,5},{5,4},{6,7},{7,6},{8,9},{9,8},{10,11... | collective-permute-start | bytes 688136 | tf_op jit(solution)/shard_map/ppermute | solution.py:427
  30.3 1.3 %project.5 = (bf16[32,3584]{1,0:T(8,128)(2,1)S(1)}, bf16[32,3584]{1,0:T(8,128)(2,1)S(1)}) custom-call(bf16[128,512]{1,0:T(8,128)(2,1)S(1)} %get-tuple-element.66.refs_0_, bf16[128,512]{1,0:T(8,128)(2,1)S(1)} %collective-permute-done.3.refs_1_, bf16[128,512]{1,0:T(8,128)(2,1)S(1)} %collective-permute-done.4.refs_2_, ...), custom_call_target="tpu_custom_call" | custom-call | flops 1879048192 | bytes 4194304 | tf_op jit(solution)/shard_map/project/pallas_call | solution.py:74
  31.7 1.8 %collective-permute-start.10 = (bf16[16,3584]{1,0:T(8,128)(2,1)S(1)}, bf16[16,3584]{1,0:T(8,128)(2,1)S(1)}, u32[]{:S(2)}, u32[]{:S(2)}) collective-permute-start(bf16[16,3584]{1,0:T(8,128)(2,1)S(1)} %add_convert_fusion.1), channel_id=1, source_target_pairs={{0,2},{1,3},{2,0},{3,1},{4,6},{5,7},{6,4},{7,5},{8,10},{9,11},{10,... | collective-permute-start | bytes 344072 | tf_op jit(solution)/shard_map/ppermute | solution.py:427
  33.6 1.2 %collective-permute-start.12 = (bf16[16,3584]{1,0:T(8,128)(2,1)S(1)}, bf16[16,3584]{1,0:T(8,128)(2,1)S(1)}, u32[]{:S(2)}, u32[]{:S(2)}) collective-permute-start(bf16[16,3584]{1,0:T(8,128)(2,1)S(1)} %add_convert_fusion), channel_id=1, source_target_pairs={{0,3},{1,2},{2,1},{3,0},{4,7},{5,6},{6,5},{7,4},{8,11},{9,10},{10,... | collective-permute-start | bytes 344072 | tf_op jit(solution)/shard_map/ppermute | solution.py:427
  34.7 3.0 %collective-permute-done.10.refs_2_ = bf16[16,3584]{1,0:T(8,128)(2,1)S(1)} collective-permute-done((bf16[16,3584]{1,0:T(8,128)(2,1)S(1)}, bf16[16,3584]{1,0:T(8,128)(2,1)S(1)}, u32[]{:S(2)}, u32[]{:S(2)}) %collective-permute-start.10) | collective-permute-done | bytes 114720 | tf_op jit(solution)/shard_map/ppermute | solution.py:427
  37.7 1.6 %collective-permute-done.12.refs_5_ = bf16[16,3584]{1,0:T(8,128)(2,1)S(1)} collective-permute-done((bf16[16,3584]{1,0:T(8,128)(2,1)S(1)}, bf16[16,3584]{1,0:T(8,128)(2,1)S(1)}, u32[]{:S(2)}, u32[]{:S(2)}) %collective-permute-start.12) | collective-permute-done | bytes 114720 | tf_op jit(solution)/shard_map/ppermute | solution.py:427
  39.4 0.8 %last_sums.1 = bf16[8,2,7168]{2,1,0:T(2,128)(2,1)} custom-call(bf16[32,3584]{1,0:T(8,128)(2,1)S(1)} %get-tuple-element.83.refs_0_, bf16[32,3584]{1,0:T(8,128)(2,1)S(1)} %collective-permute-done.9.refs_1_, bf16[16,3584]{1,0:T(8,128)(2,1)S(1)} %collective-permute-done.10.refs_2_, bf16[32,3584]{1,0:T(8,128)(2,1)S(1)} %get-tuple-element.85.refs_3_, ...), custom_call_target="tpu_custom_call" | custom-call | tf_op jit(solution)/shard_map/last_sums/pallas_call | solution.py:389
  (26 shorter events, 0.4 us)
Async XLA Ops:
  0.0 1.1 %copy-start.5 = (f32[256,576]{0,1:T(8,128)S(1)}, f32[256,576]{0,1:T(8,128)}, u32[]{:S(2)}) copy-start(f32[256,576]{0,1:T(8,128)} %param.7) | copy-start | bytes 1769476
  0.0 4.2 %copy-start.4 = (s32[8]{0:T(128)S(1)}, s32[8]{0:T(128)}, u32[]{:S(2)}) copy-start(s32[8]{0:T(128)} %refs_1_.1) | copy-start | bytes 100
  0.0 4.2 %copy-start.1 = (bf16[8,256,576]{1,2,0:T(8,128)(2,1)S(1)}, bf16[8,256,576]{1,2,0:T(8,128)(2,1)}, u32[]{:S(2)}) copy-start(bf16[8,256,576]{1,2,0:T(8,128)(2,1)} %param.8) | copy-start | bytes 7077892
  0.0 4.2 %copy-start.3 = (bf16[8,2,576]{2,1,0:T(2,128)(2,1)S(1)}, bf16[8,2,576]{2,1,0:T(2,128)(2,1)}, u32[]{:S(2)}) copy-start(bf16[8,2,576]{2,1,0:T(2,128)(2,1)} %refs_4_.2) | copy-start | bytes 55300
  1.1 3.1 %collective-permute-start = (bf16[576,256]{1,0:T(8,128)(2,1)S(1)}, bf16[576,256]{1,0:T(8,128)(2,1)S(1)}, u32[]{:S(2)}, u32[]{:S(2)}) collective-permute-start(bf16[576,256]{1,0:T(8,128)(2,1)S(1)} %convert_bitcast_fusion.refs_5_), channel_id=1, source_target_pairs={{0,1},{1,0},{2,3},{3,2},{4,5},{5,4},{6,7},{7,6},{8,9},{9,8},{10,11... | collective-permute-start | bytes 884744 | tf_op jit(solution)/shard_map/ppermute | solution.py:427
  1.6 10.2 %collective-permute-start.1 = (bf16[576,256]{1,0:T(8,128)(2,1)S(1)}, bf16[576,256]{1,0:T(8,128)(2,1)S(1)}, u32[]{:S(2)}, u32[]{:S(2)}) collective-permute-start(bf16[576,256]{1,0:T(8,128)(2,1)S(1)} %convert_bitcast_fusion.refs_5_), channel_id=1, source_target_pairs={{0,2},{1,3},{2,0},{3,1},{4,6},{5,7},{6,4},{7,5},{8,10},{9,11},{10,... | collective-permute-start | bytes 884744 | tf_op jit(solution)/shard_map/ppermute | solution.py:427
  4.2 1.3 %copy-start.2 = (bf16[8,2,64,576]{3,2,1,0:T(8,128)(2,1)S(1)}, bf16[8,2,64,576]{3,2,1,0:T(8,128)(2,1)}, u32[]{:S(2)}) copy-start(bf16[8,2,64,576]{3,2,1,0:T(8,128)(2,1)} %refs_2_.1) | copy-start | bytes 3538948
  11.8 1.6 %collective-permute-start.2 = (bf16[576,256]{1,0:T(8,128)(2,1)S(1)}, bf16[576,256]{1,0:T(8,128)(2,1)S(1)}, u32[]{:S(2)}, u32[]{:S(2)}) collective-permute-start(bf16[576,256]{1,0:T(8,128)(2,1)S(1)} %collective-permute-done.1.refs_4_), channel_id=1, source_target_pairs={{0,1},{1,0},{2,3},{3,2},{4,5},{5,4},{6,7},{7,6},{8,9},{9,8},{10,11... | collective-permute-start | bytes 884744 | tf_op jit(solution)/shard_map/ppermute | solution.py:427
  14.7 9.0 %copy-start = (bf16[16,512,128]{2,1,0:T(8,128)(2,1)S(1)}, bf16[16,512,128]{2,1,0:T(8,128)(2,1)}, u32[]{:S(2)}) copy-start(bf16[16,512,128]{2,1,0:T(8,128)(2,1)} %refs_5_.5) | copy-start | bytes 6291460
  14.7 6.6 %collective-permute-start.6 = (bf16[128,512]{1,0:T(8,128)(2,1)S(1)}, bf16[128,512]{1,0:T(8,128)(2,1)S(1)}, u32[]{:S(2)}, u32[]{:S(2)}) collective-permute-start(bf16[128,512]{1,0:T(8,128)(2,1)S(1)} %get-tuple-element.71), channel_id=1, source_target_pairs={{0,1},{1,0},{2,3},{3,2},{4,5},{5,4},{6,7},{7,6},{8,9},{9,8},{10,11... | collective-permute-start | bytes 393224 | tf_op jit(solution)/shard_map/ppermute | solution.py:427
  15.2 6.2 %collective-permute-start.7 = (bf16[128,512]{1,0:T(8,128)(2,1)S(1)}, bf16[128,512]{1,0:T(8,128)(2,1)S(1)}, u32[]{:S(2)}, u32[]{:S(2)}) collective-permute-start(bf16[128,512]{1,0:T(8,128)(2,1)S(1)} %get-tuple-element.72), channel_id=1, source_target_pairs={{0,2},{1,3},{2,0},{3,1},{4,6},{5,7},{6,4},{7,5},{8,10},{9,11},{10,... | collective-permute-start | bytes 393224 | tf_op jit(solution)/shard_map/ppermute | solution.py:427
  17.0 6.7 %collective-permute-start.8 = (bf16[128,512]{1,0:T(8,128)(2,1)S(1)}, bf16[128,512]{1,0:T(8,128)(2,1)S(1)}, u32[]{:S(2)}, u32[]{:S(2)}) collective-permute-start(bf16[128,512]{1,0:T(8,128)(2,1)S(1)} %get-tuple-element.73), channel_id=1, source_target_pairs={{0,3},{1,2},{2,1},{3,0},{4,7},{5,6},{6,5},{7,4},{8,11},{9,10},{10,... | collective-permute-start | bytes 393224 | tf_op jit(solution)/shard_map/ppermute | solution.py:427
  19.0 9.0 %collective-permute-start.3 = (bf16[128,512]{1,0:T(8,128)(2,1)S(1)}, bf16[128,512]{1,0:T(8,128)(2,1)S(1)}, u32[]{:S(2)}, u32[]{:S(2)}) collective-permute-start(bf16[128,512]{1,0:T(8,128)(2,1)S(1)} %get-tuple-element.67), channel_id=1, source_target_pairs={{0,1},{1,0},{2,3},{3,2},{4,5},{5,4},{6,7},{7,6},{8,9},{9,8},{10,11... | collective-permute-start | bytes 393224 | tf_op jit(solution)/shard_map/ppermute | solution.py:427
  19.5 8.6 %collective-permute-start.4 = (bf16[128,512]{1,0:T(8,128)(2,1)S(1)}, bf16[128,512]{1,0:T(8,128)(2,1)S(1)}, u32[]{:S(2)}, u32[]{:S(2)}) collective-permute-start(bf16[128,512]{1,0:T(8,128)(2,1)S(1)} %get-tuple-element.68), channel_id=1, source_target_pairs={{0,2},{1,3},{2,0},{3,1},{4,6},{5,7},{6,4},{7,5},{8,10},{9,11},{10,... | collective-permute-start | bytes 393224 | tf_op jit(solution)/shard_map/ppermute | solution.py:427
  21.3 7.2 %collective-permute-start.5 = (bf16[128,512]{1,0:T(8,128)(2,1)S(1)}, bf16[128,512]{1,0:T(8,128)(2,1)S(1)}, u32[]{:S(2)}, u32[]{:S(2)}) collective-permute-start(bf16[128,512]{1,0:T(8,128)(2,1)S(1)} %get-tuple-element.69), channel_id=1, source_target_pairs={{0,3},{1,2},{2,1},{3,0},{4,7},{5,6},{6,5},{7,4},{8,11},{9,10},{10,... | collective-permute-start | bytes 393224 | tf_op jit(solution)/shard_map/ppermute | solution.py:427
  29.7 2.0 %collective-permute-start.9 = (bf16[32,3584]{1,0:T(8,128)(2,1)S(1)}, bf16[32,3584]{1,0:T(8,128)(2,1)S(1)}, u32[]{:S(2)}, u32[]{:S(2)}) collective-permute-start(bf16[32,3584]{1,0:T(8,128)(2,1)S(1)} %get-tuple-element.84), channel_id=1, source_target_pairs={{0,1},{1,0},{2,3},{3,2},{4,5},{5,4},{6,7},{7,6},{8,9},{9,8},{10,11... | collective-permute-start | bytes 688136 | tf_op jit(solution)/shard_map/ppermute | solution.py:427
  31.6 1.9 %collective-permute-start.11 = (bf16[32,3584]{1,0:T(8,128)(2,1)S(1)}, bf16[32,3584]{1,0:T(8,128)(2,1)S(1)}, u32[]{:S(2)}, u32[]{:S(2)}) collective-permute-start(bf16[32,3584]{1,0:T(8,128)(2,1)S(1)} %get-tuple-element.86), channel_id=1, source_target_pairs={{0,1},{1,0},{2,3},{3,2},{4,5},{5,4},{6,7},{7,6},{8,9},{9,8},{10,11... | collective-permute-start | bytes 688136 | tf_op jit(solution)/shard_map/ppermute | solution.py:427
  31.7 6.0 %collective-permute-start.10 = (bf16[16,3584]{1,0:T(8,128)(2,1)S(1)}, bf16[16,3584]{1,0:T(8,128)(2,1)S(1)}, u32[]{:S(2)}, u32[]{:S(2)}) collective-permute-start(bf16[16,3584]{1,0:T(8,128)(2,1)S(1)} %add_convert_fusion.1), channel_id=1, source_target_pairs={{0,2},{1,3},{2,0},{3,1},{4,6},{5,7},{6,4},{7,5},{8,10},{9,11},{10,... | collective-permute-start | bytes 344072 | tf_op jit(solution)/shard_map/ppermute | solution.py:427
  33.6 5.8 %collective-permute-start.12 = (bf16[16,3584]{1,0:T(8,128)(2,1)S(1)}, bf16[16,3584]{1,0:T(8,128)(2,1)S(1)}, u32[]{:S(2)}, u32[]{:S(2)}) collective-permute-start(bf16[16,3584]{1,0:T(8,128)(2,1)S(1)} %add_convert_fusion), channel_id=1, source_target_pairs={{0,3},{1,2},{2,1},{3,0},{4,7},{5,6},{6,5},{7,4},{8,11},{9,10},{10,... | collective-permute-start | bytes 344072 | tf_op jit(solution)/shard_map/ppermute | solution.py:427

commit v5 on v4

--- a/solution.py
+++ b/solution.py
@@ -15,8 +15,8 @@
 CHUNK_HEADS = 4
 OUT_PARTS = 2
 BLOCK = 256
+K_STEP = 256
 MIB = 2**20
-W_PIECES = 2
 NEAR_LIMIT = 20
 FAR_LIMIT = 20
 PROJECT_LIMIT = 10
@@ -48,23 +48,23 @@
 
 
 def call(body, operands, in_specs, out_shape, scratch, bring, limit, flops, name, aliases=None):
-    w_out, piece_rows, pieces = bring
+    w_out, pieces = bring
     vmem, hbm = pl.BlockSpec(memory_space=pltpu.VMEM), pl.BlockSpec(memory_space=pltpu.HBM)
     n_in, n_out = len(operands), len(out_shape)
     copied = 0
     if pieces:
         operands, in_specs = [*operands, w_out], [*in_specs, hbm]
-        out_shape = [*out_shape] + [pltpu.VMEM((piece_rows, w_out.shape[1]), w_out.dtype)] * len(pieces)
+        out_shape = [*out_shape]
+        out_shape += [pltpu.VMEM((count, w_out.shape[1]), w_out.dtype) for _, count in pieces]
         scratch = [*scratch, pltpu.SemaphoreType.DMA((len(pieces),))]
-        copied = 2 * len(pieces) * piece_rows * w_out.shape[1]
+        copied = 2 * sum(count for _, count in pieces) * w_out.shape[1]
 
     def kernel(*refs):
         ins, rest = refs[: len(operands)], refs[len(operands) :]
         outs, rest = rest[: len(out_shape)], rest[len(out_shape) :]
         copies = []
         for i, piece in enumerate(pieces):
-            rows = pl.ds(piece * piece_rows, piece_rows)
-            copies.append(pltpu.make_async_copy(ins[-1].at[rows], outs[n_out + i], rest[-1].at[i]))
+            copies.append(pltpu.make_async_copy(ins[-1].at[pl.ds(*piece)], outs[n_out + i], rest[-1].at[i]))
         for copy in copies:
             copy.start()
         body(ins[:n_in], outs[:n_out], rest[: len(scratch) - bool(pieces)])
@@ -119,16 +119,16 @@
             some(i * (tasks // 2), tasks // 2)
 
 
-def near_call(paused, suffix_len, queries, suffix_t, new_latent, own, beside, units, axis_size, bring):
+def near_call(paused, suffix_len, queries, suffix_t, new_latent, own, units, axis_size, bring):
     rows, steps, heads, width = queries.shape
     tile = heads // units
     share = heads // axis_size
     per = steps * heads
 
     def body(ins, outs, _):
-        _, len_buf, q_buf, suf_buf, new_buf, own_ref, beside_ref = ins
+        _, len_buf, q_buf, suf_buf, new_buf, own_ref = ins
         qs_ref, m_ref, l_ref, acc_ref = outs
-        keys = [own_ref[...], beside_ref[...]]
+        keys = own_ref[...]
 
         def sort(r):
             by_unit = [[] for _ in range(units)]
@@ -149,7 +149,7 @@
             first = task * (BLOCK // per)
             q = [sort(first + i) for i in range(BLOCK // per)]
             both = jnp.concatenate(q, axis=0)
-            scores = [dot_nn(both, k) for k in keys]
+            scores = [dot_nn(both, keys)]
             old, new = [], []
             for i, x in enumerate(q):
                 s = dot_nn(x, suf_buf[first + i])
@@ -169,11 +169,11 @@
             weights = [jnp.exp2((s - m) * SCALE2) for s in scores]
             l = sum(jnp.sum(p, axis=1, keepdims=True) for p in weights)
             probs = [p.astype(jnp.bfloat16) for p in weights]
-            acc = dot_nt(probs[0], keys[0][:LATENT]) + dot_nt(probs[1], keys[1][:LATENT])
-            new_probs = probs[3].astype(jnp.float32)
+            acc = dot_nt(probs[0], keys[:LATENT])
+            new_probs = probs[2].astype(jnp.float32)
             for i in range(BLOCK // per):
                 here = slice(i * per, (i + 1) * per)
-                part = acc[here] + dot_nt(probs[2][here], suf_buf[first + i, :LATENT])
+                part = acc[here] + dot_nt(probs[1][here], suf_buf[first + i, :LATENT])
                 values = new_buf[first + i][:, :LATENT].astype(jnp.float32)
                 for t in range(steps):
                     part += new_probs[here, t : t + 1] * values[t : t + 1]
@@ -190,8 +190,8 @@
     f32 = jnp.float32
     return call(
         body,
-        [paused, suffix_len, queries, suffix_t, new_latent, own, beside],
-        [vmem, smem] + [vmem] * 5,
+        [paused, suffix_len, queries, suffix_t, new_latent, own],
+        [vmem, smem] + [vmem] * 4,
         [
             jax.ShapeDtypeStruct(lead + (width,), queries.dtype),
             jax.ShapeDtypeStruct(lead + (128,), f32),
@@ -201,7 +201,7 @@
         [],
         bring,
         NEAR_LIMIT,
-        4 * rows * per * 1100 * 768,
+        rows * per * 1100 * 768,
         "near_attention",
     )
 
@@ -236,8 +236,8 @@
     in_turn(size * blocks, score, finish, looped)
 
 
-def middle_call(queries, state, keys, bring):
-    units, pairs, tile, _ = queries.shape
+def middle_call(units, queries, state, keys, bring):
+    _, pairs, tile, _ = queries.shape
 
     def body(ins, outs, _):
         q_ref, m_ref, l_ref, acc_ref, *key_refs = ins
@@ -249,17 +249,17 @@
             l_out[here] = jnp.broadcast_to(l, (BLOCK, 128)).reshape(lead + (128,))
             acc_out[here] = acc.reshape(lead + (LATENT,))
 
-        merge(0, units, [k[...] for k in key_refs], q_ref, m_ref, l_ref, acc_ref, store, True)
+        merge(0, units, [k[...] for k in key_refs], q_ref, m_ref, l_ref, acc_ref, store, bool(bring[1]))
 
     operands = [queries, *state, *keys]
     return call(
         body,
         operands,
         [pl.BlockSpec(memory_space=pltpu.VMEM)] * len(operands),
-        [jax.ShapeDtypeStruct(x.shape, x.dtype) for x in state],
+        [jax.ShapeDtypeStruct((units,) + x.shape[1:], x.dtype) for x in state],
         [],
         bring,
-        28 if bring[2] else 10,
+        28 if bring[1] else 10,
         2 * units * pairs * tile * 1100 * 256 * len(keys),
         "middle_attention",
     )
@@ -273,24 +273,31 @@
         q_ref, m_ref, l_ref, acc_ref, *key_refs = ins
         (done,) = scratch
 
+        me = lax.axis_index("roll")
+
+        def part(u):
+            for k in range(axis_size):
+                there = u * per_unit + jnp.bitwise_xor(me, k) * CHUNK_HEADS
+                for i in range(CHUNK_HEADS):
+                    at = pl.ds(pl.multiple_of((u * CHUNK_HEADS + i) * pairs, pairs), pairs)
+                    for g in range(LATENT // 128):
+                        out_refs[k][at, g * 128 : (g + 1) * 128] = done[
+                            g, pl.ds(there + i, pairs, stride=tile), :
+                        ].astype(jnp.bfloat16)
+
         def store(task, here, m, l, acc):
-            attended = acc / l
+            attended = acc * (1.0 / l)
             rows = pl.ds(task * BLOCK, BLOCK)
             for g in range(LATENT // 128):
                 done[g, rows, :] = attended[:, g * 128 : (g + 1) * 128]
+            if per_unit == BLOCK:
+                part(task)
 
         keys_now = [k[...] for k in key_refs]
-        merge(first, size, keys_now, q_ref, m_ref, l_ref, acc_ref, store, bool(bring[2]))
-        me = lax.axis_index("roll")
-        for k in range(axis_size):
-            there = jnp.bitwise_xor(me, k) * CHUNK_HEADS
+        merge(first, size, keys_now, q_ref, m_ref, l_ref, acc_ref, store, bool(bring[1]))
+        if per_unit != BLOCK:
             for u in range(size):
-                for i in range(CHUNK_HEADS):
-                    at = (u * CHUNK_HEADS + i) * pairs
-                    for g in range(LATENT // 128):
-                        out_refs[k][at : at + pairs, g * 128 : (g + 1) * 128] = done[
-                            g, pl.ds(u * per_unit + there + i, pairs, stride=tile), :
-                        ].astype(jnp.bfloat16)
+                part(u)
 
     operands = [queries, *state, *keys]
     return call(
@@ -300,7 +307,7 @@
         [jax.ShapeDtypeStruct((size * CHUNK_HEADS * pairs, LATENT), jnp.bfloat16)] * axis_size,
         [pltpu.VMEM((LATENT // 128, size * per_unit + tile, 128), jnp.float32)],
         bring,
-        FAR_LIMIT if bring[2] else 8,
+        FAR_LIMIT if bring[1] else 8,
         2 * size * per_unit * 1100 * 256 * len(keys),
         "far_attention",
     )
@@ -309,8 +316,7 @@
 def project(first_head, heads, pieces, acc, w_uv, w_pieces, bring, kept=None, first_col=0, cols=None):
     pairs = pieces[0].shape[0] // heads
     total_rows = len(pieces) * pairs
-    piece_rows, width = w_pieces[0].shape
-    cols = width if cols is None else cols
+    cols = w_pieces[0].shape[1] if cols is None else cols
     block = next(b for b in (1792, 1024, 896, 512, 128) if cols % b == 0)
 
     def body(ins, outs, _):
@@ -327,10 +333,12 @@
         def block_of(b):
             here = pl.ds(b * block, block)
             there = pl.ds(first_col + b * block, block)
-            total = sum(
-                dot_nn(head_out[:, i * piece_rows : (i + 1) * piece_rows], w_ref[:, there])
-                for i, w_ref in enumerate(w_refs)
-            )
+            total, at = 0.0, 0
+            for w_ref in w_refs:
+                for row in range(0, w_ref.shape[0], K_STEP):
+                    rows = slice(row, row + K_STEP)
+                    total += dot_nn(head_out[:, at : at + K_STEP], w_ref[rows, there])
+                    at += K_STEP
             if acc_ref is not None:
                 total += acc_ref[:, there]
             if kept is None:
@@ -344,7 +352,7 @@
                 ].astype(jnp.bfloat16)
                 at[side] += 1
 
-        if bring[2]:
+        if bring[1]:
             pl.loop(0, cols // block)(block_of)
         else:
             for b in range(cols // block):
@@ -362,38 +370,41 @@
         out_shape,
         [],
         bring,
-        PROJECT_LIMIT if bring[2] else 8,
+        PROJECT_LIMIT if bring[1] else 8,
         8 * total_rows * heads * w_uv.shape[2] * cols,
         "project",
         {len(pieces): 0} if acc is not None and kept is None else {},
     )
 
 
-def last_sums(rows, steps, width, parts):
+def last_sums(shape, first_col, terms, so_far):
+    rows, steps, _ = shape
     pairs = rows * steps
-    flat = [x for part in parts for x in part]
-    cols = width // len(parts)
+    cols = terms[0][0].shape[1]
 
     def kernel(*refs):
-        refs, out_ref = list(refs[:-1]), refs[-1]
-        for i, part in enumerate(parts):
-            total = None
-            for _, first in part:
-                x = refs.pop(0)[first : first + pairs, :].astype(jnp.float32)
-                total = x if total is None else total + x
-            out_ref[:, :, i * cols : (i + 1) * cols] = total.astype(jnp.bfloat16).reshape(
-                rows, steps, cols
-            )
-
-    vmem = pl.BlockSpec(memory_space=pltpu.VMEM)
+        out_ref, buf, sem = refs[-3:]
+        total = None
+        for ref, (_, first) in zip(refs, terms):
+            x = ref[first : first + pairs, :].astype(jnp.float32)
+            total = x if total is None else total + x
+        buf[...] = total.astype(jnp.bfloat16).reshape(rows, steps, cols)
+        copy = pltpu.make_async_copy(buf, out_ref.at[:, :, pl.ds(first_col, cols)], sem)
+        copy.start()
+        copy.wait()
+
+    vmem, hbm = pl.BlockSpec(memory_space=pltpu.VMEM), pl.BlockSpec(memory_space=pltpu.HBM)
+    held = [] if so_far is None else [so_far]
     return pl.pallas_call(
         kernel,
-        in_specs=[vmem] * len(flat),
-        out_specs=vmem,
-        out_shape=jax.ShapeDtypeStruct((rows, steps, width), jnp.bfloat16),
+        in_specs=[vmem] * len(terms) + [hbm] * len(held),
+        out_specs=hbm,
+        out_shape=jax.ShapeDtypeStruct(shape, jnp.bfloat16),
+        scratch_shapes=[pltpu.VMEM((rows, steps, cols), jnp.bfloat16), pltpu.SemaphoreType.DMA],
+        input_output_aliases={len(terms): 0} if held else {},
         compiler_params=pltpu.CompilerParams(vmem_limit_bytes=8 * MIB),
         name="last_sums",
-    )(*[x for x, _ in flat])
+    )(*[x for x, _ in terms], *held)
 
 
 def on_device(prefix_latent, suffix_latent, suffix_len, new_latent, queries, w_uv, w_out):
@@ -404,19 +415,20 @@
     share = heads // n
     units = share // CHUNK_HEADS
     chunks = [(0, units // 2), (units // 2, units - units // 2)] if units > 1 else [(0, 1)]
-    piece_rows = CHUNK_HEADS * w_uv.shape[2] // W_PIECES
-    n_pieces = units * W_PIECES
-    half = n_pieces // 2
-    brings = {"near": list(range(half))}
+    depth = w_out.shape[0]
+    half, eighth = depth // 2, depth // 8
     if len(chunks) > 1:
-        brings["far", 1] = list(range(half, half + half // 4))
-        brings["project", 0] = list(range(half + half // 4, n_pieces))
+        brings = {
+            "near": [(0, half - eighth)],
+            ("far", 1): [(half - eighth, eighth)],
+            ("project", 0): [(half, depth - half)],
+        }
     else:
-        brings["middle"] = list(range(half, n_pieces))
+        brings = {"near": [(0, half)], "middle": [(half, depth - half)]}
     held = {}
 
     def bring(who):
-        return (w_out, piece_rows, brings.get(who, []))
+        return (w_out, brings.get(who, []))
 
     def keep(who, result):
         out, brought = result
@@ -439,7 +451,6 @@
             jnp.swapaxes(suffix_latent, 1, 2),
             new_latent,
             own,
-            beside,
             units,
             n,
             bring("near"),
@@ -447,11 +458,16 @@
     )
     *across, m = lax.optimization_barrier((*across, m))
     forwarded = [swap(x, 1) for x in across]
-    state = keep("middle", middle_call(queries, (m, l, acc), across, bring("middle")))
+    state = (m, l, acc)
+    middle = keep("middle", middle_call(chunks[0][1], queries, state, [beside] + across, bring("middle")))
     got = []
     for c, (first, size) in enumerate(chunks):
         who = ("far", c)
-        mine = keep(who, far_call(first, size, queries, state, forwarded, n, bring(who)))
+        if c == 0:
+            result = far_call(first, size, queries, middle, forwarded, n, bring(who))
+        else:
+            result = far_call(first, size, queries, state, [beside] + across + forwarded, n, bring(who))
+        mine = keep(who, result)
         *mine, queries = lax.optimization_barrier((*mine, queries))
         there = [mine[0]] + [None] * (n - 1)
         for k in [*range(2, n), 1]:
@@ -460,7 +476,9 @@
     acc = None
 
     def pieces_of(first, size):
-        return [held[i] for i in range(first * W_PIECES, (first + size) * W_PIECES)]
+        unit_rows = depth // units
+        first, end = first * unit_rows, (first + size) * unit_rows
+        return [held[piece] for piece in sorted(held) if first <= piece[0] < end]
 
     for c, (first, size) in enumerate(chunks[:-1]):
         who = ("project", c)
@@ -505,7 +523,10 @@
             both = piece(stay, i + 1) + piece(recv, left.index(k ^ 1))
             terms.append((swap(both.astype(jnp.bfloat16), k), 0))
         parts.append(terms)
-    return last_sums(rows, steps, width, parts)
+    out = None
+    for part, terms in enumerate(parts):
+        out = last_sums((rows, steps, width), part * cols, terms, out)
+    return out
 
 
 def solution(mesh):

time: 40.4 us -> 39.5 us (0.978)
  waiting for transfers between devices: 7.83 us -> 6.51 us
  Pallas kernels: 18.5 us -> 19.4 us
  starting transfers between devices: 11.3 us -> 10.7 us
    ppermute x13, waiting for transfers between devices: 7.83 us -> 6.51 us  [swap(): return lax.ppermute(x, 'roll', [(i, i ^ k) for i in range(n)])]
    pallas_call x1 -> x2, Pallas kernels: 0.8 us -> 1.43 us  [last_sums(): pl.pallas_call(kernel, in_specs=[vmem] * len(terms) + [hbm] * len(held),...]
    ppermute x13, starting transfers between devices: 11.3 us -> 10.7 us  [swap(): return lax.ppermute(x, 'roll', [(i, i ^ k) for i in range(n)])]
  transfers between devices with their start and end apart: 13 -> 13, of which waited for: 6 -> 6; matrix products, arithmetic and copies ran while one was open for 0% -> 0% of each run, Pallas kernels for 38% -> 41%
where the time goes in v5:
time: 39.5 us; the launch traced here: 39.2 us
  Pallas kernels  19.4 us (49%)
  starting transfers between devices  10.7 us (27%)
  waiting for transfers between devices  6.51 us (16%)
  local copies, waits for them, and re-layouts  2.38 us (6%)
    pallas_call x7, Pallas kernels, call(): pl.pallas_call(kernel, in_specs=in_specs, out_specs=[vmem] * len(out_shap...  18 us
    ppermute x13, starting transfers between devices, swap(): return lax.ppermute(x, 'roll', [(i, i ^ k) for i in range(n)])  10.7 us
    ppermute x13, waiting for transfers between devices, swap(): return lax.ppermute(x, 'roll', [(i, i ^ k) for i in range(n)])  6.51 us
    unnamed x12, local copies, waits for them, and re-layouts  2.38 us
    pallas_call x2, Pallas kernels, last_sums(): pl.pallas_call(kernel, in_specs=[vmem] * len(terms) + [hbm] * len(held),...  1.43 us
  transfers between devices with their start and end apart: 13, of which 6 were waited for; matrix products, arithmetic and copies ran while one was open for 0% of the time, Pallas kernels for 41%

profile of v5, /device:TPU:0, one launch (start us, length us, event | category | flops | bytes accessed | tf_op | source)
XLA Modules:
  0.0 39.2 jit_solution(17335575656637027652)
XLA Ops:
  0.0 1.1 %copy-done.5 = f32[256,576]{0,1:T(8,128)S(1)} copy-done((f32[256,576]{0,1:T(8,128)S(1)}, f32[256,576]{0,1:T(8,128)}, u32[]{:S(2)}) %copy-start.5) | copy-done | bytes 589848
  1.1 3.0 %collective-permute-start = (bf16[576,256]{1,0:T(8,128)(2,1)S(1)}, bf16[576,256]{1,0:T(8,128)(2,1)S(1)}, u32[]{:S(2)}, u32[]{:S(2)}) collective-permute-start(bf16[576,256]{1,0:T(8,128)(2,1)S(1)} %convert_bitcast_fusion.refs_5_), channel_id=1, source_target_pairs={{0,2},{1,3},{2,0},{3,1},{4,6},{5,7},{6,4},{7,5},{8,10},{9,11},{10,... | collective-permute-start | bytes 884744 | tf_op jit(solution)/shard_map/ppermute | solution.py:439
  4.1 1.3 %copy-done.2 = bf16[8,2,64,576]{3,2,1,0:T(8,128)(2,1)S(1)} copy-done((bf16[8,2,64,576]{3,2,1,0:T(8,128)(2,1)S(1)}, bf16[8,2,64,576]{3,2,1,0:T(8,128)(2,1)}, u32[]{:S(2)}) %copy-start.2) | copy-done | bytes 1179672
  5.4 4.7 %near_attention.1 = (bf16[4,16,16,576]{3,2,1,0:T(8,128)(2,1)S(1)}, f32[4,16,16,128]{3,2,1,0:T(8,128)S(1)}, f32[4,16,16,128]{3,2,1,0:T(8,128)S(1)}, f32[4,16,16,512]{3,2,1,0:T(8,128)S(1)}, bf16[768,7168]{1,0:T(8,128)(2,1)S(1)}) custom-call(f32[8,128]{1,0:T(8,128)S(1)} %pause.1.refs_0_, s32[8]{0:T(128)S(1)} %copy-done.4, ...), custom_call_target="tpu_custom_call" | custom-call | flops 865075200 | bytes 15204352 | tf_op jit(solution)/shard_map/near_attention/pallas_call | solution.py:74
  10.1 1.0 %collective-permute-done.refs_5_ = bf16[576,256]{1,0:T(8,128)(2,1)S(1)} collective-permute-done((bf16[576,256]{1,0:T(8,128)(2,1)S(1)}, bf16[576,256]{1,0:T(8,128)(2,1)S(1)}, u32[]{:S(2)}, u32[]{:S(2)}) %collective-permute-start) | collective-permute-done | bytes 294944 | tf_op jit(solution)/shard_map/ppermute | solution.py:439
  11.1 1.3 %middle_attention.1 = (f32[2,16,16,128]{3,2,1,0:T(8,128)S(1)}, f32[2,16,16,128]{3,2,1,0:T(8,128)S(1)}, f32[2,16,16,512]{3,2,1,0:T(8,128)S(1)}) custom-call(bf16[4,16,16,576]{3,2,1,0:T(8,128)(2,1)S(1)} %get-tuple-element.56.refs_0_, f32[4,16,16,128]{3,2,1,0:T(8,128)S(1)} %get-tuple-element.45.refs_1_, f32[4,16,16,128]{3,2,1,0:T(8,128)S(1)} %get-tuple-element.46.refs_2_, ...), custom_call_target="tpu_custom_call" | custom-call | flops 576716800 | bytes 4194304 | tf_op jit(solution)/shard_map/middle_attention/pallas_call | solution.py:74
  12.4 0.3 collective-permute-done.2.refs_4_.refs_6_
  12.7 1.3 %far_attention.2 = (bf16[128,512]{1,0:T(8,128)(2,1)S(1)}, bf16[128,512]{1,0:T(8,128)(2,1)S(1)}, bf16[128,512]{1,0:T(8,128)(2,1)S(1)}, bf16[128,512]{1,0:T(8,128)(2,1)S(1)}) custom-call(bf16[4,16,16,576]{3,2,1,0:T(8,128)(2,1)S(1)} %get-tuple-element.56.refs_0_, f32[2,16,16,128]{3,2,1,0:T(8,128)S(1)} %get-tuple-element.49.refs_1_, ...), custom_call_target="tpu_custom_call" | custom-call | flops 288358400 | bytes 4194304 | tf_op jit(solution)/shard_map/far_attention/pallas_call | solution.py:74
  14.2 1.7 %collective-permute-start.7 = (bf16[128,512]{1,0:T(8,128)(2,1)S(1)}, bf16[128,512]{1,0:T(8,128)(2,1)S(1)}, u32[]{:S(2)}, u32[]{:S(2)}) collective-permute-start(bf16[128,512]{1,0:T(8,128)(2,1)S(1)} %get-tuple-element.67), channel_id=1, source_target_pairs={{0,2},{1,3},{2,0},{3,1},{4,6},{5,7},{6,4},{7,5},{8,10},{9,11},{10,... | collective-permute-start | bytes 393224 | tf_op jit(solution)/shard_map/ppermute | solution.py:439
  16.0 3.1 %far_attention.3 = (bf16[128,512]{1,0:T(8,128)(2,1)S(1)}, bf16[128,512]{1,0:T(8,128)(2,1)S(1)}, bf16[128,512]{1,0:T(8,128)(2,1)S(1)}, bf16[128,512]{1,0:T(8,128)(2,1)S(1)}, bf16[256,7168]{1,0:T(8,128)(2,1)S(1)}) custom-call(bf16[4,16,16,576]{3,2,1,0:T(8,128)(2,1)S(1)} %get-tuple-element.56.refs_0_, f32[4,16,16,128]{3,2,1,0:T(8,128)S(1)} %get-tuple-element.45.refs_1_, ...), custom_call_target="tpu_custom_call" | custom-call | flops 865075200 | bytes 7864320 | tf_op jit(solution)/shard_map/far_attention/pallas_call | solution.py:74
  19.1 0.5 %collective-permute-start.3 = (bf16[128,512]{1,0:T(8,128)(2,1)S(1)}, bf16[128,512]{1,0:T(8,128)(2,1)S(1)}, u32[]{:S(2)}, u32[]{:S(2)}) collective-permute-start(bf16[128,512]{1,0:T(8,128)(2,1)S(1)} %get-tuple-element.62), channel_id=1, source_target_pairs={{0,1},{1,0},{2,3},{3,2},{4,5},{5,4},{6,7},{7,6},{8,9},{9,8},{10,11... | collective-permute-start | bytes 393224 | tf_op jit(solution)/shard_map/ppermute | solution.py:439
  19.6 1.7 %collective-permute-start.4 = (bf16[128,512]{1,0:T(8,128)(2,1)S(1)}, bf16[128,512]{1,0:T(8,128)(2,1)S(1)}, u32[]{:S(2)}, u32[]{:S(2)}) collective-permute-start(bf16[128,512]{1,0:T(8,128)(2,1)S(1)} %get-tuple-element.63), channel_id=1, source_target_pairs={{0,2},{1,3},{2,0},{3,1},{4,6},{5,7},{6,4},{7,5},{8,10},{9,11},{10,... | collective-permute-start | bytes 393224 | tf_op jit(solution)/shard_map/ppermute | solution.py:439
  21.3 1.2 %collective-permute-done.8.refs_3_ = bf16[128,512]{1,0:T(8,128)(2,1)S(1)} collective-permute-done((bf16[128,512]{1,0:T(8,128)(2,1)S(1)}, bf16[128,512]{1,0:T(8,128)(2,1)S(1)}, u32[]{:S(2)}, u32[]{:S(2)}) %collective-permute-start.8) | collective-permute-done | bytes 131104 | tf_op jit(solution)/shard_map/ppermute | solution.py:439
  22.5 5.2 %project.3 = (f32[64,7168]{1,0:T(8,128)S(1)}, bf16[1024,7168]{1,0:T(8,128)(2,1)S(1)}) custom-call(bf16[128,512]{1,0:T(8,128)(2,1)S(1)} %get-tuple-element.65.refs_0_, bf16[128,512]{1,0:T(8,128)(2,1)S(1)} %collective-permute-done.6.refs_1_, bf16[128,512]{1,0:T(8,128)(2,1)S(1)} %collective-permute-done.7.refs_2_, ...), custom_call_target="tpu_custom_call" | custom-call | flops 3758096384 | bytes 18874368 | tf_op jit(solution)/shard_map/project/pallas_call | solution.py:74
  27.9 1.3 %project.5 = (bf16[32,3584]{1,0:T(8,128)(2,1)S(1)}, bf16[32,3584]{1,0:T(8,128)(2,1)S(1)}) custom-call(bf16[128,512]{1,0:T(8,128)(2,1)S(1)} %get-tuple-element.61.refs_0_, bf16[128,512]{1,0:T(8,128)(2,1)S(1)} %collective-permute-done.3.refs_1_, bf16[128,512]{1,0:T(8,128)(2,1)S(1)} %collective-permute-done.4.refs_2_, ...), custom_call_target="tpu_custom_call" | custom-call | flops 1879048192 | bytes 4194304 | tf_op jit(solution)/shard_map/project/pallas_call | solution.py:74
  29.2 0.4 collective-permute-start.11
  29.6 1.3 %project.4 = (bf16[32,3584]{1,0:T(8,128)(2,1)S(1)}, bf16[32,3584]{1,0:T(8,128)(2,1)S(1)}) custom-call(bf16[128,512]{1,0:T(8,128)(2,1)S(1)} %get-tuple-element.61.refs_0_, bf16[128,512]{1,0:T(8,128)(2,1)S(1)} %collective-permute-done.3.refs_1_, bf16[128,512]{1,0:T(8,128)(2,1)S(1)} %collective-permute-done.4.refs_2_, ...), custom_call_target="tpu_custom_call" | custom-call | flops 1879048192 | bytes 4194304 | tf_op jit(solution)/shard_map/project/pallas_call | solution.py:74
  30.9 0.3 collective-permute-start.9
  31.2 1.8 %collective-permute-start.12 = (bf16[16,3584]{1,0:T(8,128)(2,1)S(1)}, bf16[16,3584]{1,0:T(8,128)(2,1)S(1)}, u32[]{:S(2)}, u32[]{:S(2)}) collective-permute-start(bf16[16,3584]{1,0:T(8,128)(2,1)S(1)} %add_convert_fusion), channel_id=1, source_target_pairs={{0,2},{1,3},{2,0},{3,1},{4,6},{5,7},{6,4},{7,5},{8,10},{9,11},{10,... | collective-permute-start | bytes 344072 | tf_op jit(solution)/shard_map/ppermute | solution.py:439
  33.0 1.1 %collective-permute-start.10 = (bf16[16,3584]{1,0:T(8,128)(2,1)S(1)}, bf16[16,3584]{1,0:T(8,128)(2,1)S(1)}, u32[]{:S(2)}, u32[]{:S(2)}) collective-permute-start(bf16[16,3584]{1,0:T(8,128)(2,1)S(1)} %add_convert_fusion.1), channel_id=1, source_target_pairs={{0,3},{1,2},{2,1},{3,0},{4,7},{5,6},{6,5},{7,4},{8,11},{9,10},{10,... | collective-permute-start | bytes 344072 | tf_op jit(solution)/shard_map/ppermute | solution.py:439
  34.0 3.1 %collective-permute-done.12.refs_2_ = bf16[16,3584]{1,0:T(8,128)(2,1)S(1)} collective-permute-done((bf16[16,3584]{1,0:T(8,128)(2,1)S(1)}, bf16[16,3584]{1,0:T(8,128)(2,1)S(1)}, u32[]{:S(2)}, u32[]{:S(2)}) %collective-permute-start.12) | collective-permute-done | bytes 114720 | tf_op jit(solution)/shard_map/ppermute | solution.py:439
  37.1 0.7 %last_sums.2.refs_3_ = bf16[8,2,7168]{2,1,0:T(2,128)(2,1)} custom-call(bf16[32,3584]{1,0:T(8,128)(2,1)S(1)} %get-tuple-element.75.refs_0_, bf16[32,3584]{1,0:T(8,128)(2,1)S(1)} %collective-permute-done.11.refs_1_, bf16[16,3584]{1,0:T(8,128)(2,1)S(1)} %collective-permute-done.12.refs_2_), custom_call_target="tpu_custom_call" | custom-call | tf_op jit(solution)/shard_map/last_sums/pallas_call | solution.py:398
  37.9 0.7 %collective-permute-done.10.refs_2_ = bf16[16,3584]{1,0:T(8,128)(2,1)S(1)} collective-permute-done((bf16[16,3584]{1,0:T(8,128)(2,1)S(1)}, bf16[16,3584]{1,0:T(8,128)(2,1)S(1)}, u32[]{:S(2)}, u32[]{:S(2)}) %collective-permute-start.10) | collective-permute-done | bytes 114720 | tf_op jit(solution)/shard_map/ppermute | solution.py:439
  38.5 0.7 %last_sums.3 = bf16[8,2,7168]{2,1,0:T(2,128)(2,1)} custom-call(bf16[32,3584]{1,0:T(8,128)(2,1)S(1)} %get-tuple-element.73.refs_0_, bf16[32,3584]{1,0:T(8,128)(2,1)S(1)} %collective-permute-done.9.refs_1_, bf16[16,3584]{1,0:T(8,128)(2,1)S(1)} %collective-permute-done.10.refs_2_, bf16[8,2,7168]{2,1,0:T(2,128)(2,1)} %last_sums.2.refs_3_), custom_call_target="tpu_custom_call", output_to_operand_aliasing={{}: (3, {})} | custom-call | tf_op jit(solution)/shard_map/last_sums/pallas_call | solution.py:398
  (27 shorter events, 0.7 us)
Async XLA Ops:
  0.0 1.1 %copy-start.5 = (f32[256,576]{0,1:T(8,128)S(1)}, f32[256,576]{0,1:T(8,128)}, u32[]{:S(2)}) copy-start(f32[256,576]{0,1:T(8,128)} %param.7) | copy-start | bytes 1769476
  0.0 4.1 %copy-start.3 = (bf16[8,2,576]{2,1,0:T(2,128)(2,1)S(1)}, bf16[8,2,576]{2,1,0:T(2,128)(2,1)}, u32[]{:S(2)}) copy-start(bf16[8,2,576]{2,1,0:T(2,128)(2,1)} %refs_4_.2) | copy-start | bytes 55300
  0.0 4.1 %copy-start.4 = (s32[8]{0:T(128)S(1)}, s32[8]{0:T(128)}, u32[]{:S(2)}) copy-start(s32[8]{0:T(128)} %refs_1_.1) | copy-start | bytes 100
  0.0 4.1 %copy-start.1 = (bf16[8,256,576]{1,2,0:T(8,128)(2,1)S(1)}, bf16[8,256,576]{1,2,0:T(8,128)(2,1)}, u32[]{:S(2)}) copy-start(bf16[8,256,576]{1,2,0:T(8,128)(2,1)} %param.8) | copy-start | bytes 7077892
  1.1 10.0 %collective-permute-start = (bf16[576,256]{1,0:T(8,128)(2,1)S(1)}, bf16[576,256]{1,0:T(8,128)(2,1)S(1)}, u32[]{:S(2)}, u32[]{:S(2)}) collective-permute-start(bf16[576,256]{1,0:T(8,128)(2,1)S(1)} %convert_bitcast_fusion.refs_5_), channel_id=1, source_target_pairs={{0,2},{1,3},{2,0},{3,1},{4,6},{5,7},{6,4},{7,5},{8,10},{9,11},{10,... | collective-permute-start | bytes 884744 | tf_op jit(solution)/shard_map/ppermute | solution.py:439
  4.1 7.0 %collective-permute-start.1 = (bf16[576,256]{1,0:T(8,128)(2,1)S(1)}, bf16[576,256]{1,0:T(8,128)(2,1)S(1)}, u32[]{:S(2)}, u32[]{:S(2)}) collective-permute-start(bf16[576,256]{1,0:T(8,128)(2,1)S(1)} %convert_bitcast_fusion.refs_5_), channel_id=1, source_target_pairs={{0,1},{1,0},{2,3},{3,2},{4,5},{5,4},{6,7},{7,6},{8,9},{9,8},{10,11... | collective-permute-start | bytes 884744 | tf_op jit(solution)/shard_map/ppermute | solution.py:439
  4.1 1.3 %copy-start.2 = (bf16[8,2,64,576]{3,2,1,0:T(8,128)(2,1)S(1)}, bf16[8,2,64,576]{3,2,1,0:T(8,128)(2,1)}, u32[]{:S(2)}) copy-start(bf16[8,2,64,576]{3,2,1,0:T(8,128)(2,1)} %refs_2_.1) | copy-start | bytes 3538948
  11.1 1.6 %collective-permute-start.2 = (bf16[576,256]{1,0:T(8,128)(2,1)S(1)}, bf16[576,256]{1,0:T(8,128)(2,1)S(1)}, u32[]{:S(2)}, u32[]{:S(2)}) collective-permute-start(bf16[576,256]{1,0:T(8,128)(2,1)S(1)} %collective-permute-done.refs_5_), channel_id=1, source_target_pairs={{0,1},{1,0},{2,3},{3,2},{4,5},{5,4},{6,7},{7,6},{8,9},{9,8},{10,11... | collective-permute-start | bytes 884744 | tf_op jit(solution)/shard_map/ppermute | solution.py:439
  14.0 8.5 %copy-start = (bf16[16,512,128]{2,1,0:T(8,128)(2,1)S(1)}, bf16[16,512,128]{2,1,0:T(8,128)(2,1)}, u32[]{:S(2)}) copy-start(bf16[16,512,128]{2,1,0:T(8,128)(2,1)} %refs_5_.3) | copy-start | bytes 6291460
  14.0 7.3 %collective-permute-start.6 = (bf16[128,512]{1,0:T(8,128)(2,1)S(1)}, bf16[128,512]{1,0:T(8,128)(2,1)S(1)}, u32[]{:S(2)}, u32[]{:S(2)}) collective-permute-start(bf16[128,512]{1,0:T(8,128)(2,1)S(1)} %get-tuple-element.66), channel_id=1, source_target_pairs={{0,1},{1,0},{2,3},{3,2},{4,5},{5,4},{6,7},{7,6},{8,9},{9,8},{10,11... | collective-permute-start | bytes 393224 | tf_op jit(solution)/shard_map/ppermute | solution.py:439
  14.2 7.1 %collective-permute-start.7 = (bf16[128,512]{1,0:T(8,128)(2,1)S(1)}, bf16[128,512]{1,0:T(8,128)(2,1)S(1)}, u32[]{:S(2)}, u32[]{:S(2)}) collective-permute-start(bf16[128,512]{1,0:T(8,128)(2,1)S(1)} %get-tuple-element.67), channel_id=1, source_target_pairs={{0,2},{1,3},{2,0},{3,1},{4,6},{5,7},{6,4},{7,5},{8,10},{9,11},{10,... | collective-permute-start | bytes 393224 | tf_op jit(solution)/shard_map/ppermute | solution.py:439
  16.0 6.5 %collective-permute-start.8 = (bf16[128,512]{1,0:T(8,128)(2,1)S(1)}, bf16[128,512]{1,0:T(8,128)(2,1)S(1)}, u32[]{:S(2)}, u32[]{:S(2)}) collective-permute-start(bf16[128,512]{1,0:T(8,128)(2,1)S(1)} %get-tuple-element.68), channel_id=1, source_target_pairs={{0,3},{1,2},{2,1},{3,0},{4,7},{5,6},{6,5},{7,4},{8,11},{9,10},{10,... | collective-permute-start | bytes 393224 | tf_op jit(solution)/shard_map/ppermute | solution.py:439
  19.1 8.6 %collective-permute-start.3 = (bf16[128,512]{1,0:T(8,128)(2,1)S(1)}, bf16[128,512]{1,0:T(8,128)(2,1)S(1)}, u32[]{:S(2)}, u32[]{:S(2)}) collective-permute-start(bf16[128,512]{1,0:T(8,128)(2,1)S(1)} %get-tuple-element.62), channel_id=1, source_target_pairs={{0,1},{1,0},{2,3},{3,2},{4,5},{5,4},{6,7},{7,6},{8,9},{9,8},{10,11... | collective-permute-start | bytes 393224 | tf_op jit(solution)/shard_map/ppermute | solution.py:439
  19.6 8.1 %collective-permute-start.4 = (bf16[128,512]{1,0:T(8,128)(2,1)S(1)}, bf16[128,512]{1,0:T(8,128)(2,1)S(1)}, u32[]{:S(2)}, u32[]{:S(2)}) collective-permute-start(bf16[128,512]{1,0:T(8,128)(2,1)S(1)} %get-tuple-element.63), channel_id=1, source_target_pairs={{0,2},{1,3},{2,0},{3,1},{4,6},{5,7},{6,4},{7,5},{8,10},{9,11},{10,... | collective-permute-start | bytes 393224 | tf_op jit(solution)/shard_map/ppermute | solution.py:439
  21.3 6.6 %collective-permute-start.5 = (bf16[128,512]{1,0:T(8,128)(2,1)S(1)}, bf16[128,512]{1,0:T(8,128)(2,1)S(1)}, u32[]{:S(2)}, u32[]{:S(2)}) collective-permute-start(bf16[128,512]{1,0:T(8,128)(2,1)S(1)} %get-tuple-element.64), channel_id=1, source_target_pairs={{0,3},{1,2},{2,1},{3,0},{4,7},{5,6},{6,5},{7,4},{8,11},{9,10},{10,... | collective-permute-start | bytes 393224 | tf_op jit(solution)/shard_map/ppermute | solution.py:439
  29.2 1.9 %collective-permute-start.11 = (bf16[32,3584]{1,0:T(8,128)(2,1)S(1)}, bf16[32,3584]{1,0:T(8,128)(2,1)S(1)}, u32[]{:S(2)}, u32[]{:S(2)}) collective-permute-start(bf16[32,3584]{1,0:T(8,128)(2,1)S(1)} %get-tuple-element.76), channel_id=1, source_target_pairs={{0,1},{1,0},{2,3},{3,2},{4,5},{5,4},{6,7},{7,6},{8,9},{9,8},{10,11... | collective-permute-start | bytes 688136 | tf_op jit(solution)/shard_map/ppermute | solution.py:439
  30.9 2.1 %collective-permute-start.9 = (bf16[32,3584]{1,0:T(8,128)(2,1)S(1)}, bf16[32,3584]{1,0:T(8,128)(2,1)S(1)}, u32[]{:S(2)}, u32[]{:S(2)}) collective-permute-start(bf16[32,3584]{1,0:T(8,128)(2,1)S(1)} %get-tuple-element.74), channel_id=1, source_target_pairs={{0,1},{1,0},{2,3},{3,2},{4,5},{5,4},{6,7},{7,6},{8,9},{9,8},{10,11... | collective-permute-start | bytes 688136 | tf_op jit(solution)/shard_map/ppermute | solution.py:439
  31.2 6.0 %collective-permute-start.12 = (bf16[16,3584]{1,0:T(8,128)(2,1)S(1)}, bf16[16,3584]{1,0:T(8,128)(2,1)S(1)}, u32[]{:S(2)}, u32[]{:S(2)}) collective-permute-start(bf16[16,3584]{1,0:T(8,128)(2,1)S(1)} %add_convert_fusion), channel_id=1, source_target_pairs={{0,2},{1,3},{2,0},{3,1},{4,6},{5,7},{6,4},{7,5},{8,10},{9,11},{10,... | collective-permute-start | bytes 344072 | tf_op jit(solution)/shard_map/ppermute | solution.py:439
  33.0 5.5 %collective-permute-start.10 = (bf16[16,3584]{1,0:T(8,128)(2,1)S(1)}, bf16[16,3584]{1,0:T(8,128)(2,1)S(1)}, u32[]{:S(2)}, u32[]{:S(2)}) collective-permute-start(bf16[16,3584]{1,0:T(8,128)(2,1)S(1)} %add_convert_fusion.1), channel_id=1, source_target_pairs={{0,3},{1,2},{2,1},{3,0},{4,7},{5,6},{6,5},{7,4},{8,11},{9,10},{10,... | collective-permute-start | bytes 344072 | tf_op jit(solution)/shard_map/ppermute | solution.py:439

commit v6 on v5

--- a/solution.py
+++ b/solution.py
@@ -469,10 +469,15 @@
             result = far_call(first, size, queries, state, [beside] + across + forwarded, n, bring(who))
         mine = keep(who, result)
         *mine, queries = lax.optimization_barrier((*mine, queries))
-        there = [mine[0]] + [None] * (n - 1)
+        if c == 1:
+            *mine, late = lax.optimization_barrier((*mine, late))
+            got[0][1] = swap(late, 1)
+        got.append([mine[0]] + [None] * (n - 1))
         for k in [*range(2, n), 1]:
-            there[k] = swap(mine[k], k)
-        got.append(there)
+            if k == 1 and c == 0 and len(chunks) > 1:
+                late = mine[1]
+            else:
+                got[c][k] = swap(mine[k], k)
     acc = None
 
     def pieces_of(first, size):

time: 39.5 us -> 39.2 us (level)
  transfers between devices with their start and end apart: 13 -> 13, of which waited for: 6 -> 6; matrix products, arithmetic and copies ran while one was open for 0% -> 0% of each run, Pallas kernels for 41% -> 42%
where the time goes in v6:
time: 39.2 us; the launch traced here: 39 us
  Pallas kernels  19.4 us (49%)
  starting transfers between devices  10.7 us (27%)
  waiting for transfers between devices  6.25 us (16%)
  local copies, waits for them, and re-layouts  2.38 us (6%)
    pallas_call x7, Pallas kernels, call(): pl.pallas_call(kernel, in_specs=in_specs, out_specs=[vmem] * len(out_shap...  18 us
    ppermute x13, starting transfers between devices, swap(): return lax.ppermute(x, 'roll', [(i, i ^ k) for i in range(n)])  10.7 us
    ppermute x13, waiting for transfers between devices, swap(): return lax.ppermute(x, 'roll', [(i, i ^ k) for i in range(n)])  6.25 us
    unnamed x12, local copies, waits for them, and re-layouts  2.38 us
    pallas_call x2, Pallas kernels, last_sums(): pl.pallas_call(kernel, in_specs=[vmem] * len(terms) + [hbm] * len(held),...  1.43 us
  transfers between devices with their start and end apart: 13, of which 6 were waited for; matrix products, arithmetic and copies ran while one was open for 0% of the time, Pallas kernels for 42%

profile of v6, /device:TPU:0, one launch (start us, length us, event | category | flops | bytes accessed | tf_op | source)
XLA Modules:
  0.0 39.0 jit_solution(9538077757003657895)
XLA Ops:
  0.0 1.1 %copy-done.5 = f32[256,576]{0,1:T(8,128)S(1)} copy-done((f32[256,576]{0,1:T(8,128)S(1)}, f32[256,576]{0,1:T(8,128)}, u32[]{:S(2)}) %copy-start.5) | copy-done | bytes 589848
  1.1 3.0 %collective-permute-start = (bf16[576,256]{1,0:T(8,128)(2,1)S(1)}, bf16[576,256]{1,0:T(8,128)(2,1)S(1)}, u32[]{:S(2)}, u32[]{:S(2)}) collective-permute-start(bf16[576,256]{1,0:T(8,128)(2,1)S(1)} %convert_bitcast_fusion.refs_5_), channel_id=1, source_target_pairs={{0,2},{1,3},{2,0},{3,1},{4,6},{5,7},{6,4},{7,5},{8,10},{9,11},{10,... | collective-permute-start | bytes 884744 | tf_op jit(solution)/shard_map/ppermute | solution.py:439
  4.1 1.3 %copy-done.2 = bf16[8,2,64,576]{3,2,1,0:T(8,128)(2,1)S(1)} copy-done((bf16[8,2,64,576]{3,2,1,0:T(8,128)(2,1)S(1)}, bf16[8,2,64,576]{3,2,1,0:T(8,128)(2,1)}, u32[]{:S(2)}) %copy-start.2) | copy-done | bytes 1179672
  5.4 4.7 %near_attention.1 = (bf16[4,16,16,576]{3,2,1,0:T(8,128)(2,1)S(1)}, f32[4,16,16,128]{3,2,1,0:T(8,128)S(1)}, f32[4,16,16,128]{3,2,1,0:T(8,128)S(1)}, f32[4,16,16,512]{3,2,1,0:T(8,128)S(1)}, bf16[768,7168]{1,0:T(8,128)(2,1)S(1)}) custom-call(f32[8,128]{1,0:T(8,128)S(1)} %pause.1.refs_0_, s32[8]{0:T(128)S(1)} %copy-done.4, ...), custom_call_target="tpu_custom_call" | custom-call | flops 865075200 | bytes 15204352 | tf_op jit(solution)/shard_map/near_attention/pallas_call | solution.py:74
  10.1 1.0 %collective-permute-done.refs_5_ = bf16[576,256]{1,0:T(8,128)(2,1)S(1)} collective-permute-done((bf16[576,256]{1,0:T(8,128)(2,1)S(1)}, bf16[576,256]{1,0:T(8,128)(2,1)S(1)}, u32[]{:S(2)}, u32[]{:S(2)}) %collective-permute-start) | collective-permute-done | bytes 294944 | tf_op jit(solution)/shard_map/ppermute | solution.py:439
  11.1 1.3 %middle_attention.1 = (f32[2,16,16,128]{3,2,1,0:T(8,128)S(1)}, f32[2,16,16,128]{3,2,1,0:T(8,128)S(1)}, f32[2,16,16,512]{3,2,1,0:T(8,128)S(1)}) custom-call(bf16[4,16,16,576]{3,2,1,0:T(8,128)(2,1)S(1)} %get-tuple-element.61.refs_0_, f32[4,16,16,128]{3,2,1,0:T(8,128)S(1)} %get-tuple-element.50.refs_1_, f32[4,16,16,128]{3,2,1,0:T(8,128)S(1)} %get-tuple-element.51.refs_2_, ...), custom_call_target="tpu_custom_call" | custom-call | flops 576716800 | bytes 4194304 | tf_op jit(solution)/shard_map/middle_attention/pallas_call | solution.py:74
  12.4 0.3 collective-permute-done.2.refs_4_.refs_6_
  12.7 1.3 %far_attention.2 = (bf16[128,512]{1,0:T(8,128)(2,1)S(1)}, bf16[128,512]{1,0:T(8,128)(2,1)S(1)}, bf16[128,512]{1,0:T(8,128)(2,1)S(1)}, bf16[128,512]{1,0:T(8,128)(2,1)S(1)}) custom-call(bf16[4,16,16,576]{3,2,1,0:T(8,128)(2,1)S(1)} %get-tuple-element.61.refs_0_, f32[2,16,16,128]{3,2,1,0:T(8,128)S(1)} %get-tuple-element.54.refs_1_, ...), custom_call_target="tpu_custom_call" | custom-call | flops 288358400 | bytes 4194304 | tf_op jit(solution)/shard_map/far_attention/pallas_call | solution.py:74
  14.0 1.8 %collective-permute-start.7 = (bf16[128,512]{1,0:T(8,128)(2,1)S(1)}, bf16[128,512]{1,0:T(8,128)(2,1)S(1)}, u32[]{:S(2)}, u32[]{:S(2)}) collective-permute-start(bf16[128,512]{1,0:T(8,128)(2,1)S(1)} %get-tuple-element.77), channel_id=1, source_target_pairs={{0,2},{1,3},{2,0},{3,1},{4,6},{5,7},{6,4},{7,5},{8,10},{9,11},{10,... | collective-permute-start | bytes 393224 | tf_op jit(solution)/shard_map/ppermute | solution.py:439
  15.8 3.1 %far_attention.3 = (bf16[128,512]{1,0:T(8,128)(2,1)S(1)}, bf16[128,512]{1,0:T(8,128)(2,1)S(1)}, bf16[128,512]{1,0:T(8,128)(2,1)S(1)}, bf16[128,512]{1,0:T(8,128)(2,1)S(1)}, bf16[256,7168]{1,0:T(8,128)(2,1)S(1)}) custom-call(bf16[4,16,16,576]{3,2,1,0:T(8,128)(2,1)S(1)} %get-tuple-element.61.refs_0_, f32[4,16,16,128]{3,2,1,0:T(8,128)S(1)} %get-tuple-element.50.refs_1_, ...), custom_call_target="tpu_custom_call" | custom-call | flops 865075200 | bytes 7864320 | tf_op jit(solution)/shard_map/far_attention/pallas_call | solution.py:74
  18.9 0.5 %collective-permute-start.6 = (bf16[128,512]{1,0:T(8,128)(2,1)S(1)}, bf16[128,512]{1,0:T(8,128)(2,1)S(1)}, u32[]{:S(2)}, u32[]{:S(2)}) collective-permute-start(bf16[128,512]{1,0:T(8,128)(2,1)S(1)} %get-tuple-element.76), channel_id=1, source_target_pairs={{0,1},{1,0},{2,3},{3,2},{4,5},{5,4},{6,7},{7,6},{8,9},{9,8},{10,11... | collective-permute-start | bytes 393224 | tf_op jit(solution)/shard_map/ppermute | solution.py:439
  19.5 1.7 %collective-permute-start.4 = (bf16[128,512]{1,0:T(8,128)(2,1)S(1)}, bf16[128,512]{1,0:T(8,128)(2,1)S(1)}, u32[]{:S(2)}, u32[]{:S(2)}) collective-permute-start(bf16[128,512]{1,0:T(8,128)(2,1)S(1)} %get-tuple-element.73), channel_id=1, source_target_pairs={{0,2},{1,3},{2,0},{3,1},{4,6},{5,7},{6,4},{7,5},{8,10},{9,11},{10,... | collective-permute-start | bytes 393224 | tf_op jit(solution)/shard_map/ppermute | solution.py:439
  21.2 0.5 %collective-permute-done.8.refs_3_ = bf16[128,512]{1,0:T(8,128)(2,1)S(1)} collective-permute-done((bf16[128,512]{1,0:T(8,128)(2,1)S(1)}, bf16[128,512]{1,0:T(8,128)(2,1)S(1)}, u32[]{:S(2)}, u32[]{:S(2)}) %collective-permute-start.8) | collective-permute-done | bytes 131104 | tf_op jit(solution)/shard_map/ppermute | solution.py:439
  21.7 5.2 %project.3 = (f32[64,7168]{1,0:T(8,128)S(1)}, bf16[1024,7168]{1,0:T(8,128)(2,1)S(1)}) custom-call(bf16[128,512]{1,0:T(8,128)(2,1)S(1)} %get-tuple-element.75.refs_0_, bf16[128,512]{1,0:T(8,128)(2,1)S(1)} %collective-permute-done.6.refs_1_, bf16[128,512]{1,0:T(8,128)(2,1)S(1)} %collective-permute-done.7.refs_2_, ...), custom_call_target="tpu_custom_call" | custom-call | flops 3758096384 | bytes 18874368 | tf_op jit(solution)/shard_map/project/pallas_call | solution.py:74
  26.9 0.7 %collective-permute-done.5.refs_3_ = bf16[128,512]{1,0:T(8,128)(2,1)S(1)} collective-permute-done((bf16[128,512]{1,0:T(8,128)(2,1)S(1)}, bf16[128,512]{1,0:T(8,128)(2,1)S(1)}, u32[]{:S(2)}, u32[]{:S(2)}) %collective-permute-start.5) | collective-permute-done | bytes 131104 | tf_op jit(solution)/shard_map/ppermute | solution.py:439
  27.6 1.3 %project.5 = (bf16[32,3584]{1,0:T(8,128)(2,1)S(1)}, bf16[32,3584]{1,0:T(8,128)(2,1)S(1)}) custom-call(bf16[128,512]{1,0:T(8,128)(2,1)S(1)} %get-tuple-element.71.refs_0_, bf16[128,512]{1,0:T(8,128)(2,1)S(1)} %collective-permute-done.3.refs_1_, bf16[128,512]{1,0:T(8,128)(2,1)S(1)} %collective-permute-done.4.refs_2_, ...), custom_call_target="tpu_custom_call" | custom-call | flops 1879048192 | bytes 4194304 | tf_op jit(solution)/shard_map/project/pallas_call | solution.py:74
  28.9 0.4 collective-permute-start.11
  29.3 1.3 %project.4 = (bf16[32,3584]{1,0:T(8,128)(2,1)S(1)}, bf16[32,3584]{1,0:T(8,128)(2,1)S(1)}) custom-call(bf16[128,512]{1,0:T(8,128)(2,1)S(1)} %get-tuple-element.71.refs_0_, bf16[128,512]{1,0:T(8,128)(2,1)S(1)} %collective-permute-done.3.refs_1_, bf16[128,512]{1,0:T(8,128)(2,1)S(1)} %collective-permute-done.4.refs_2_, ...), custom_call_target="tpu_custom_call" | custom-call | flops 1879048192 | bytes 4194304 | tf_op jit(solution)/shard_map/project/pallas_call | solution.py:74
  30.9 1.8 %collective-permute-start.12 = (bf16[16,3584]{1,0:T(8,128)(2,1)S(1)}, bf16[16,3584]{1,0:T(8,128)(2,1)S(1)}, u32[]{:S(2)}, u32[]{:S(2)}) collective-permute-start(bf16[16,3584]{1,0:T(8,128)(2,1)S(1)} %add_convert_fusion), channel_id=1, source_target_pairs={{0,2},{1,3},{2,0},{3,1},{4,6},{5,7},{6,4},{7,5},{8,10},{9,11},{10,... | collective-permute-start | bytes 344072 | tf_op jit(solution)/shard_map/ppermute | solution.py:439
  32.7 1.1 %collective-permute-start.10 = (bf16[16,3584]{1,0:T(8,128)(2,1)S(1)}, bf16[16,3584]{1,0:T(8,128)(2,1)S(1)}, u32[]{:S(2)}, u32[]{:S(2)}) collective-permute-start(bf16[16,3584]{1,0:T(8,128)(2,1)S(1)} %add_convert_fusion.1), channel_id=1, source_target_pairs={{0,3},{1,2},{2,1},{3,0},{4,7},{5,6},{6,5},{7,4},{8,11},{9,10},{10,... | collective-permute-start | bytes 344072 | tf_op jit(solution)/shard_map/ppermute | solution.py:439
  33.8 3.0 %collective-permute-done.12.refs_2_ = bf16[16,3584]{1,0:T(8,128)(2,1)S(1)} collective-permute-done((bf16[16,3584]{1,0:T(8,128)(2,1)S(1)}, bf16[16,3584]{1,0:T(8,128)(2,1)S(1)}, u32[]{:S(2)}, u32[]{:S(2)}) %collective-permute-start.12) | collective-permute-done | bytes 114720 | tf_op jit(solution)/shard_map/ppermute | solution.py:439
  36.7 0.7 %last_sums.2.refs_3_ = bf16[8,2,7168]{2,1,0:T(2,128)(2,1)} custom-call(bf16[32,3584]{1,0:T(8,128)(2,1)S(1)} %get-tuple-element.85.refs_0_, bf16[32,3584]{1,0:T(8,128)(2,1)S(1)} %collective-permute-done.11.refs_1_, bf16[16,3584]{1,0:T(8,128)(2,1)S(1)} %collective-permute-done.12.refs_2_), custom_call_target="tpu_custom_call" | custom-call | tf_op jit(solution)/shard_map/last_sums/pallas_call | solution.py:398
  37.5 0.8 %collective-permute-done.10.refs_2_ = bf16[16,3584]{1,0:T(8,128)(2,1)S(1)} collective-permute-done((bf16[16,3584]{1,0:T(8,128)(2,1)S(1)}, bf16[16,3584]{1,0:T(8,128)(2,1)S(1)}, u32[]{:S(2)}, u32[]{:S(2)}) %collective-permute-start.10) | collective-permute-done | bytes 114720 | tf_op jit(solution)/shard_map/ppermute | solution.py:439
  38.3 0.7 %last_sums.3 = bf16[8,2,7168]{2,1,0:T(2,128)(2,1)} custom-call(bf16[32,3584]{1,0:T(8,128)(2,1)S(1)} %get-tuple-element.83.refs_0_, bf16[32,3584]{1,0:T(8,128)(2,1)S(1)} %collective-permute-done.9.refs_1_, bf16[16,3584]{1,0:T(8,128)(2,1)S(1)} %collective-permute-done.10.refs_2_, bf16[8,2,7168]{2,1,0:T(2,128)(2,1)} %last_sums.2.refs_3_), custom_call_target="tpu_custom_call", output_to_operand_aliasing={{}: (3, {})} | custom-call | tf_op jit(solution)/shard_map/last_sums/pallas_call | solution.py:398
  (27 shorter events, 0.6 us)
Async XLA Ops:
  0.0 1.1 %copy-start.5 = (f32[256,576]{0,1:T(8,128)S(1)}, f32[256,576]{0,1:T(8,128)}, u32[]{:S(2)}) copy-start(f32[256,576]{0,1:T(8,128)} %param.7) | copy-start | bytes 1769476
  0.0 4.1 %copy-start.3 = (bf16[8,2,576]{2,1,0:T(2,128)(2,1)S(1)}, bf16[8,2,576]{2,1,0:T(2,128)(2,1)}, u32[]{:S(2)}) copy-start(bf16[8,2,576]{2,1,0:T(2,128)(2,1)} %refs_4_.2) | copy-start | bytes 55300
  0.0 4.1 %copy-start.4 = (s32[8]{0:T(128)S(1)}, s32[8]{0:T(128)}, u32[]{:S(2)}) copy-start(s32[8]{0:T(128)} %refs_1_.1) | copy-start | bytes 100
  0.0 4.1 %copy-start.1 = (bf16[8,256,576]{1,2,0:T(8,128)(2,1)S(1)}, bf16[8,256,576]{1,2,0:T(8,128)(2,1)}, u32[]{:S(2)}) copy-start(bf16[8,256,576]{1,2,0:T(8,128)(2,1)} %param.8) | copy-start | bytes 7077892
  1.1 10.0 %collective-permute-start = (bf16[576,256]{1,0:T(8,128)(2,1)S(1)}, bf16[576,256]{1,0:T(8,128)(2,1)S(1)}, u32[]{:S(2)}, u32[]{:S(2)}) collective-permute-start(bf16[576,256]{1,0:T(8,128)(2,1)S(1)} %convert_bitcast_fusion.refs_5_), channel_id=1, source_target_pairs={{0,2},{1,3},{2,0},{3,1},{4,6},{5,7},{6,4},{7,5},{8,10},{9,11},{10,... | collective-permute-start | bytes 884744 | tf_op jit(solution)/shard_map/ppermute | solution.py:439
  4.1 7.0 %collective-permute-start.1 = (bf16[576,256]{1,0:T(8,128)(2,1)S(1)}, bf16[576,256]{1,0:T(8,128)(2,1)S(1)}, u32[]{:S(2)}, u32[]{:S(2)}) collective-permute-start(bf16[576,256]{1,0:T(8,128)(2,1)S(1)} %convert_bitcast_fusion.refs_5_), channel_id=1, source_target_pairs={{0,1},{1,0},{2,3},{3,2},{4,5},{5,4},{6,7},{7,6},{8,9},{9,8},{10,11... | collective-permute-start | bytes 884744 | tf_op jit(solution)/shard_map/ppermute | solution.py:439
  4.1 1.3 %copy-start.2 = (bf16[8,2,64,576]{3,2,1,0:T(8,128)(2,1)S(1)}, bf16[8,2,64,576]{3,2,1,0:T(8,128)(2,1)}, u32[]{:S(2)}) copy-start(bf16[8,2,64,576]{3,2,1,0:T(8,128)(2,1)} %refs_2_.1) | copy-start | bytes 3538948
  11.1 1.6 %collective-permute-start.2 = (bf16[576,256]{1,0:T(8,128)(2,1)S(1)}, bf16[576,256]{1,0:T(8,128)(2,1)S(1)}, u32[]{:S(2)}, u32[]{:S(2)}) collective-permute-start(bf16[576,256]{1,0:T(8,128)(2,1)S(1)} %collective-permute-done.refs_5_), channel_id=1, source_target_pairs={{0,1},{1,0},{2,3},{3,2},{4,5},{5,4},{6,7},{7,6},{8,9},{9,8},{10,11... | collective-permute-start | bytes 884744 | tf_op jit(solution)/shard_map/ppermute | solution.py:439
  14.0 7.8 %copy-start = (bf16[16,512,128]{2,1,0:T(8,128)(2,1)S(1)}, bf16[16,512,128]{2,1,0:T(8,128)(2,1)}, u32[]{:S(2)}) copy-start(bf16[16,512,128]{2,1,0:T(8,128)(2,1)} %refs_5_.3) | copy-start | bytes 6291460
  14.0 7.2 %collective-permute-start.7 = (bf16[128,512]{1,0:T(8,128)(2,1)S(1)}, bf16[128,512]{1,0:T(8,128)(2,1)S(1)}, u32[]{:S(2)}, u32[]{:S(2)}) collective-permute-start(bf16[128,512]{1,0:T(8,128)(2,1)S(1)} %get-tuple-element.77), channel_id=1, source_target_pairs={{0,2},{1,3},{2,0},{3,1},{4,6},{5,7},{6,4},{7,5},{8,10},{9,11},{10,... | collective-permute-start | bytes 393224 | tf_op jit(solution)/shard_map/ppermute | solution.py:439
  15.8 5.9 %collective-permute-start.8 = (bf16[128,512]{1,0:T(8,128)(2,1)S(1)}, bf16[128,512]{1,0:T(8,128)(2,1)S(1)}, u32[]{:S(2)}, u32[]{:S(2)}) collective-permute-start(bf16[128,512]{1,0:T(8,128)(2,1)S(1)} %get-tuple-element.78), channel_id=1, source_target_pairs={{0,3},{1,2},{2,1},{3,0},{4,7},{5,6},{6,5},{7,4},{8,11},{9,10},{10,... | collective-permute-start | bytes 393224 | tf_op jit(solution)/shard_map/ppermute | solution.py:439
  18.9 2.8 %collective-permute-start.6 = (bf16[128,512]{1,0:T(8,128)(2,1)S(1)}, bf16[128,512]{1,0:T(8,128)(2,1)S(1)}, u32[]{:S(2)}, u32[]{:S(2)}) collective-permute-start(bf16[128,512]{1,0:T(8,128)(2,1)S(1)} %get-tuple-element.76), channel_id=1, source_target_pairs={{0,1},{1,0},{2,3},{3,2},{4,5},{5,4},{6,7},{7,6},{8,9},{9,8},{10,11... | collective-permute-start | bytes 393224 | tf_op jit(solution)/shard_map/ppermute | solution.py:439
  19.4 7.5 %collective-permute-start.3 = (bf16[128,512]{1,0:T(8,128)(2,1)S(1)}, bf16[128,512]{1,0:T(8,128)(2,1)S(1)}, u32[]{:S(2)}, u32[]{:S(2)}) collective-permute-start(bf16[128,512]{1,0:T(8,128)(2,1)S(1)} %get-tuple-element.72), channel_id=1, source_target_pairs={{0,1},{1,0},{2,3},{3,2},{4,5},{5,4},{6,7},{7,6},{8,9},{9,8},{10,11... | collective-permute-start | bytes 393224 | tf_op jit(solution)/shard_map/ppermute | solution.py:439
  19.5 7.4 %collective-permute-start.4 = (bf16[128,512]{1,0:T(8,128)(2,1)S(1)}, bf16[128,512]{1,0:T(8,128)(2,1)S(1)}, u32[]{:S(2)}, u32[]{:S(2)}) collective-permute-start(bf16[128,512]{1,0:T(8,128)(2,1)S(1)} %get-tuple-element.73), channel_id=1, source_target_pairs={{0,2},{1,3},{2,0},{3,1},{4,6},{5,7},{6,4},{7,5},{8,10},{9,11},{10,... | collective-permute-start | bytes 393224 | tf_op jit(solution)/shard_map/ppermute | solution.py:439
  21.2 6.5 %collective-permute-start.5 = (bf16[128,512]{1,0:T(8,128)(2,1)S(1)}, bf16[128,512]{1,0:T(8,128)(2,1)S(1)}, u32[]{:S(2)}, u32[]{:S(2)}) collective-permute-start(bf16[128,512]{1,0:T(8,128)(2,1)S(1)} %get-tuple-element.74), channel_id=1, source_target_pairs={{0,3},{1,2},{2,1},{3,0},{4,7},{5,6},{6,5},{7,4},{8,11},{9,10},{10,... | collective-permute-start | bytes 393224 | tf_op jit(solution)/shard_map/ppermute | solution.py:439
  28.9 1.9 %collective-permute-start.11 = (bf16[32,3584]{1,0:T(8,128)(2,1)S(1)}, bf16[32,3584]{1,0:T(8,128)(2,1)S(1)}, u32[]{:S(2)}, u32[]{:S(2)}) collective-permute-start(bf16[32,3584]{1,0:T(8,128)(2,1)S(1)} %get-tuple-element.86), channel_id=1, source_target_pairs={{0,1},{1,0},{2,3},{3,2},{4,5},{5,4},{6,7},{7,6},{8,9},{9,8},{10,11... | collective-permute-start | bytes 688136 | tf_op jit(solution)/shard_map/ppermute | solution.py:439
  30.5 2.1 %collective-permute-start.9 = (bf16[32,3584]{1,0:T(8,128)(2,1)S(1)}, bf16[32,3584]{1,0:T(8,128)(2,1)S(1)}, u32[]{:S(2)}, u32[]{:S(2)}) collective-permute-start(bf16[32,3584]{1,0:T(8,128)(2,1)S(1)} %get-tuple-element.84), channel_id=1, source_target_pairs={{0,1},{1,0},{2,3},{3,2},{4,5},{5,4},{6,7},{7,6},{8,9},{9,8},{10,11... | collective-permute-start | bytes 688136 | tf_op jit(solution)/shard_map/ppermute | solution.py:439
  30.9 5.9 %collective-permute-start.12 = (bf16[16,3584]{1,0:T(8,128)(2,1)S(1)}, bf16[16,3584]{1,0:T(8,128)(2,1)S(1)}, u32[]{:S(2)}, u32[]{:S(2)}) collective-permute-start(bf16[16,3584]{1,0:T(8,128)(2,1)S(1)} %add_convert_fusion), channel_id=1, source_target_pairs={{0,2},{1,3},{2,0},{3,1},{4,6},{5,7},{6,4},{7,5},{8,10},{9,11},{10,... | collective-permute-start | bytes 344072 | tf_op jit(solution)/shard_map/ppermute | solution.py:439
  32.7 5.5 %collective-permute-start.10 = (bf16[16,3584]{1,0:T(8,128)(2,1)S(1)}, bf16[16,3584]{1,0:T(8,128)(2,1)S(1)}, u32[]{:S(2)}, u32[]{:S(2)}) collective-permute-start(bf16[16,3584]{1,0:T(8,128)(2,1)S(1)} %add_convert_fusion.1), channel_id=1, source_target_pairs={{0,3},{1,2},{2,1},{3,0},{4,7},{5,6},{6,5},{7,4},{8,11},{9,10},{10,... | collective-permute-start | bytes 344072 | tf_op jit(solution)/shard_map/ppermute | solution.py:439

commit v7 on v6

--- a/solution.py
+++ b/solution.py
@@ -294,6 +294,8 @@
                 part(task)
 
         keys_now = [k[...] for k in key_refs]
+        if len(keys) <= 3:
+            keys_now = [jnp.concatenate(keys_now, axis=1)]
         merge(first, size, keys_now, q_ref, m_ref, l_ref, acc_ref, store, bool(bring[1]))
         if per_unit != BLOCK:
             for u in range(size):

time: 39.2 us -> 39.4 us (level)
  waiting for transfers between devices: 6.25 us -> 6.97 us
  Pallas kernels: 19.4 us -> 18.7 us
    ppermute x13, waiting for transfers between devices: 6.25 us -> 6.97 us  [swap(): return lax.ppermute(x, 'roll', [(i, i ^ k) for i in range(n)])]
    pallas_call x7, Pallas kernels: 18 us -> 17.3 us  [call(): pl.pallas_call(kernel, in_specs=in_specs, out_specs=[vmem] * len(out_shap...]
  transfers between devices with their start and end apart: 13 -> 13, of which waited for: 6 -> 5; matrix products, arithmetic and copies ran while one was open for 0% -> 0% of each run, Pallas kernels for 42% -> 40%
where the time goes in v7:
time: 39.4 us; the launch traced here: 39.2 us
  Pallas kernels  18.7 us (47%)
  starting transfers between devices  10.9 us (28%)
  waiting for transfers between devices  6.97 us (18%)
  local copies, waits for them, and re-layouts  2.38 us (6%)
    pallas_call x7, Pallas kernels, call(): pl.pallas_call(kernel, in_specs=in_specs, out_specs=[vmem] * len(out_shap...  17.3 us
    ppermute x13, starting transfers between devices, swap(): return lax.ppermute(x, 'roll', [(i, i ^ k) for i in range(n)])  10.9 us
    ppermute x13, waiting for transfers between devices, swap(): return lax.ppermute(x, 'roll', [(i, i ^ k) for i in range(n)])  6.97 us
    unnamed x12, local copies, waits for them, and re-layouts  2.38 us
    pallas_call x2, Pallas kernels, last_sums(): pl.pallas_call(kernel, in_specs=[vmem] * len(terms) + [hbm] * len(held),...  1.43 us
  transfers between devices with their start and end apart: 13, of which 5 were waited for; matrix products, arithmetic and copies ran while one was open for 0% of the time, Pallas kernels for 40%

profile of v7, /device:TPU:0, one launch (start us, length us, event | category | flops | bytes accessed | tf_op | source)
XLA Modules:
  0.0 39.2 jit_solution(8434118807882953368)
XLA Ops:
  0.0 1.1 %copy-done.5 = f32[256,576]{0,1:T(8,128)S(1)} copy-done((f32[256,576]{0,1:T(8,128)S(1)}, f32[256,576]{0,1:T(8,128)}, u32[]{:S(2)}) %copy-start.5) | copy-done | bytes 589848
  1.1 3.0 %collective-permute-start = (bf16[576,256]{1,0:T(8,128)(2,1)S(1)}, bf16[576,256]{1,0:T(8,128)(2,1)S(1)}, u32[]{:S(2)}, u32[]{:S(2)}) collective-permute-start(bf16[576,256]{1,0:T(8,128)(2,1)S(1)} %convert_bitcast_fusion.refs_5_), channel_id=1, source_target_pairs={{0,2},{1,3},{2,0},{3,1},{4,6},{5,7},{6,4},{7,5},{8,10},{9,11},{10,... | collective-permute-start | bytes 884744 | tf_op jit(solution)/shard_map/ppermute | solution.py:441
  4.1 1.3 %copy-done.2 = bf16[8,2,64,576]{3,2,1,0:T(8,128)(2,1)S(1)} copy-done((bf16[8,2,64,576]{3,2,1,0:T(8,128)(2,1)S(1)}, bf16[8,2,64,576]{3,2,1,0:T(8,128)(2,1)}, u32[]{:S(2)}) %copy-start.2) | copy-done | bytes 1179672
  5.4 4.7 %near_attention.1 = (bf16[4,16,16,576]{3,2,1,0:T(8,128)(2,1)S(1)}, f32[4,16,16,128]{3,2,1,0:T(8,128)S(1)}, f32[4,16,16,128]{3,2,1,0:T(8,128)S(1)}, f32[4,16,16,512]{3,2,1,0:T(8,128)S(1)}, bf16[768,7168]{1,0:T(8,128)(2,1)S(1)}) custom-call(f32[8,128]{1,0:T(8,128)S(1)} %pause.1.refs_0_, s32[8]{0:T(128)S(1)} %copy-done.4, ...), custom_call_target="tpu_custom_call" | custom-call | flops 865075200 | bytes 15204352 | tf_op jit(solution)/shard_map/near_attention/pallas_call | solution.py:74
  10.1 1.0 %collective-permute-done.refs_5_ = bf16[576,256]{1,0:T(8,128)(2,1)S(1)} collective-permute-done((bf16[576,256]{1,0:T(8,128)(2,1)S(1)}, bf16[576,256]{1,0:T(8,128)(2,1)S(1)}, u32[]{:S(2)}, u32[]{:S(2)}) %collective-permute-start) | collective-permute-done | bytes 294944 | tf_op jit(solution)/shard_map/ppermute | solution.py:441
  11.1 1.3 %middle_attention.1 = (f32[2,16,16,128]{3,2,1,0:T(8,128)S(1)}, f32[2,16,16,128]{3,2,1,0:T(8,128)S(1)}, f32[2,16,16,512]{3,2,1,0:T(8,128)S(1)}) custom-call(bf16[4,16,16,576]{3,2,1,0:T(8,128)(2,1)S(1)} %get-tuple-element.61.refs_0_, f32[4,16,16,128]{3,2,1,0:T(8,128)S(1)} %get-tuple-element.50.refs_1_, f32[4,16,16,128]{3,2,1,0:T(8,128)S(1)} %get-tuple-element.51.refs_2_, ...), custom_call_target="tpu_custom_call" | custom-call | flops 576716800 | bytes 4194304 | tf_op jit(solution)/shard_map/middle_attention/pallas_call | solution.py:74
  12.4 0.3 collective-permute-done.2.refs_4_.refs_6_
  12.7 1.3 %far_attention.2 = (bf16[128,512]{1,0:T(8,128)(2,1)S(1)}, bf16[128,512]{1,0:T(8,128)(2,1)S(1)}, bf16[128,512]{1,0:T(8,128)(2,1)S(1)}, bf16[128,512]{1,0:T(8,128)(2,1)S(1)}) custom-call(bf16[4,16,16,576]{3,2,1,0:T(8,128)(2,1)S(1)} %get-tuple-element.61.refs_0_, f32[2,16,16,128]{3,2,1,0:T(8,128)S(1)} %get-tuple-element.54.refs_1_, ...), custom_call_target="tpu_custom_call" | custom-call | flops 288358400 | bytes 4194304 | tf_op jit(solution)/shard_map/far_attention/pallas_call | solution.py:74
  14.0 1.8 %collective-permute-start.7 = (bf16[128,512]{1,0:T(8,128)(2,1)S(1)}, bf16[128,512]{1,0:T(8,128)(2,1)S(1)}, u32[]{:S(2)}, u32[]{:S(2)}) collective-permute-start(bf16[128,512]{1,0:T(8,128)(2,1)S(1)} %get-tuple-element.77), channel_id=1, source_target_pairs={{0,2},{1,3},{2,0},{3,1},{4,6},{5,7},{6,4},{7,5},{8,10},{9,11},{10,... | collective-permute-start | bytes 393224 | tf_op jit(solution)/shard_map/ppermute | solution.py:441
  15.8 2.4 %far_attention.3 = (bf16[128,512]{1,0:T(8,128)(2,1)S(1)}, bf16[128,512]{1,0:T(8,128)(2,1)S(1)}, bf16[128,512]{1,0:T(8,128)(2,1)S(1)}, bf16[128,512]{1,0:T(8,128)(2,1)S(1)}, bf16[256,7168]{1,0:T(8,128)(2,1)S(1)}) custom-call(bf16[4,16,16,576]{3,2,1,0:T(8,128)(2,1)S(1)} %get-tuple-element.61.refs_0_, f32[4,16,16,128]{3,2,1,0:T(8,128)S(1)} %get-tuple-element.50.refs_1_, ...), custom_call_target="tpu_custom_call" | custom-call | flops 865075200 | bytes 7864320 | tf_op jit(solution)/shard_map/far_attention/pallas_call | solution.py:74
  18.2 0.5 %collective-permute-start.6 = (bf16[128,512]{1,0:T(8,128)(2,1)S(1)}, bf16[128,512]{1,0:T(8,128)(2,1)S(1)}, u32[]{:S(2)}, u32[]{:S(2)}) collective-permute-start(bf16[128,512]{1,0:T(8,128)(2,1)S(1)} %get-tuple-element.76), channel_id=1, source_target_pairs={{0,1},{1,0},{2,3},{3,2},{4,5},{5,4},{6,7},{7,6},{8,9},{9,8},{10,11... | collective-permute-start | bytes 393224 | tf_op jit(solution)/shard_map/ppermute | solution.py:441
  18.7 0.1 collective-permute-start.3
  18.8 1.7 %collective-permute-start.4 = (bf16[128,512]{1,0:T(8,128)(2,1)S(1)}, bf16[128,512]{1,0:T(8,128)(2,1)S(1)}, u32[]{:S(2)}, u32[]{:S(2)}) collective-permute-start(bf16[128,512]{1,0:T(8,128)(2,1)S(1)} %get-tuple-element.73), channel_id=1, source_target_pairs={{0,2},{1,3},{2,0},{3,1},{4,6},{5,7},{6,4},{7,5},{8,10},{9,11},{10,... | collective-permute-start | bytes 393224 | tf_op jit(solution)/shard_map/ppermute | solution.py:441
  20.6 1.7 %collective-permute-done.8.refs_3_ = bf16[128,512]{1,0:T(8,128)(2,1)S(1)} collective-permute-done((bf16[128,512]{1,0:T(8,128)(2,1)S(1)}, bf16[128,512]{1,0:T(8,128)(2,1)S(1)}, u32[]{:S(2)}, u32[]{:S(2)}) %collective-permute-start.8) | collective-permute-done | bytes 131104 | tf_op jit(solution)/shard_map/ppermute | solution.py:441
  22.3 5.2 %project.3 = (f32[64,7168]{1,0:T(8,128)S(1)}, bf16[1024,7168]{1,0:T(8,128)(2,1)S(1)}) custom-call(bf16[128,512]{1,0:T(8,128)(2,1)S(1)} %get-tuple-element.75.refs_0_, bf16[128,512]{1,0:T(8,128)(2,1)S(1)} %collective-permute-done.6.refs_1_, bf16[128,512]{1,0:T(8,128)(2,1)S(1)} %collective-permute-done.7.refs_2_, ...), custom_call_target="tpu_custom_call" | custom-call | flops 3758096384 | bytes 18874368 | tf_op jit(solution)/shard_map/project/pallas_call | solution.py:74
  27.5 1.3 %project.5 = (bf16[32,3584]{1,0:T(8,128)(2,1)S(1)}, bf16[32,3584]{1,0:T(8,128)(2,1)S(1)}) custom-call(bf16[128,512]{1,0:T(8,128)(2,1)S(1)} %get-tuple-element.71.refs_0_, bf16[128,512]{1,0:T(8,128)(2,1)S(1)} %collective-permute-done.3.refs_1_, bf16[128,512]{1,0:T(8,128)(2,1)S(1)} %collective-permute-done.4.refs_2_, ...), custom_call_target="tpu_custom_call" | custom-call | flops 1879048192 | bytes 4194304 | tf_op jit(solution)/shard_map/project/pallas_call | solution.py:74
  28.8 0.6 %collective-permute-start.11 = (bf16[32,3584]{1,0:T(8,128)(2,1)S(1)}, bf16[32,3584]{1,0:T(8,128)(2,1)S(1)}, u32[]{:S(2)}, u32[]{:S(2)}) collective-permute-start(bf16[32,3584]{1,0:T(8,128)(2,1)S(1)} %get-tuple-element.86), channel_id=1, source_target_pairs={{0,1},{1,0},{2,3},{3,2},{4,5},{5,4},{6,7},{7,6},{8,9},{9,8},{10,11... | collective-permute-start | bytes 688136 | tf_op jit(solution)/shard_map/ppermute | solution.py:441
  29.4 1.3 %project.4 = (bf16[32,3584]{1,0:T(8,128)(2,1)S(1)}, bf16[32,3584]{1,0:T(8,128)(2,1)S(1)}) custom-call(bf16[128,512]{1,0:T(8,128)(2,1)S(1)} %get-tuple-element.71.refs_0_, bf16[128,512]{1,0:T(8,128)(2,1)S(1)} %collective-permute-done.3.refs_1_, bf16[128,512]{1,0:T(8,128)(2,1)S(1)} %collective-permute-done.4.refs_2_, ...), custom_call_target="tpu_custom_call" | custom-call | flops 1879048192 | bytes 4194304 | tf_op jit(solution)/shard_map/project/pallas_call | solution.py:74
  30.8 1.8 %collective-permute-start.12 = (bf16[16,3584]{1,0:T(8,128)(2,1)S(1)}, bf16[16,3584]{1,0:T(8,128)(2,1)S(1)}, u32[]{:S(2)}, u32[]{:S(2)}) collective-permute-start(bf16[16,3584]{1,0:T(8,128)(2,1)S(1)} %add_convert_fusion), channel_id=1, source_target_pairs={{0,2},{1,3},{2,0},{3,1},{4,6},{5,7},{6,4},{7,5},{8,10},{9,11},{10,... | collective-permute-start | bytes 344072 | tf_op jit(solution)/shard_map/ppermute | solution.py:441
  32.7 1.2 %collective-permute-start.10 = (bf16[16,3584]{1,0:T(8,128)(2,1)S(1)}, bf16[16,3584]{1,0:T(8,128)(2,1)S(1)}, u32[]{:S(2)}, u32[]{:S(2)}) collective-permute-start(bf16[16,3584]{1,0:T(8,128)(2,1)S(1)} %add_convert_fusion.1), channel_id=1, source_target_pairs={{0,3},{1,2},{2,1},{3,0},{4,7},{5,6},{6,5},{7,4},{8,11},{9,10},{10,... | collective-permute-start | bytes 344072 | tf_op jit(solution)/shard_map/ppermute | solution.py:441
  33.8 3.0 %collective-permute-done.12.refs_2_ = bf16[16,3584]{1,0:T(8,128)(2,1)S(1)} collective-permute-done((bf16[16,3584]{1,0:T(8,128)(2,1)S(1)}, bf16[16,3584]{1,0:T(8,128)(2,1)S(1)}, u32[]{:S(2)}, u32[]{:S(2)}) %collective-permute-start.12) | collective-permute-done | bytes 114720 | tf_op jit(solution)/shard_map/ppermute | solution.py:441
  36.8 0.7 %last_sums.2.refs_3_ = bf16[8,2,7168]{2,1,0:T(2,128)(2,1)} custom-call(bf16[32,3584]{1,0:T(8,128)(2,1)S(1)} %get-tuple-element.85.refs_0_, bf16[32,3584]{1,0:T(8,128)(2,1)S(1)} %collective-permute-done.11.refs_1_, bf16[16,3584]{1,0:T(8,128)(2,1)S(1)} %collective-permute-done.12.refs_2_), custom_call_target="tpu_custom_call" | custom-call | tf_op jit(solution)/shard_map/last_sums/pallas_call | solution.py:400
  37.6 0.9 %collective-permute-done.10.refs_2_ = bf16[16,3584]{1,0:T(8,128)(2,1)S(1)} collective-permute-done((bf16[16,3584]{1,0:T(8,128)(2,1)S(1)}, bf16[16,3584]{1,0:T(8,128)(2,1)S(1)}, u32[]{:S(2)}, u32[]{:S(2)}) %collective-permute-start.10) | collective-permute-done | bytes 114720 | tf_op jit(solution)/shard_map/ppermute | solution.py:441
  38.5 0.7 %last_sums.3 = bf16[8,2,7168]{2,1,0:T(2,128)(2,1)} custom-call(bf16[32,3584]{1,0:T(8,128)(2,1)S(1)} %get-tuple-element.83.refs_0_, bf16[32,3584]{1,0:T(8,128)(2,1)S(1)} %collective-permute-done.9.refs_1_, bf16[16,3584]{1,0:T(8,128)(2,1)S(1)} %collective-permute-done.10.refs_2_, bf16[8,2,7168]{2,1,0:T(2,128)(2,1)} %last_sums.2.refs_3_), custom_call_target="tpu_custom_call", output_to_operand_aliasing={{}: (3, {})} | custom-call | tf_op jit(solution)/shard_map/last_sums/pallas_call | solution.py:400
  (27 shorter events, 0.3 us)
Async XLA Ops:
  0.0 1.1 %copy-start.5 = (f32[256,576]{0,1:T(8,128)S(1)}, f32[256,576]{0,1:T(8,128)}, u32[]{:S(2)}) copy-start(f32[256,576]{0,1:T(8,128)} %param.7) | copy-start | bytes 1769476
  0.0 4.1 %copy-start.3 = (bf16[8,2,576]{2,1,0:T(2,128)(2,1)S(1)}, bf16[8,2,576]{2,1,0:T(2,128)(2,1)}, u32[]{:S(2)}) copy-start(bf16[8,2,576]{2,1,0:T(2,128)(2,1)} %refs_4_.2) | copy-start | bytes 55300
  0.0 4.1 %copy-start.4 = (s32[8]{0:T(128)S(1)}, s32[8]{0:T(128)}, u32[]{:S(2)}) copy-start(s32[8]{0:T(128)} %refs_1_.1) | copy-start | bytes 100
  0.0 4.1 %copy-start.1 = (bf16[8,256,576]{1,2,0:T(8,128)(2,1)S(1)}, bf16[8,256,576]{1,2,0:T(8,128)(2,1)}, u32[]{:S(2)}) copy-start(bf16[8,256,576]{1,2,0:T(8,128)(2,1)} %param.8) | copy-start | bytes 7077892
  1.1 10.0 %collective-permute-start = (bf16[576,256]{1,0:T(8,128)(2,1)S(1)}, bf16[576,256]{1,0:T(8,128)(2,1)S(1)}, u32[]{:S(2)}, u32[]{:S(2)}) collective-permute-start(bf16[576,256]{1,0:T(8,128)(2,1)S(1)} %convert_bitcast_fusion.refs_5_), channel_id=1, source_target_pairs={{0,2},{1,3},{2,0},{3,1},{4,6},{5,7},{6,4},{7,5},{8,10},{9,11},{10,... | collective-permute-start | bytes 884744 | tf_op jit(solution)/shard_map/ppermute | solution.py:441
  4.1 7.0 %collective-permute-start.1 = (bf16[576,256]{1,0:T(8,128)(2,1)S(1)}, bf16[576,256]{1,0:T(8,128)(2,1)S(1)}, u32[]{:S(2)}, u32[]{:S(2)}) collective-permute-start(bf16[576,256]{1,0:T(8,128)(2,1)S(1)} %convert_bitcast_fusion.refs_5_), channel_id=1, source_target_pairs={{0,1},{1,0},{2,3},{3,2},{4,5},{5,4},{6,7},{7,6},{8,9},{9,8},{10,11... | collective-permute-start | bytes 884744 | tf_op jit(solution)/shard_map/ppermute | solution.py:441
  4.1 1.3 %copy-start.2 = (bf16[8,2,64,576]{3,2,1,0:T(8,128)(2,1)S(1)}, bf16[8,2,64,576]{3,2,1,0:T(8,128)(2,1)}, u32[]{:S(2)}) copy-start(bf16[8,2,64,576]{3,2,1,0:T(8,128)(2,1)} %refs_2_.1) | copy-start | bytes 3538948
  11.1 1.6 %collective-permute-start.2 = (bf16[576,256]{1,0:T(8,128)(2,1)S(1)}, bf16[576,256]{1,0:T(8,128)(2,1)S(1)}, u32[]{:S(2)}, u32[]{:S(2)}) collective-permute-start(bf16[576,256]{1,0:T(8,128)(2,1)S(1)} %collective-permute-done.refs_5_), channel_id=1, source_target_pairs={{0,1},{1,0},{2,3},{3,2},{4,5},{5,4},{6,7},{7,6},{8,9},{9,8},{10,11... | collective-permute-start | bytes 884744 | tf_op jit(solution)/shard_map/ppermute | solution.py:441
  14.0 8.3 %copy-start = (bf16[16,512,128]{2,1,0:T(8,128)(2,1)S(1)}, bf16[16,512,128]{2,1,0:T(8,128)(2,1)}, u32[]{:S(2)}) copy-start(bf16[16,512,128]{2,1,0:T(8,128)(2,1)} %refs_5_.3) | copy-start | bytes 6291460
  14.0 6.5 %collective-permute-start.7 = (bf16[128,512]{1,0:T(8,128)(2,1)S(1)}, bf16[128,512]{1,0:T(8,128)(2,1)S(1)}, u32[]{:S(2)}, u32[]{:S(2)}) collective-permute-start(bf16[128,512]{1,0:T(8,128)(2,1)S(1)} %get-tuple-element.77), channel_id=1, source_target_pairs={{0,2},{1,3},{2,0},{3,1},{4,6},{5,7},{6,4},{7,5},{8,10},{9,11},{10,... | collective-permute-start | bytes 393224 | tf_op jit(solution)/shard_map/ppermute | solution.py:441
  15.8 6.5 %collective-permute-start.8 = (bf16[128,512]{1,0:T(8,128)(2,1)S(1)}, bf16[128,512]{1,0:T(8,128)(2,1)S(1)}, u32[]{:S(2)}, u32[]{:S(2)}) collective-permute-start(bf16[128,512]{1,0:T(8,128)(2,1)S(1)} %get-tuple-element.78), channel_id=1, source_target_pairs={{0,3},{1,2},{2,1},{3,0},{4,7},{5,6},{6,5},{7,4},{8,11},{9,10},{10,... | collective-permute-start | bytes 393224 | tf_op jit(solution)/shard_map/ppermute | solution.py:441
  18.2 4.1 %collective-permute-start.6 = (bf16[128,512]{1,0:T(8,128)(2,1)S(1)}, bf16[128,512]{1,0:T(8,128)(2,1)S(1)}, u32[]{:S(2)}, u32[]{:S(2)}) collective-permute-start(bf16[128,512]{1,0:T(8,128)(2,1)S(1)} %get-tuple-element.76), channel_id=1, source_target_pairs={{0,1},{1,0},{2,3},{3,2},{4,5},{5,4},{6,7},{7,6},{8,9},{9,8},{10,11... | collective-permute-start | bytes 393224 | tf_op jit(solution)/shard_map/ppermute | solution.py:441
  18.7 8.8 %collective-permute-start.3 = (bf16[128,512]{1,0:T(8,128)(2,1)S(1)}, bf16[128,512]{1,0:T(8,128)(2,1)S(1)}, u32[]{:S(2)}, u32[]{:S(2)}) collective-permute-start(bf16[128,512]{1,0:T(8,128)(2,1)S(1)} %get-tuple-element.72), channel_id=1, source_target_pairs={{0,1},{1,0},{2,3},{3,2},{4,5},{5,4},{6,7},{7,6},{8,9},{9,8},{10,11... | collective-permute-start | bytes 393224 | tf_op jit(solution)/shard_map/ppermute | solution.py:441
  18.8 8.7 %collective-permute-start.4 = (bf16[128,512]{1,0:T(8,128)(2,1)S(1)}, bf16[128,512]{1,0:T(8,128)(2,1)S(1)}, u32[]{:S(2)}, u32[]{:S(2)}) collective-permute-start(bf16[128,512]{1,0:T(8,128)(2,1)S(1)} %get-tuple-element.73), channel_id=1, source_target_pairs={{0,2},{1,3},{2,0},{3,1},{4,6},{5,7},{6,4},{7,5},{8,10},{9,11},{10,... | collective-permute-start | bytes 393224 | tf_op jit(solution)/shard_map/ppermute | solution.py:441
  20.5 7.0 %collective-permute-start.5 = (bf16[128,512]{1,0:T(8,128)(2,1)S(1)}, bf16[128,512]{1,0:T(8,128)(2,1)S(1)}, u32[]{:S(2)}, u32[]{:S(2)}) collective-permute-start(bf16[128,512]{1,0:T(8,128)(2,1)S(1)} %get-tuple-element.74), channel_id=1, source_target_pairs={{0,3},{1,2},{2,1},{3,0},{4,7},{5,6},{6,5},{7,4},{8,11},{9,10},{10,... | collective-permute-start | bytes 393224 | tf_op jit(solution)/shard_map/ppermute | solution.py:441
  28.8 2.0 %collective-permute-start.11 = (bf16[32,3584]{1,0:T(8,128)(2,1)S(1)}, bf16[32,3584]{1,0:T(8,128)(2,1)S(1)}, u32[]{:S(2)}, u32[]{:S(2)}) collective-permute-start(bf16[32,3584]{1,0:T(8,128)(2,1)S(1)} %get-tuple-element.86), channel_id=1, source_target_pairs={{0,1},{1,0},{2,3},{3,2},{4,5},{5,4},{6,7},{7,6},{8,9},{9,8},{10,11... | collective-permute-start | bytes 688136 | tf_op jit(solution)/shard_map/ppermute | solution.py:441
  30.7 1.9 %collective-permute-start.9 = (bf16[32,3584]{1,0:T(8,128)(2,1)S(1)}, bf16[32,3584]{1,0:T(8,128)(2,1)S(1)}, u32[]{:S(2)}, u32[]{:S(2)}) collective-permute-start(bf16[32,3584]{1,0:T(8,128)(2,1)S(1)} %get-tuple-element.84), channel_id=1, source_target_pairs={{0,1},{1,0},{2,3},{3,2},{4,5},{5,4},{6,7},{7,6},{8,9},{9,8},{10,11... | collective-permute-start | bytes 688136 | tf_op jit(solution)/shard_map/ppermute | solution.py:441
  30.8 6.0 %collective-permute-start.12 = (bf16[16,3584]{1,0:T(8,128)(2,1)S(1)}, bf16[16,3584]{1,0:T(8,128)(2,1)S(1)}, u32[]{:S(2)}, u32[]{:S(2)}) collective-permute-start(bf16[16,3584]{1,0:T(8,128)(2,1)S(1)} %add_convert_fusion), channel_id=1, source_target_pairs={{0,2},{1,3},{2,0},{3,1},{4,6},{5,7},{6,4},{7,5},{8,10},{9,11},{10,... | collective-permute-start | bytes 344072 | tf_op jit(solution)/shard_map/ppermute | solution.py:441
  32.7 5.8 %collective-permute-start.10 = (bf16[16,3584]{1,0:T(8,128)(2,1)S(1)}, bf16[16,3584]{1,0:T(8,128)(2,1)S(1)}, u32[]{:S(2)}, u32[]{:S(2)}) collective-permute-start(bf16[16,3584]{1,0:T(8,128)(2,1)S(1)} %add_convert_fusion.1), channel_id=1, source_target_pairs={{0,3},{1,2},{2,1},{3,0},{4,7},{5,6},{6,5},{7,4},{8,11},{9,10},{10,... | collective-permute-start | bytes 344072 | tf_op jit(solution)/shard_map/ppermute | solution.py:441
